TPU v7x, 32 devices: a whole 2x2x4 slice. The times are simulated.
32 devices in a mesh: node: 16 (over z, x, core), head: 2 (over y).
Axes of the slice: x: 2, y: 2, z: 4, core: 2. Of those that a mesh axis runs over, the one named last changes fastest.
Arguments:
- features: bfloat16 [65536, 512], P(('node', 'head')), may hold values from -8 to 8
- w_query: bfloat16 [512, 512], replicated, may hold values from -0.25 to 0.25
- w_key_value: bfloat16 [512, 2, 512], replicated, may hold values from -0.25 to 0.25
- edge_local: float32 [512], P('head'), may hold values from 0.5 to 2
- edge_expand: float32 [512], P('head'), may hold values from 0.5 to 2
- local_cols: int32 [512, 8], P('node'), may hold values from 0 to 35, as said below
- exp_rows: int32 [16, 4, 16], P('node'), may hold values from 0 to 31
- exp_cols: int32 [16, 4, 16], P('node'), may hold values from 0 to 31
Outputs:
- attention: bfloat16 [65536, 512], P(('node', 'head'))
Inputs may be any that keep to these rules, and one draw needn't show every extreme that they name: `local_cols`: the first slot of every row names a tile of the row's own node block, a value from 2 to 33.
All inputs are finite; a program needn't handle non-finite values.
Results may differ from a plain program's by a relative error of at most 0.009.
Values may be sent and summed in bfloat16 or wider, within the bound.
No kernel may reach another device: no remote copies, remote signals or barrier semaphores. Data moves between devices by JAX's collectives and lax.ppermute only.
A program may use at most 128 MiB of HBM per device.

v0:
```python
import math

import jax
import jax.numpy as jnp
from jax import lax
from jax.sharding import PartitionSpec as P

HEADS = 8
TILE = 128
HT = 2
MATCH = 4


highest = lax.Precision.HIGHEST


def padded(x, sides, width):
    for axis, dim in sides:
        devices, length = (lax.axis_size(axis), x.shape[dim])
        up = [(i, (i + 1) % devices) for i in range(devices - 1)]
        down = [(j, i) for i, j in up]
        last = lax.slice_in_dim(x, length - width, length, axis=dim)
        first = lax.slice_in_dim(x, 0, width, axis=dim)
        before = lax.ppermute(last, axis, up)
        after = lax.ppermute(first, axis, down)
        x = jnp.concatenate([before, x, after], axis=dim)
    return x


def partner(block, axis, stride):
    count = lax.axis_size(axis)
    route = []
    for low in range(count):
        high = low | 1 << stride
        if high != low and high < count:
            route += [(low, high), (high, low)]
    return lax.ppermute(block, axis, route)


def attend(queries, pair_block, usable):
    head_width = queries.shape[3] // 2
    scores = jnp.einsum("gqhe,gkhe->ghqk", queries, pair_block, preferred_element_type=jnp.float32)
    weights = jnp.exp(jnp.clip(scores, -5.0, 5.0))
    weights = jnp.where(usable[:, None, None, :], weights, jnp.zeros_like(weights))
    denominator = jnp.sum(weights, axis=3)
    combined = jnp.einsum(
        "ghqk,gkhe->gqhe",
        weights.astype(jnp.bfloat16),
        pair_block,
        preferred_element_type=jnp.float32,
    )
    return (combined[:, :, :, head_width:], jnp.transpose(denominator, (0, 2, 1)))


def local_part(queries, extended, columns, first_tile, tile_count, tile_rows, halo_tiles):
    row_count, head_count, double_width = queries.shape
    row_tiles = row_count // tile_rows
    group_size = min(row_tiles, max(1, 512 // tile_rows))
    group_count = row_tiles // group_size
    ext_tiles = extended.reshape(-1, tile_rows, head_count, double_width)
    grouped_queries = queries.reshape(group_count, group_size, tile_rows, head_count, double_width)
    grouped_columns = columns.reshape(group_count, group_size, columns.shape[1])

    def one_group(pair):
        block_queries, block_columns = pair
        picked = ext_tiles[block_columns].reshape(group_size, -1, head_count, double_width)
        global_tile = first_tile + block_columns - halo_tiles
        usable = jnp.logical_and(global_tile >= 0, global_tile < tile_count)
        usable = jnp.repeat(usable, tile_rows, axis=1)
        return attend(block_queries, picked, usable)

    numerator, denominator = lax.map(one_group, (grouped_queries, grouped_columns))
    return (
        numerator.reshape(row_count, head_count, double_width // 2),
        denominator.reshape(row_count, head_count),
    )


def expander_part(queries, key_tiles, row_index):
    row_count, head_count, double_width = queries.shape
    tile_rows = key_tiles.shape[1]
    row_tiles = row_count // tile_rows
    pair_count = key_tiles.shape[0]
    chosen = queries.reshape(row_tiles, tile_rows, head_count, double_width)[row_index]
    pairs = key_tiles.reshape(pair_count, tile_rows, head_count, double_width)
    usable = jnp.ones((pair_count, tile_rows), dtype=jnp.bool_)
    numerator, denominator = attend(chosen, pairs, usable)
    selector = (row_index[None, :] == jnp.arange(row_tiles, dtype=jnp.int32)[:, None]).astype(
        jnp.float32
    )
    numerator = jnp.einsum("te,eqhw->tqhw", selector, numerator, precision=highest)
    denominator = jnp.einsum("te,eqh->tqh", selector, denominator, precision=highest)
    return (
        numerator.reshape(row_count, head_count, double_width // 2),
        denominator.reshape(row_count, head_count),
    )


def widen_query(query_part, heads_here, head_width):
    shaped = query_part.reshape(-1, heads_here, head_width)
    return jnp.concatenate([shaped, jnp.zeros_like(shaped)], axis=2)


def local(features, w_query, w_key_value, edge_local, edge_expand, local_cols, exp_rows, exp_cols):
    groups = lax.axis_size("head")
    node_count = lax.axis_size("node")
    width = features.shape[1]
    head_width = width // HEADS
    local_width = width // groups
    heads_here = local_width // head_width
    scale = 1.0 / math.sqrt(head_width)
    query_cols = w_query.reshape(width, groups, local_width)
    pair_cols = w_key_value.reshape(width, 2, groups, heads_here, head_width)
    pair_cols = jnp.transpose(pair_cols, (0, 2, 3, 1, 4)).reshape(width, groups, 2 * local_width)
    all_cols = jnp.concatenate([query_cols, pair_cols], axis=2).reshape(
        width, groups * 3 * local_width
    )
    projected = jnp.dot(features, all_cols, preferred_element_type=jnp.float32).astype(jnp.bfloat16)
    projected = projected.reshape(-1, groups, 3 * local_width)
    received = lax.all_to_all(projected, "head", split_axis=1, concat_axis=0, tiled=True)
    row_count = received.shape[0]
    received = received.reshape(row_count, 3 * local_width)
    row_tiles = row_count // TILE
    query_wide = lax.optimization_barrier(received[:, :local_width]).astype(jnp.float32)
    local_q = widen_query(
        (query_wide * edge_local * scale).astype(jnp.bfloat16), heads_here, head_width
    )
    expand_q = widen_query(
        (query_wide * edge_expand * scale).astype(jnp.bfloat16), heads_here, head_width
    )
    pair_here = received[:, local_width:]
    extended = padded(pair_here, (("node", 0),), HT * TILE)
    first_tile = lax.axis_index("node") * row_tiles
    numerator, denominator = local_part(
        local_q, extended, local_cols, first_tile, node_count * row_tiles, TILE, HT
    )
    log_count = node_count.bit_length() - 1
    tile_list = []
    row_list = []
    for matching in range(MATCH):
        flip_bit = matching * log_count // 4
        wanted_cols = exp_cols[0, matching]
        partner_pairs = partner(pair_here, "node", flip_bit)
        fetched = partner_pairs.reshape(row_tiles, TILE, 2 * local_width)[wanted_cols]
        tile_list.append(fetched)
        row_list.append(exp_rows[0, matching])
    extra_num, extra_den = expander_part(
        expand_q, jnp.concatenate(tile_list, axis=0), jnp.concatenate(row_list, axis=0)
    )
    result = ((numerator + extra_num) / (denominator + extra_den)[:, :, None]).astype(jnp.bfloat16)
    result = result.reshape(row_count, 1, local_width)
    returned = lax.all_to_all(result, "head", split_axis=0, concat_axis=1, tiled=True)
    return returned.reshape(-1, width)


def solution(mesh):
    return jax.shard_map(
        local,
        mesh=mesh,
        in_specs=(
            P(("node", "head"), None),
            P(),
            P(),
            P("head"),
            P("head"),
            P("node", None),
            P("node", None, None),
            P("node", None, None),
        ),
        out_specs=P(("node", "head"), None),
        check_vma=False,
    )
```

profile of v0, /device:TPU:25, one launch (start us, length us, event | category | flops | bytes accessed | tf_op | source)
XLA Modules:
  0.0 628.7 jit_solution(10081470963893969547)
XLA Ops:
  8.3 5.5 convolution_convert_fusion
  13.8 8.6 %copy.95 = bf16[2048,2,768]{2,0,1:T(8,128)(2,1)} copy(bf16[2048,2,768]{0,2,1:T(8,128)(2,1)} %bitcast.150) | data formatting | bytes 12582912 | tf_op jit(solution)/shard_map/reshape | solution.py:119
  22.4 6.4 %all-to-all-start = ((bf16[2048,2,768]{2,0,1:T(8,128)(2,1)}), bf16[2048,2,768]{2,0,1:T(8,128)(2,1)}, u32[]{:S(2)}, u32[]{:S(2)}) async-start(bf16[2048,2,768]{2,0,1:T(8,128)(2,1)} %copy.95), calls=%async_computation | async-start | bytes 12582912 | tf_op jit(solution)/shard_map/all_to_all | solution.py:120
  29.8 68.4 %all-to-all-done = bf16[2048,2,768]{2,0,1:T(8,128)(2,1)} async-done(((bf16[2048,2,768]{2,0,1:T(8,128)(2,1)}), bf16[2048,2,768]{2,0,1:T(8,128)(2,1)}, u32[]{:S(2)}, u32[]{:S(2)}) %all-to-all-start) | async-done | bytes 6291488 | tf_op jit(solution)/shard_map/all_to_all | solution.py:120
  136.1 8.4 %copy.103 = bf16[64,128,4,64]{3,1,2,0:T(8,128)(2,1)} copy(bf16[64,128,4,64]{1,3,2,0:T(8,128)(2,1)} %gather_fusion.5) | data formatting | bytes 8388608 | tf_op jit(solution)/shard_map/gather | solution.py:84
  149.5 53.7 %collective-permute-done.1 = bf16[256,512]{1,0:T(8,128)(2,1)S(1)} collective-permute-done((bf16[256,512]{1,0:T(8,128)(2,1)S(1)}, bf16[256,512]{1,0:T(8,128)(2,1)S(1)}, u32[]{:S(2)}, u32[]{:S(2)}) %collective-permute-start.1) | collective-permute-done | bytes 262176 | tf_op jit(solution)/shard_map/ppermute | solution.py:25
  203.2 86.2 %collective-permute-start.2 = (bf16[4096,512]{1,0:T(8,128)(2,1)}, bf16[4096,512]{1,0:T(8,128)(2,1)}, u32[]{:S(2)}, u32[]{:S(2)}) collective-permute-start(bf16[4096,512]{1,0:T(8,128)(2,1)} %slice.74), channel_id=1, source_target_pairs={{0,2},{2,0},{4,6},{6,4},{8,10},{10,8},{12,14},{14,12},{16,18},{18,... | collective-permute-start | bytes 12582920 | tf_op jit(solution)/shard_map/ppermute | solution.py:37
  293.3 7.7 %reshape.443 = bf16[36,128,4,128]{3,2,1,0:T(4,128)(2,1)} reshape(bf16[4608,512]{1,0:T(8,128)(2,1)} %pad_maximum_fusion.1) | data formatting | bytes 9437184 | tf_op jit(solution)/shard_map/reshape | solution.py:60
  301.0 187.9 %while.14 = (s32[]{:T(128)}, f32[8,4,128,4,64]{2,1,0,4,3:T(4,128)}, f32[8,4,128,4]{2,3,1,0:T(4,128)S(1)}, s32[8,4,8]{2,1,0:T(4,128)S(1)}, bf16[36,128,4,128]{3,2...) while((s32[]{:T(128)}, f32[8,4,128,4,64]{2,1,0,4,3:T(4,128)}, ...), condition=%wide.region_2.3_spmd, body=%wide.region_0.2_spmd.sunk | while | flops 1086323968 | bytes 62440528 | solution.py:72
  301.1 8.2 %gather_fusion = bf16[32,128,4,128]{3,2,1,0:T(4,128)(2,1)} fusion(bf16[36,128,4,128]{3,2,1,0:T(4,128)(2,1)} %get-tuple-element.237, s32[1024]{0:T(1024)S(1)} %pad_clamp_fusion.7), kind=kCustom, calls=%fused_computation.clone.1 | custom fusion | bytes 8388736 | tf_op jit(solution)/shard_map/while/body/eval_jaxpr/gather | solution.py:66
  309.3 7.5 %copy.143 = bf16[4,1024,4,128]{1,3,2,0:T(8,128)(2,1)} copy(bf16[4,1024,4,128]{3,2,1,0:T(4,128)(2,1)} %bitcast.142) | data formatting | bytes 8388608 | tf_op jit(solution)/shard_map/while/body/eval_jaxpr/reshape | solution.py:66
  324.6 8.2 %gather_fusion = bf16[32,128,4,128]{3,2,1,0:T(4,128)(2,1)} fusion(bf16[36,128,4,128]{3,2,1,0:T(4,128)(2,1)} %get-tuple-element.237, s32[1024]{0:T(1024)S(1)} %pad_clamp_fusion.7), kind=kCustom, calls=%fused_computation.clone.1 | custom fusion | bytes 8388736 | tf_op jit(solution)/shard_map/while/body/eval_jaxpr/gather | solution.py:66
  332.8 7.5 %copy.143 = bf16[4,1024,4,128]{1,3,2,0:T(8,128)(2,1)} copy(bf16[4,1024,4,128]{3,2,1,0:T(4,128)(2,1)} %bitcast.142) | data formatting | bytes 8388608 | tf_op jit(solution)/shard_map/while/body/eval_jaxpr/reshape | solution.py:66
  348.1 8.2 %gather_fusion = bf16[32,128,4,128]{3,2,1,0:T(4,128)(2,1)} fusion(bf16[36,128,4,128]{3,2,1,0:T(4,128)(2,1)} %get-tuple-element.237, s32[1024]{0:T(1024)S(1)} %pad_clamp_fusion.7), kind=kCustom, calls=%fused_computation.clone.1 | custom fusion | bytes 8388736 | tf_op jit(solution)/shard_map/while/body/eval_jaxpr/gather | solution.py:66
  356.3 7.5 %copy.143 = bf16[4,1024,4,128]{1,3,2,0:T(8,128)(2,1)} copy(bf16[4,1024,4,128]{3,2,1,0:T(4,128)(2,1)} %bitcast.142) | data formatting | bytes 8388608 | tf_op jit(solution)/shard_map/while/body/eval_jaxpr/reshape | solution.py:66
  371.6 8.2 %gather_fusion = bf16[32,128,4,128]{3,2,1,0:T(4,128)(2,1)} fusion(bf16[36,128,4,128]{3,2,1,0:T(4,128)(2,1)} %get-tuple-element.237, s32[1024]{0:T(1024)S(1)} %pad_clamp_fusion.7), kind=kCustom, calls=%fused_computation.clone.1 | custom fusion | bytes 8388736 | tf_op jit(solution)/shard_map/while/body/eval_jaxpr/gather | solution.py:66
  379.8 7.5 %copy.143 = bf16[4,1024,4,128]{1,3,2,0:T(8,128)(2,1)} copy(bf16[4,1024,4,128]{3,2,1,0:T(4,128)(2,1)} %bitcast.142) | data formatting | bytes 8388608 | tf_op jit(solution)/shard_map/while/body/eval_jaxpr/reshape | solution.py:66
  395.1 8.2 %gather_fusion = bf16[32,128,4,128]{3,2,1,0:T(4,128)(2,1)} fusion(bf16[36,128,4,128]{3,2,1,0:T(4,128)(2,1)} %get-tuple-element.237, s32[1024]{0:T(1024)S(1)} %pad_clamp_fusion.7), kind=kCustom, calls=%fused_computation.clone.1 | custom fusion | bytes 8388736 | tf_op jit(solution)/shard_map/while/body/eval_jaxpr/gather | solution.py:66
  403.2 7.5 %copy.143 = bf16[4,1024,4,128]{1,3,2,0:T(8,128)(2,1)} copy(bf16[4,1024,4,128]{3,2,1,0:T(4,128)(2,1)} %bitcast.142) | data formatting | bytes 8388608 | tf_op jit(solution)/shard_map/while/body/eval_jaxpr/reshape | solution.py:66
  418.5 8.2 %gather_fusion = bf16[32,128,4,128]{3,2,1,0:T(4,128)(2,1)} fusion(bf16[36,128,4,128]{3,2,1,0:T(4,128)(2,1)} %get-tuple-element.237, s32[1024]{0:T(1024)S(1)} %pad_clamp_fusion.7), kind=kCustom, calls=%fused_computation.clone.1 | custom fusion | bytes 8388736 | tf_op jit(solution)/shard_map/while/body/eval_jaxpr/gather | solution.py:66
  426.7 7.5 %copy.143 = bf16[4,1024,4,128]{1,3,2,0:T(8,128)(2,1)} copy(bf16[4,1024,4,128]{3,2,1,0:T(4,128)(2,1)} %bitcast.142) | data formatting | bytes 8388608 | tf_op jit(solution)/shard_map/while/body/eval_jaxpr/reshape | solution.py:66
  442.0 8.2 %gather_fusion = bf16[32,128,4,128]{3,2,1,0:T(4,128)(2,1)} fusion(bf16[36,128,4,128]{3,2,1,0:T(4,128)(2,1)} %get-tuple-element.237, s32[1024]{0:T(1024)S(1)} %pad_clamp_fusion.7), kind=kCustom, calls=%fused_computation.clone.1 | custom fusion | bytes 8388736 | tf_op jit(solution)/shard_map/while/body/eval_jaxpr/gather | solution.py:66
  450.2 7.5 %copy.143 = bf16[4,1024,4,128]{1,3,2,0:T(8,128)(2,1)} copy(bf16[4,1024,4,128]{3,2,1,0:T(4,128)(2,1)} %bitcast.142) | data formatting | bytes 8388608 | tf_op jit(solution)/shard_map/while/body/eval_jaxpr/reshape | solution.py:66
  465.5 8.2 %gather_fusion = bf16[32,128,4,128]{3,2,1,0:T(4,128)(2,1)} fusion(bf16[36,128,4,128]{3,2,1,0:T(4,128)(2,1)} %get-tuple-element.237, s32[1024]{0:T(1024)S(1)} %pad_clamp_fusion.7), kind=kCustom, calls=%fused_computation.clone.1 | custom fusion | bytes 8388736 | tf_op jit(solution)/shard_map/while/body/eval_jaxpr/gather | solution.py:66
  473.7 7.5 %copy.143 = bf16[4,1024,4,128]{1,3,2,0:T(8,128)(2,1)} copy(bf16[4,1024,4,128]{3,2,1,0:T(4,128)(2,1)} %bitcast.142) | data formatting | bytes 8388608 | tf_op jit(solution)/shard_map/while/body/eval_jaxpr/reshape | solution.py:66
  488.9 5.5 reshape.446
  509.8 6.7 %pad_maximum_fusion = bf16[64,128,512]{2,1,0:T(8,128)(2,1)} fusion(bf16[16,128,512]{2,1,0:T(8,128)(2,1)S(1)} %gather_fusion.4, bf16[16,128,512]{2,1,0:T(8,128)(2,1)} %gather_fusion.3, bf16[16,128,512]{2,1,0:T(8,128)(2,1)} %gather_fusion.2, bf16[16,128,512]{2,1,0:T(8,128)(2,1)} %gather_fusion.1), kind=kLoop, calls=%fused_computation.34 | loop fusion | flops 12582912 | bytes 16777216 | tf_op jit(solution)/shard_map/concatenate | solution.py:148
  516.5 11.9 %copy.100 = bf16[64,128,512]{1,2,0:T(8,128)(2,1)} copy(bf16[64,128,512]{2,1,0:T(8,128)(2,1)} %pad_maximum_fusion) | data formatting | bytes 16777216 | tf_op jit(solution)/shard_map/concatenate | solution.py:148
  528.5 13.1 %fusion.15 = (f32[64,4,128]{2,1,0:T(4,128)S(1)}, f32[64,4,128,128]{2,3,1,0:T(8,128)}) fusion(bf16[64,128,4,128]{1,3,2,0:T(8,128)(2,1)} %bitcast.143, bf16[64,128,4,64]{3,1,2,0:T(8,128)(2,1)} %copy.103), kind=kOutput, calls=%fused_computation.31 | convolution fusion | flops 1082097664 | bytes 29491200 | tf_op jit(solution)/shard_map/gqhe,gkhe->ghqk/dot_general | solution.py:42
  541.6 16.5 %convolution_bitcast_fusion = f32[64,128,4,128]{1,3,2,0:T(8,128)} fusion(bf16[64,128,4,128]{1,3,2,0:T(8,128)(2,1)} %bitcast.144, f32[64,4,128,128]{2,3,1,0:T(8,128)} %get-tuple-element.165), kind=kOutput, calls=%fused_computation.33 | convolution fusion | flops 1082130432 | bytes 41943040 | tf_op jit(solution)/shard_map/ghqk,gkhe->gqhe/dot_general | solution.py:46
  561.4 8.0 %fusion.18 = f32[32,128,4,64]{1,0,3,2:T(8,128)} fusion(f32[64,128,4,64]{1,3,2,0:T(8,128)S(1)} %slice-done, s32[64]{0:T(128)S(1)} %copy-done.4), kind=kOutput, calls=%fused_computation.35 | convolution fusion | flops 805308416 | bytes 12583168 | tf_op jit(solution)/shard_map/te,eqhw->tqhw/dot_general | solution.py:91
  588.2 25.5 %all_to_all.30 = bf16[2,2,262144]{2,1,0:T(2,128)(2,1)S(1)} all-to-all(bf16[2,2,262144]{2,1,0:T(2,128)(2,1)} %reshape.509), channel_id=1, replica_groups=mesh['node'=16,'head'=2] {'head'}, dimensions={0} | all-to-all | bytes 4194304 | tf_op jit(solution)/shard_map/all_to_all | solution.py:152
  (176 shorter events, 170.7 us)
Async XLA Ops:
  0.0 8.3 %copy-start = (bf16[2048,512]{1,0:T(8,128)(2,1)S(1)}, bf16[2048,512]{1,0:T(8,128)(2,1)}, u32[]{:S(2)}) copy-start(bf16[2048,512]{1,0:T(8,128)(2,1)} %param.10) | copy-start | bytes 6291460
  22.4 6.5 %copy-start.5 = (s32[32,8]{0,1:T(8,128)S(1)}, s32[32,8]{0,1:T(8,128)}, u32[]{:S(2)}) copy-start(s32[32,8]{0,1:T(8,128)} %param.15) | copy-start | bytes 3076
  22.4 6.5 %copy-start.6 = (s32[1,4,16]{2,1,0:T(4,128)S(1)}, s32[1,4,16]{2,1,0:T(4,128)}, u32[]{:S(2)}) copy-start(s32[1,4,16]{2,1,0:T(4,128)} %param.16) | copy-start | bytes 772
  22.4 7.3 %copy-start.7 = (s32[1,4,16]{2,1,0:T(4,128)S(1)}, s32[1,4,16]{2,1,0:T(4,128)}, u32[]{:S(2)}) copy-start(s32[1,4,16]{2,1,0:T(4,128)} %param.17) | copy-start | bytes 772
  22.4 75.7 %all-to-all-start = ((bf16[2048,2,768]{2,0,1:T(8,128)(2,1)}), bf16[2048,2,768]{2,0,1:T(8,128)(2,1)}, u32[]{:S(2)}, u32[]{:S(2)}) async-start(bf16[2048,2,768]{2,0,1:T(8,128)(2,1)} %copy.95), calls=%async_computation | async-start | bytes 12582912 | tf_op jit(solution)/shard_map/all_to_all | solution.py:120
  103.7 9.5 %copy-start.8 = (f32[256]{0:T(256)S(1)}, f32[256]{0:T(256)}, u32[]{:S(2)}) copy-start(f32[256]{0:T(256)} %param.14) | copy-start | bytes 3076
  103.7 9.5 %copy-start.9 = (f32[256]{0:T(256)S(1)}, f32[256]{0:T(256)}, u32[]{:S(2)}) copy-start(f32[256]{0:T(256)} %param.13) | copy-start | bytes 3076
  105.5 388.9 %collective-permute-start.5 = (bf16[4096,512]{1,0:T(8,128)(2,1)}, bf16[4096,512]{1,0:T(8,128)(2,1)}, u32[]{:S(2)}, u32[]{:S(2)}) collective-permute-start(bf16[4096,512]{1,0:T(8,128)(2,1)} %slice.74), channel_id=1, source_target_pairs={{0,16},{16,0},{2,18},{18,2},{4,20},{20,4},{6,22},{22,6},{8,24},{24... | collective-permute-start | bytes 12582920 | tf_op jit(solution)/shard_map/ppermute | solution.py:37
  105.6 391.7 %collective-permute-start.4 = (bf16[4096,512]{1,0:T(8,128)(2,1)}, bf16[4096,512]{1,0:T(8,128)(2,1)}, u32[]{:S(2)}, u32[]{:S(2)}) collective-permute-start(bf16[4096,512]{1,0:T(8,128)(2,1)} %slice.74), channel_id=1, source_target_pairs={{0,8},{8,0},{2,10},{10,2},{4,12},{12,4},{6,14},{14,6},{16,24},{24,... | collective-permute-start | bytes 12582920 | tf_op jit(solution)/shard_map/ppermute | solution.py:37
  105.9 395.6 %collective-permute-start.3 = (bf16[4096,512]{1,0:T(8,128)(2,1)}, bf16[4096,512]{1,0:T(8,128)(2,1)}, u32[]{:S(2)}, u32[]{:S(2)}) collective-permute-start(bf16[4096,512]{1,0:T(8,128)(2,1)} %slice.74), channel_id=1, source_target_pairs={{0,4},{4,0},{2,6},{6,2},{8,12},{12,8},{10,14},{14,10},{16,20},{20,... | collective-permute-start | bytes 12582920 | tf_op jit(solution)/shard_map/ppermute | solution.py:37
  107.0 96.1 %collective-permute-start.1 = (bf16[256,512]{1,0:T(8,128)(2,1)S(1)}, bf16[256,512]{1,0:T(8,128)(2,1)S(1)}, u32[]{:S(2)}, u32[]{:S(2)}) collective-permute-start(bf16[256,512]{1,0:T(8,128)(2,1)S(1)} %get-tuple-element.149), channel_id=1, source_target_pairs={{2,0},{4,2},{6,4},{8,6},{10,8},{12,10},{14,12},{16,14},{18,16},{20... | collective-permute-start | bytes 786440 | tf_op jit(solution)/shard_map/ppermute | solution.py:25
  111.3 178.1 %collective-permute-start = (bf16[256,512]{1,0:T(8,128)(2,1)S(1)}, bf16[256,512]{1,0:T(8,128)(2,1)S(1)}, u32[]{:S(2)}, u32[]{:S(2)}) collective-permute-start(bf16[256,512]{1,0:T(8,128)(2,1)S(1)} %get-tuple-element.148), channel_id=1, source_target_pairs={{0,2},{2,4},{4,6},{6,8},{8,10},{10,12},{12,14},{14,16},{16,18},{18... | collective-permute-start | bytes 786440 | tf_op jit(solution)/shard_map/ppermute | solution.py:24
  203.2 302.5 %collective-permute-start.2 = (bf16[4096,512]{1,0:T(8,128)(2,1)}, bf16[4096,512]{1,0:T(8,128)(2,1)}, u32[]{:S(2)}, u32[]{:S(2)}) collective-permute-start(bf16[4096,512]{1,0:T(8,128)(2,1)} %slice.74), channel_id=1, source_target_pairs={{0,2},{2,0},{4,6},{6,4},{8,10},{10,8},{12,14},{14,12},{16,18},{18,... | collective-permute-start | bytes 12582920 | tf_op jit(solution)/shard_map/ppermute | solution.py:37
  316.9 5.0 copy-start.2
  340.4 5.0 copy-start.2
  363.9 5.0 copy-start.2
  387.4 5.0 copy-start.2
  410.8 5.0 copy-start.2
  434.3 5.0 copy-start.2
  457.8 5.0 copy-start.2
  481.3 5.0 copy-start.2
  558.0 3.4 slice-start
  558.0 3.4 copy-start.4
  574.3 2.2 copy-start.3
  620.6 8.1 %copy-start.1 = (bf16[2048,512]{1,0:T(8,128)(2,1)S(1)}, bf16[2048,512]{1,0:T(8,128)(2,1)}, u32[]{:S(2)}) copy-start(bf16[2048,512]{1,0:T(8,128)(2,1)} %param.10) | copy-start | bytes 6291460
where the time goes:
time: 639 us; the launch traced here: 629 us
  local copies, waits for them, and re-layouts  265 us (41%)
  waiting for transfers between devices  122 us (19%)
  starting transfers between devices  100 us (16%)
  matrix products  93.8 us (15%)
  blocking collectives  25.5 us (4%)
  other arithmetic  21.3 us (3%)
    ppermute x4, starting transfers between devices, partner(): return lax.ppermute(block, axis, route)  87.7 us
    all_to_all x1, waiting for transfers between devices, local(): lax.all_to_all(projected, 'head', split_axis=1, concat_axis=0, tiled=True)  68.4 us
    gather x8, local copies, waits for them, and re-layouts, one_group(): ext_tiles[block_columns].reshape(group_size, -1, head_count, double_width)  65.4 us
    reshape x8, local copies, waits for them, and re-layouts, one_group(): ext_tiles[block_columns].reshape(group_size, -1, head_count, double_width)  60.1 us
    ppermute x1, waiting for transfers between devices, padded(): after = lax.ppermute(first, axis, down)  53.7 us
    dot_general x9, matrix products, attend(): jnp.einsum('gqhe,gkhe->ghqk', queries, pair_block, preferred_element_type...  52.8 us
    dot_general x9, matrix products, attend(): jnp.einsum('ghqk,gkhe->gqhe', weights.astype(jnp.bfloat16), pair_block, p...  27.4 us
    all_to_all x1, blocking collectives, local(): lax.all_to_all(result, 'head', split_axis=0, concat_axis=1, tiled=True)  25.5 us
  transfers between devices with their start and end apart: 7, of which 2 were waited for; matrix products, arithmetic and copies ran while one was open for 40% of the time, Pallas kernels for 0%

commit v1 on v0

v1 whole, which is shorter than its diff:
```python
import functools
import math

import jax
import jax.numpy as jnp
from jax import lax
from jax.experimental import pallas as pl
from jax.experimental.pallas import tpu as pltpu
from jax.sharding import PartitionSpec as P

HEADS = 8
TILE = 128
HT = 2
MATCH = 4
LANES = 128
GROUP = 4
MIB = 1024 * 1024

ANY = pl.BlockSpec(memory_space=pl.ANY)
SMEM = pl.BlockSpec(memory_space=pltpu.SMEM)
VMEM = pl.BlockSpec(memory_space=pltpu.VMEM)
HBM = pl.BlockSpec(memory_space=pltpu.HBM)


def piece_copies(pieces, target, sems):
    copies = []
    start = 0
    for index, piece in enumerate(pieces):
        size = piece.shape[0]
        copies.append(
            pltpu.make_async_copy(piece, target.at[pl.ds(start, size)], sems.at[index])
        )
        start += size
    return copies


def lane_masks():
    lane = lax.broadcasted_iota(jnp.int32, (TILE, LANES), 1)
    return lane < LANES // 2, lane % (LANES // 2)


def pack_denominators(pieces):
    _, within = lane_masks()
    size = LANES // 2 // len(pieces)
    packed = pieces[-1]
    for pair in range(len(pieces) - 2, -1, -1):
        packed = jnp.where(within < (pair + 1) * size, pieces[pair], packed)
    return packed


def spread_denominators(packed, pairs):
    size = LANES // 2 // pairs
    inverse = 1.0 / packed
    coarse = inverse.astype(jnp.bfloat16)
    fine = (inverse - coarse.astype(jnp.float32)).astype(jnp.bfloat16)
    shape = (2 * LANES, pairs * LANES)
    source = lax.broadcasted_iota(jnp.int32, shape, 0) % LANES
    target = lax.broadcasted_iota(jnp.int32, shape, 1)
    wanted = target // LANES * size + (target % LANES) // (LANES // 2) * (LANES // 2)
    chooser = jnp.where(source == wanted, 1.0, 0.0).astype(jnp.bfloat16)
    return jnp.dot(
        jnp.concatenate([coarse, fine], axis=1), chooser, preferred_element_type=jnp.float32
    )


def project(rows, w, keys, values, first):
    new_keys = jnp.dot(rows, w[0], preferred_element_type=jnp.float32).astype(jnp.bfloat16).T
    new_values = jnp.dot(rows, w[1], preferred_element_type=jnp.float32).astype(jnp.bfloat16)
    for index in range(rows.shape[0] // TILE):
        span = slice(index * TILE, (index + 1) * TILE)
        keys[first + index] = new_keys[:, span]
        values[first + index] = new_values[span, :]


def attend_row(queries, keys, values, ones, tiles):
    low, _ = lane_masks()
    low_mask = jnp.where(low, 1.0, 0.0).astype(jnp.bfloat16)
    high_mask = jnp.where(low, 0.0, 1.0).astype(jnp.bfloat16)
    results = []
    for pair in range(queries.shape[1] // LANES):
        part = slice(pair * LANES, (pair + 1) * LANES)
        both = jnp.concatenate([queries[:, part] * low_mask, queries[:, part] * high_mask], axis=0)
        weights = []
        for start in range(0, len(tiles), 2):
            slab = jnp.concatenate([keys[tile, part, :] for tile in tiles[start : start + 2]], axis=1)
            scores = jnp.dot(both, slab, preferred_element_type=jnp.float32)
            weights.append(jnp.exp(jnp.clip(scores, -5.0, 5.0)).astype(jnp.bfloat16))
        weights = jnp.concatenate(weights, axis=1)
        wide = jnp.concatenate(
            [
                jnp.concatenate([values[tile, :, part], ones[0]], axis=1) for tile in tiles[:-1]
            ]
            + [jnp.concatenate([values[tiles[-1], :, part] * ones[1], ones[1]], axis=1)],
            axis=0,
        )
        sums = jnp.dot(weights, wide, preferred_element_type=jnp.float32)
        results.append(
            (
                jnp.where(low, sums[:TILE, :LANES], sums[TILE:, :LANES]),
                jnp.where(low, sums[:TILE, LANES:], sums[TILE:, LANES:]),
            )
        )
    return results


def attend_units(queries, keys, values, num, den, units):
    low_lanes, _ = lane_masks()
    low = jnp.where(low_lanes, 1.0, 0.0).astype(jnp.bfloat16)
    high = jnp.where(low_lanes, 0.0, 1.0).astype(jnp.bfloat16)
    nothing = jnp.zeros((LANES // 2, TILE), jnp.bfloat16)
    rows = [pl.ds(pl.multiple_of(row * TILE, TILE), TILE) for row, _ in units]
    last = queries.shape[0] // TILE - 1
    query_rows = [
        pl.ds(pl.multiple_of(jnp.minimum(row, last) * TILE, TILE), TILE) for row, _ in units
    ]
    denominators = [[] for _ in units]
    for pair in range(queries.shape[1] // LANES):
        part = slice(pair * LANES, (pair + 1) * LANES)
        middle = pair * LANES + LANES // 2
        weights = []
        for row, (_, tile) in zip(query_rows, units):
            first = jnp.concatenate([keys[tile, pair * LANES : middle, :], nothing], axis=0)
            second = jnp.concatenate([nothing, keys[tile, middle : (pair + 1) * LANES, :]], axis=0)
            scores = jnp.dot(
                queries[row, part],
                jnp.concatenate([first, second], axis=1),
                preferred_element_type=jnp.float32,
            )
            weights.append(jnp.exp(jnp.clip(scores, -5.0, 5.0)).astype(jnp.bfloat16))
        sums = []
        for weight, (_, tile) in zip(weights, units):
            value = values[tile, :, part]
            wide = jnp.concatenate(
                [
                    jnp.concatenate([value * low, low], axis=1),
                    jnp.concatenate([value * high, high], axis=1),
                ],
                axis=0,
            )
            sums.append(jnp.dot(weight, wide, preferred_element_type=jnp.float32))
        for row, both, listed in zip(rows, sums, denominators):
            num[row, part] += both[:, :LANES]
            listed.append(both[:, LANES:])
    for row, listed in zip(rows, denominators):
        den[row, :] += pack_denominators(listed)


def sums_copies(num, den, num_out, den_out, sems, inward):
    rows = num_out.shape[0]
    copies = []
    for index, (here, there) in enumerate([(num, num_out), (den, den_out)]):
        here = here.at[pl.ds(0, rows)]
        source, target = (there, here) if inward else (here, there)
        copies.append(pltpu.make_async_copy(source, target, sems.at[index]))
    return copies


def project_pieces(pieces, w, keys, values, at):
    for piece in pieces:
        tiles = piece.shape[0] // TILE
        size = math.gcd(tiles, GROUP)

        def some_tiles(index, carry, piece=piece, at=at, size=size):
            some = piece[pl.ds(pl.multiple_of(index * size * TILE, TILE), size * TILE), :]
            project(some, w, keys, values, at + index * size)
            return carry

        lax.fori_loop(0, tiles // size, some_tiles, 0)
        at += tiles


def attend_rows(span, fresh, place_ref, cols_ref, where_ref, local_ref, keys, values, sums, scratch):
    num, den, num_out, den_out = sums
    ones, list_ref, sems = scratch
    width = num.shape[1]
    tiles_here = local_ref.shape[0] // TILE
    slots = cols_ref.shape[1]
    ones[0] = jnp.ones(ones.shape[1:], ones.dtype)
    ones[1] = jnp.zeros(ones.shape[1:], ones.dtype)

    def one_row(row, carry):
        target = pl.ds(pl.multiple_of(row * TILE, TILE), TILE)
        half = row // (tiles_here // 2)
        found = jnp.int32(0)
        for slot in range(slots):
            tile = where_ref[half, cols_ref[place_ref[0] * tiles_here + row, slot]]
            list_ref[found] = tile
            found = found + (tile >= 0).astype(jnp.int32)
        list_ref[found] = 0
        odd = lax.rem(found, 2)
        if fresh:

            @pl.when(found == 0)
            def _():
                num[target, :] = jnp.zeros((TILE, width), jnp.float32)
                den[target, :] = jnp.zeros((TILE, LANES), jnp.float32)

        for chunks in range(1, slots // 2 + 1):

            @pl.when((found + 1) // 2 == chunks)
            def _():
                tiles = [list_ref[index] for index in range(2 * chunks)]
                units = (ones[0], ones[odd])
                results = attend_row(local_ref[target, :], keys, values, units, tiles)
                packed = pack_denominators([denominator for _, denominator in results])
                for pair, (numerator, _) in enumerate(results):
                    part = slice(pair * LANES, (pair + 1) * LANES)
                    num[target, part] = numerator if fresh else num[target, part] + numerator
                den[target, :] = packed if fresh else den[target, :] + packed

        for index, (here, there) in enumerate([(num, num_out), (den, den_out)]):
            pltpu.make_async_copy(here.at[target], there.at[target], sems.at[index]).start()
        return carry

    lax.fori_loop(*span, one_row, 0)
    every = pl.ds(span[0] * TILE, (span[1] - span[0]) * TILE)
    for index, (here, there) in enumerate([(num, num_out), (den, den_out)]):
        pltpu.make_async_copy(here.at[every], there.at[every], sems.at[index]).wait()


def own_kernel(span, place_ref, cols_ref, where_ref, rows, w, wq, scales, *refs):
    (num_out, den_out, keys, values, local_ref, expand_ref, num, den, *scratch) = refs
    width = rows.shape[1]
    tiles = rows.shape[0] // TILE
    size = min(GROUP, tiles)
    project_pieces([rows], w, keys, values, 0)

    def some_queries(index, carry):
        target = pl.ds(pl.multiple_of(index * size * TILE, TILE), size * TILE)
        queries = jnp.dot(rows[target, :], wq[...], preferred_element_type=jnp.float32)
        queries = queries.astype(jnp.bfloat16).astype(jnp.float32)
        scale = 1.0 / math.sqrt(width // HEADS)
        local_ref[target, :] = (queries * scales[0:1, :] * scale).astype(jnp.bfloat16)
        expand_ref[target, :] = (queries * scales[1:2, :] * scale).astype(jnp.bfloat16)
        return carry

    lax.fori_loop(0, tiles // size, some_queries, 0)
    sums = (num, den, num_out, den_out)
    attend_rows(span, True, place_ref, cols_ref, where_ref, local_ref, keys, values, sums, scratch)


def near_kernel(span, count, place_ref, cols_ref, where_ref, *refs):
    pieces = refs[:count]
    (w, local_ref, own_keys, own_values, _, _, num_out, den_out) = refs[count : count + 8]
    (num, den, ones, list_ref, sems, keys, values, own_sems) = refs[count + 8 :]
    tiles = own_keys.shape[0]
    copies = [
        pltpu.make_async_copy(own_keys, keys.at[pl.ds(0, tiles)], own_sems.at[0]),
        pltpu.make_async_copy(own_values, values.at[pl.ds(0, tiles)], own_sems.at[1]),
    ]
    for copy in copies:
        copy.start()
    project_pieces(pieces, w, keys, values, tiles)
    for copy in copies:
        copy.wait()
    sums = (num, den, num_out, den_out)
    scratch = (ones, list_ref, sems)
    attend_rows(span, True, place_ref, cols_ref, where_ref, local_ref, keys, values, sums, scratch)


def rest_kernel(span, count, place_ref, cols_ref, where_ref, *refs):
    pieces = refs[:count]
    (w, local_ref, num_in, den_in, num_out, den_out) = refs[count : count + 6]
    (num, den, ones, list_ref, sems, keys, values, sums_sems) = refs[count + 6 :]
    incoming = sums_copies(num, den, num_in, den_in, sums_sems, True)
    for copy in incoming:
        copy.start()
    project_pieces(pieces, w, keys, values, 0)
    for copy in incoming:
        copy.wait()
    sums = (num, den, num_out, den_out)
    scratch = (ones, list_ref, sems)
    attend_rows(span, False, place_ref, cols_ref, where_ref, local_ref, keys, values, sums, scratch)


def local_call(kernel, tables, pieces, extra, extra_specs, span, sums, more_outs, scratch, limit, flops):
    own_rows, width = extra[1].shape if kernel is not own_kernel else pieces[0].shape
    shapes = [
        jax.ShapeDtypeStruct((own_rows, width), jnp.float32),
        jax.ShapeDtypeStruct((own_rows, LANES), jnp.float32),
    ]
    arguments = [*tables, *pieces, *extra, *(sums or ())]
    aliases = {}
    if sums:
        aliases = {len(arguments) - 2: 0, len(arguments) - 1: 1}
    bound = functools.partial(kernel, span)
    if kernel is not own_kernel:
        bound = functools.partial(kernel, span, len(pieces))
    return pl.pallas_call(
        bound,
        in_specs=[SMEM] * 3 + [VMEM] * len(pieces) + extra_specs + [HBM] * len(sums or ()),
        out_specs=[HBM, HBM] + [VMEM] * len(more_outs),
        out_shape=shapes + more_outs,
        input_output_aliases=aliases,
        scratch_shapes=[
            pltpu.VMEM((own_rows, width), jnp.float32),
            pltpu.VMEM((own_rows, LANES), jnp.float32),
            pltpu.VMEM((2, TILE, LANES), jnp.bfloat16),
            pltpu.SMEM((tables[1].shape[1] + 1,), jnp.int32),
            pltpu.SemaphoreType.DMA((2,)),
        ]
        + scratch,
        compiler_params=pltpu.CompilerParams(vmem_limit_bytes=limit * MIB),
        cost_estimate=pl.CostEstimate(flops=flops, bytes_accessed=10**5, transcendentals=0),
    )(*arguments)


def key_scratch(tiles, width):
    return [
        pltpu.VMEM((tiles, width, TILE), jnp.bfloat16),
        pltpu.VMEM((tiles, TILE, width), jnp.bfloat16),
        pltpu.SemaphoreType.DMA((2,)),
    ]


def own_attention(tables, rows, w, wq, scales, span):
    width = rows.shape[1]
    tiles = rows.shape[0] // TILE
    shapes = [(tiles, width, TILE), (tiles, TILE, width), rows.shape, rows.shape]
    outs = [jax.ShapeDtypeStruct(shape, jnp.bfloat16) for shape in shapes]
    return local_call(
        own_kernel, tables, [rows], [w, wq, scales], [VMEM] * 3, span, None, outs, [], 24, 10**8
    )


def near_attention(tables, pieces, w, local_q, keys, values, num, den, span):
    tiles = keys.shape[0] + sum(piece.shape[0] // TILE for piece in pieces)
    scratch = key_scratch(tiles, local_q.shape[1])
    extra = [w, local_q, keys, values]
    specs = [VMEM, VMEM, ANY, ANY]
    return local_call(
        near_kernel, tables, pieces, extra, specs, span, (num, den), [], scratch, 24, 10**12
    )


def rest_attention(tables, pieces, w, local_q, num, den, span):
    scratch = key_scratch(sum(piece.shape[0] // TILE for piece in pieces), local_q.shape[1])
    extra = [w, local_q]
    return local_call(
        rest_kernel, tables, pieces, extra, [VMEM] * 2, span, (num, den), [], scratch, 24, 10**8
    )


def expand_kernel(count, last, place_ref, rows_ref, spots_ref, *refs):
    sources = refs[:count]
    (expand_q, num_in, den_in, w) = refs[count : count + 4]
    refs = refs[count + 4 :]
    if last:
        (out_ref, features, keys, values, num, den, row_list, tile_list, sems) = refs
    else:
        (num_out, den_out, features, keys, values, num, den, row_list, tile_list, sems) = refs
    own_rows, width = num_in.shape
    tiles_here = own_rows // TILE
    matchings, edges = rows_ref.shape
    copies = piece_copies(sources, features, sems)
    for copy in copies:
        copy.start()

    def clear(tile, carry):
        target = pl.ds(pl.multiple_of(tile * TILE, TILE), TILE)
        num[target, :] = jnp.zeros((TILE, width), jnp.float32)
        den[target, :] = jnp.zeros((TILE, LANES), jnp.float32)
        return carry

    lax.fori_loop(0, tiles_here + 1, clear, 0)

    def visit(edge, found):
        for matching in range(matchings):
            row = rows_ref[matching, edge] - place_ref[0] * tiles_here
            spot = spots_ref[matching, edge]
            mine = jnp.logical_and(jnp.logical_and(row >= 0, row < tiles_here), spot >= 0)
            row_list[found] = row
            tile_list[found] = spot
            found = found + mine.astype(jnp.int32)
        return found

    found = lax.fori_loop(0, edges, visit, jnp.int32(0))
    for inner in range(GROUP):
        row_list[found + inner] = tiles_here
        tile_list[found + inner] = 0
    for copy in copies:
        copy.wait()

    def group(index, carry):
        first = index * GROUP
        some = jnp.concatenate(
            [
                features[pl.ds(pl.multiple_of(tile_list[first + i] * TILE, TILE), TILE), :]
                for i in range(GROUP)
            ],
            axis=0,
        )
        project(some, w, keys, values, 0)
        units = [(row_list[first + i], i) for i in range(GROUP)]
        attend_units(expand_q, keys, values, num, den, units)
        return carry

    lax.fori_loop(0, (found + GROUP - 1) // GROUP, group, 0)

    def finish(tile, carry):
        target = pl.ds(pl.multiple_of(tile * TILE, TILE), TILE)
        total = num_in[target, :] + num[target, :]
        count = den_in[target, :] + den[target, :]
        if last:
            inverse = spread_denominators(count, width // LANES)
            out_ref[target, :] = (total * inverse).astype(jnp.bfloat16)
        else:
            num_out[target, :] = total
            den_out[target, :] = count
        return carry

    lax.fori_loop(0, tiles_here, finish, 0)


def expand_attention(place, exp_rows, spots, sources, expand_q, num, den, w, last):
    own_rows, width = num.shape
    most = exp_rows.shape[0] * exp_rows.shape[1] + GROUP
    tiles = sum(source.shape[0] for source in sources) // TILE
    sums = [jax.ShapeDtypeStruct(num.shape, num.dtype), jax.ShapeDtypeStruct(den.shape, den.dtype)]
    return pl.pallas_call(
        functools.partial(expand_kernel, len(sources), last),
        in_specs=[SMEM] * 3 + [ANY] * len(sources) + [VMEM] * 4,
        out_specs=VMEM if last else [VMEM, VMEM],
        out_shape=jax.ShapeDtypeStruct((own_rows, width), jnp.bfloat16) if last else sums,
        scratch_shapes=[
            pltpu.VMEM((tiles * TILE, width), jnp.bfloat16),
            pltpu.VMEM((GROUP, width, TILE), jnp.bfloat16),
            pltpu.VMEM((GROUP, TILE, width), jnp.bfloat16),
            pltpu.VMEM((own_rows + TILE, width), jnp.float32),
            pltpu.VMEM((own_rows + TILE, LANES), jnp.float32),
            pltpu.SMEM((most,), jnp.int32),
            pltpu.SMEM((most,), jnp.int32),
            pltpu.SemaphoreType.DMA((len(sources),)),
        ],
        compiler_params=pltpu.CompilerParams(vmem_limit_bytes=36 * MIB),
        cost_estimate=pl.CostEstimate(
            flops=own_rows * width * 256, bytes_accessed=own_rows * width, transcendentals=0
        ),
    )(place, exp_rows, spots, *sources, expand_q, num, den, w)


def cut_kernel(margin, here_ref, features, lower, edge, sems):
    start = pl.multiple_of(here_ref[0] * (features.shape[0] - margin), TILE)
    copies = [
        pltpu.make_async_copy(features.at[pl.ds(0, lower.shape[0])], lower, sems.at[0]),
        pltpu.make_async_copy(features.at[pl.ds(start, margin)], edge, sems.at[1]),
    ]
    for copy in copies:
        copy.start()
    for copy in copies:
        copy.wait()


def cut(here, features, margin):
    rows, width = features.shape
    return pl.pallas_call(
        functools.partial(cut_kernel, margin),
        in_specs=[SMEM, ANY],
        out_specs=[VMEM, VMEM],
        out_shape=[
            jax.ShapeDtypeStruct((rows // 2, width), jnp.bfloat16),
            jax.ShapeDtypeStruct((margin, width), jnp.bfloat16),
        ],
        scratch_shapes=[pltpu.SemaphoreType.DMA((2,))],
        compiler_params=pltpu.CompilerParams(vmem_limit_bytes=8 * MIB),
    )(here, features)


def select_kernel(jobs, share, sources, place_ref, *refs):
    matchings = len(refs) - sources - len(jobs)
    wanted = refs[:matchings]
    parts = refs[matchings : matchings + sources]
    outs = refs[matchings + sources :]
    here = place_ref[0]
    even = lax.rem(place_ref[1], 2) == 0
    quarter = parts[1].shape[0] // TILE
    per_part = 2 * quarter
    flat = []
    for (of_even, of_odd, lines), out in zip(jobs, outs):
        at = 0
        for line in lines:
            start = (here if line == 0 else 1 - here) * share
            for slot in range(share):
                tile = wanted[of_even][0, start + slot]
                if of_odd != of_even:
                    tile = jnp.where(even, tile, wanted[of_odd][0, start + slot])
                flat.append((tile, out, at))
                at += 1
    for tile, out, slot in flat:
        own = tile // per_part == here
        lower = lax.rem(tile // quarter, 2) == 0
        target = slice(slot * TILE, (slot + 1) * TILE)

        @pl.when(own)
        def _():
            start = pl.multiple_of(lax.rem(tile, per_part) * TILE, TILE)
            out[target, :] = parts[0][pl.ds(start, TILE), :]

        start = pl.multiple_of(lax.rem(tile, quarter) * TILE, TILE)

        @pl.when(jnp.logical_and(jnp.logical_not(own), lower))
        def _():
            out[target, :] = parts[1][pl.ds(start, TILE), :]

        if sources > 2:

            @pl.when(jnp.logical_not(jnp.logical_or(own, lower)))
            def _():
                out[target, :] = parts[2][pl.ds(start, TILE), :]


def select(place, jobs, share, wanted, parts):
    width = parts[0].shape[1]
    sizes = [share * len(lines) for _, _, lines in jobs]
    return pl.pallas_call(
        functools.partial(select_kernel, jobs, share, len(parts)),
        in_specs=[SMEM] * (1 + len(wanted)) + [VMEM] * len(parts),
        out_specs=[VMEM] * len(jobs),
        out_shape=[jax.ShapeDtypeStruct((size * TILE, width), jnp.bfloat16) for size in sizes],
        compiler_params=pltpu.CompilerParams(vmem_limit_bytes=16 * MIB),
    )(place, *wanted, *parts)


def distinct_kernel(tiles, lines, place_ref, cols_ref, near_ref, last_ref, *refs):
    wanted_refs = refs[:-2]
    mark, rank_of = refs[-2:]
    matchings, edges = cols_ref.shape
    share = edges // lines
    here = place_ref[0]
    odd = lax.rem(place_ref[1], 2)
    every = range(matchings)

    def clear(tile, carry):
        for matching in every:
            mark[matching, tile] = 0
        return carry

    def count(edge, missing):
        left = []
        for matching in every:
            tile = cols_ref[matching, edge]
            left.append(missing[matching] - (1 - mark[matching, tile]))
            mark[matching, tile] = 1
        return tuple(left)

    def place(at, carry):
        quarter = tiles // 4
        tile = jnp.where(at < quarter, at + quarter, jnp.where(at < 2 * quarter, at - quarter, at))
        ranks, left = [], []
        for matching, (rank, missing) in enumerate(zip(*carry)):
            present = mark[matching, tile]
            added = jnp.where(jnp.logical_and(present == 0, missing > 0), 1, 0)
            wanted_refs[matching][0, rank] = tile
            rank_of[matching, tile] = rank
            ranks.append(rank + present + added)
            left.append(missing - added)
        return tuple(ranks), tuple(left)

    def look_up(edge, carry):
        for matching in every:
            slot = rank_of[matching, cols_ref[matching, edge]]
            away = jnp.where(slot // share == here, 0, 1)
            within = lax.rem(slot, share)
            if matching < matchings - 2:
                near_ref[matching, edge] = (2 * matching + away) * share + within
                last_ref[matching, edge] = -1
            else:
                second = odd if matching == matchings - 1 else 1 - odd
                third = 2 * (matchings - 2)
                near = jnp.where(away == 0, third + second, third + 2)
                later = jnp.logical_and(away == 1, second == 1)
                near_ref[matching, edge] = jnp.where(later, -1, near * share + within)
                last_ref[matching, edge] = jnp.where(later, within, -1)
        return carry

    zero = jnp.int32(0)
    lax.fori_loop(0, tiles, clear, 0)
    missing = lax.fori_loop(0, edges, count, (jnp.int32(edges),) * matchings)
    lax.fori_loop(0, tiles, place, ((zero,) * matchings, missing))
    lax.fori_loop(0, edges, look_up, 0)


def distinct_slots(place, cols, tiles, lines):
    matchings, edges = cols.shape
    wanted = jax.ShapeDtypeStruct((1, 2 * edges), jnp.int32)
    spots = jax.ShapeDtypeStruct(cols.shape, jnp.int32)
    near, last, *wanted = pl.pallas_call(
        functools.partial(distinct_kernel, tiles, lines),
        in_specs=[SMEM, SMEM],
        out_specs=[SMEM] * (2 + matchings),
        out_shape=[spots, spots] + [wanted] * matchings,
        scratch_shapes=[pltpu.SMEM((matchings, tiles), jnp.int32)] * 2,
        cost_estimate=pl.CostEstimate(flops=10**11, bytes_accessed=4096, transcendentals=0),
    )(place, cols)
    return near, last, wanted


def local(features, w_query, w_key_value, edge_local, edge_expand, local_cols, exp_rows, exp_cols):
    groups = lax.axis_size("head")
    blocks = lax.axis_size("node")
    own_rows, width = features.shape
    here = lax.axis_index("head")
    block = lax.axis_index("node")
    edges = exp_cols.shape[2]
    tiles = local_cols.shape[0]
    own_tiles = own_rows // TILE
    margin = HT * TILE
    exp_rows, exp_cols = exp_rows[0], exp_cols[0]
    log_count = blocks.bit_length() - 1
    flips = [1 << matching * log_count // MATCH for matching in range(MATCH)]

    def swap(x, matching, of_odd=None):
        flip = [flips[matching], flips[matching if of_odd is None else of_odd]]
        return lax.ppermute(x, "node", [(i, i ^ flip[i % 2]) for i in range(blocks)])

    def other(x):
        return lax.ppermute(x, "head", [(0, 1), (1, 0)])

    scales = jnp.stack([edge_local, edge_expand])
    two = groups == 2 and min(flips[2:]) > 1
    if two:
        lower, edge_rows = cut(jnp.reshape(here, (1,)).astype(jnp.int32), features, margin)
        beside = other(scales)
        lower, edge_rows, exp_cols, beside, w_query, w_key_value, block, here = (
            lax.optimization_barrier(
                (lower, edge_rows, exp_cols, beside, w_query, w_key_value, block, here)
            )
        )
    place = jnp.stack([here, block]).astype(jnp.int32)
    column = jnp.arange(tiles + 2 * HT, dtype=jnp.int32) - HT
    usable = block * tiles + column
    usable = jnp.logical_and(usable >= 0, usable < blocks * tiles)
    own = column // own_tiles == here
    own_place = column - here * own_tiles
    split = own_tiles // 2

    if two:
        half = own_rows // 2
        quarter = own_tiles // 2
        lower_here = column // quarter % 2 == 0
        inside = jnp.logical_and(column >= 0, column < tiles)
        after = column >= tiles
        in_halo = jnp.where(after, column - tiles, column + HT)
        in_halo += jnp.where(after == (here == 0), 2 * quarter + HT, 2 * quarter)
        place_in = jnp.where(lower_here, column % quarter, quarter + column % quarter)
        rest = jnp.where(inside, place_in, in_halo)
        near = jnp.where(own, own_place, own_tiles + place_in)
        near = jnp.where(jnp.logical_and(inside, jnp.logical_or(own, lower_here)), near, -1)
        rest_low = jnp.where(jnp.logical_and(usable, jnp.logical_not(own)), rest, -1)
        rest_high = jnp.where(jnp.logical_and(usable, near < 0), rest, -1)
        where_own = jnp.where(own, own_place, -1)
        tables = jnp.stack([where_own, where_own, near, near, rest_low, rest_high])
        w = jnp.transpose(w_key_value, (1, 0, 2))
        lower = other(lower)
        near_spots, last_spots, wanted = distinct_slots(place, exp_cols, tiles, groups)
        edge_rows, *wanted = lax.optimization_barrier((edge_rows, *wanted))
        route = [(2 * i, 2 * i - 2) for i in range(1, blocks)]
        route += [(2 * i + 1, 2 * i + 3) for i in range(blocks - 1)]
        halo = lax.ppermute(edge_rows, ("node", "head"), route)
        wanted = [swap(wanted[m], m) for m in range(MATCH)]
        upper = jnp.concatenate([features[half:], halo], axis=0)
        scales = jnp.where(
            here == 0,
            jnp.concatenate([scales, beside], axis=1),
            jnp.concatenate([beside, scales], axis=1),
        )
        num, den, keys, values, local_q, expand_q = own_attention(
            (place, local_cols, tables[:2]), features, w, w_query, scales, (0, split)
        )
        where_near, where_rest = tables[2:4], tables[4:]
        lower, upper, num, den, where_near, where_rest = lax.optimization_barrier(
            (lower, upper, num, den, where_near, where_rest)
        )
        upper = other(upper)
        share = edges // groups
        sources = [features, lower]
        chosen = select(place, ((3, 2, (0,)), (2, 3, (0,)), (1, 1, (0,))), share, wanted, sources)
        where_near, *chosen = lax.optimization_barrier((where_near, *chosen))
        first = swap(chosen[0], 3, 2)
        second = swap(chosen[1], 2, 3)
        early = swap(chosen[2], 1)
        num, den = near_attention(
            (place, local_cols, where_near),
            [lower],
            w,
            local_q,
            keys,
            values,
            num,
            den,
            (split, own_tiles),
        )
        upper, num, den = lax.optimization_barrier((upper, num, den))
        sources = [features, lower, upper]
        chosen = select(place, ((1, 1, (1,)), (0, 0, (0, 1))), share, wanted, sources)
        where_rest, first, early, *chosen = lax.optimization_barrier(
            (where_rest, first, early, *chosen)
        )
        first_beside = other(first)
        late = swap(chosen[0], 1)
        pair = swap(chosen[1], 0)
        num, den = rest_attention(
            (place, local_cols, where_rest),
            [lower, upper, halo],
            w,
            local_q,
            num,
            den,
            (0, own_tiles),
        )
        second, num, den = lax.optimization_barrier((second, num, den))
        last_sources = [other(second)]
        near_sources = [pair, early, late, first, second, first_beside]
    else:
        w = jnp.transpose(w_key_value, (1, 0, 2))
        gather = lambda x: lax.all_gather(x, "head", axis=0, tiled=True)
        scales = lax.all_gather(scales, "head", axis=1, tiled=True)
        full = gather(features)
        before = lax.ppermute(full[-margin:], "node", [(i, i + 1) for i in range(blocks - 1)])
        after = lax.ppermute(full[:margin], "node", [(i + 1, i) for i in range(blocks - 1)])
        received = [gather(swap(features, m)) for m in range(MATCH)]
        near_sources, last_sources = received[:2], received[2:]
        matching = jnp.arange(MATCH, dtype=jnp.int32)[:, None]
        near_spots = jnp.where(matching < 2, matching * tiles + exp_cols, -1)
        last_spots = jnp.where(matching < 2, -1, (matching - 2) * tiles + exp_cols)
        where_own = jnp.where(own, own_place, -1)
        where_own = jnp.stack([where_own, where_own])
        where_rest = jnp.where(jnp.logical_and(usable, jnp.logical_not(own)), column + HT, -1)
        where_rest = jnp.stack([where_rest, where_rest])
        num, den, keys, values, local_q, expand_q = own_attention(
            (place, local_cols, where_own), features, w, w_query, scales, (0, own_tiles)
        )
        num, den = rest_attention(
            (place, local_cols, where_rest),
            [before, full, after],
            w,
            local_q,
            num,
            den,
            (0, own_tiles),
        )
    num, den = expand_attention(
        place, exp_rows, near_spots, near_sources, expand_q, num, den, w, False
    )
    return expand_attention(
        place, exp_rows, last_spots, last_sources, expand_q, num, den, w, True
    )


def solution(mesh):
    return jax.shard_map(
        local,
        mesh=mesh,
        in_specs=(
            P(("node", "head"), None),
            P(),
            P(),
            P("head"),
            P("head"),
            P("node", None),
            P("node", None, None),
            P("node", None, None),
        ),
        out_specs=P(("node", "head"), None),
        check_vma=False,
    )
```

time: 639 us -> 132 us (0.21)
  the two profiles are of different devices: /device:TPU:25 before, /device:TPU:0 now
where the time goes in v1:
time: 132 us
  Pallas kernels  85.7 us (65%)
  starting transfers between devices  20.1 us (15%)
  waiting for transfers between devices  18.4 us (14%)
  local copies, waits for them, and re-layouts  4.17 us (3%)
  other arithmetic  2.73 us (2%)
    pallas_call x3, Pallas kernels, local_call(): pl.pallas_call(bound, in_specs=[SMEM] * 3 + [VMEM] * len(pieces) + extra_...  48.6 us
    pallas_call x2, Pallas kernels, expand_attention(): pl.pallas_call(functools.partial(expand_kernel, len(sources), last), in_s...  27.6 us
    ppermute x5, waiting for transfers between devices, other(): return lax.ppermute(x, 'head', [(0, 1), (1, 0)])  18.3 us
    ppermute x9, starting transfers between devices, swap(): lax.ppermute(x, 'node', [(i, i ^ flip[i % 2]) for i in range(blocks)])  12 us
    ppermute x5, starting transfers between devices, other(): return lax.ppermute(x, 'head', [(0, 1), (1, 0)])  6.74 us
    pallas_call x2, Pallas kernels, select(): pl.pallas_call(functools.partial(select_kernel, jobs, share, len(parts)),...  4.82 us
    pallas_call x1, Pallas kernels, distinct_slots(): pl.pallas_call(functools.partial(distinct_kernel, tiles, lines), in_specs...  3.48 us
    unnamed x25, local copies, waits for them, and re-layouts  2.78 us
  transfers between devices with their start and end apart: 15, of which 4 were waited for; matrix products, arithmetic and copies ran while one was open for 3% of the time, Pallas kernels for 58%

profile of v1, /device:TPU:0, one launch (start us, length us, event | category | flops | bytes accessed | tf_op | source)
XLA Modules:
  0.0 131.5 jit_solution(6522065166785076944)
XLA Ops:
  0.0 0.9 pad_maximum_fusion.1
  0.9 3.0 %collective-permute-start = (f32[2,256]{1,0:T(2,128)S(1)}, f32[2,256]{1,0:T(2,128)S(1)}, u32[]{:S(2)}, u32[]{:S(2)}) collective-permute-start(f32[2,256]{1,0:T(2,128)S(1)} %pad_maximum_fusion.1), channel_id=1, source_target_pairs={{0,1},{1,0},{2,3},{3,2},{4,5},{5,4},{6,7},{7,6},{8,9},{9,8},{10,11... | collective-permute-start | bytes 6152 | tf_op jit(solution)/shard_map/ppermute | solution.py:617
  3.8 0.8 copy.14.cols_ref
  4.6 1.1 shard_map.82
  5.7 1.7 %collective-permute-start.1 = (bf16[1024,512]{1,0:T(8,128)(2,1)}, bf16[1024,512]{1,0:T(8,128)(2,1)S(1)}, u32[]{:S(2)}, u32[]{:S(2)}) collective-permute-start(bf16[1024,512]{1,0:T(8,128)(2,1)} %get-tuple-element.70), channel_id=1, source_target_pairs={{0,1},{1,0},{2,3},{3,2},{4,5},{5,4},{6,7},{7,6},{8,9},{9,8},{10,11... | collective-permute-start | bytes 3145736 | tf_op jit(solution)/shard_map/ppermute | solution.py:617
  7.4 0.6 pad_add_fusion.3.place_ref
  8.1 3.5 %shard_map.83 = (s32[4,16]{1,0:T(4,128)}, s32[4,16]{1,0:T(4,128)}, s32[1,32]{1,0:T(1,128)}, s32[1,32]{1,0:T(1,128)}, s32[1,32]{1,0:T(1,128)}, /*index=5*/s32[1,32]{1,0:T(1,128)}) custom-call(s32[2]{0:T(128)} %pad_add_fusion.3.place_ref, s32[4,16]{1,0:T(4,128)} %bitcast.21), custom_call_target="tpu_custom_call" | custom-call | flops 99999997952 | bytes 4096 | tf_op jit(solution)/shard_map/pallas_call | solution.py:587
  11.6 1.4 %collective-permute-start.2 = (bf16[256,512]{1,0:T(8,128)(2,1)S(1)}, bf16[256,512]{1,0:T(8,128)(2,1)S(1)}, u32[]{:S(2)}, u32[]{:S(2)}) collective-permute-start(bf16[256,512]{1,0:T(8,128)(2,1)S(1)} %get-tuple-element.76), channel_id=1, source_target_pairs={{2,0},{4,2},{6,4},{8,6},{10,8},{12,10},{14,12},{16,14},{18,16},{20... | collective-permute-start | bytes 786440 | tf_op jit(solution)/shard_map/ppermute | solution.py:659
  13.1 1.2 collective-permute-start.3
  14.3 1.5 %collective-permute-start.4 = (s32[1,32]{1,0:T(1,128)}, s32[1,32]{1,0:T(1,128)S(1)}, u32[]{:S(2)}, u32[]{:S(2)}) collective-permute-start(s32[1,32]{1,0:T(1,128)} %get-tuple-element.84), channel_id=1, source_target_pairs={{0,4},{2,6},{4,0},{6,2},{8,12},{10,14},{12,8},{14,10},{16,20},{18,... | collective-permute-start | bytes 392 | tf_op jit(solution)/shard_map/ppermute | solution.py:614
  15.8 1.6 %collective-permute-start.5 = (s32[1,32]{1,0:T(1,128)}, s32[1,32]{1,0:T(1,128)S(1)}, u32[]{:S(2)}, u32[]{:S(2)}) collective-permute-start(s32[1,32]{1,0:T(1,128)} %get-tuple-element.85), channel_id=1, source_target_pairs={{0,8},{2,10},{4,12},{6,14},{8,0},{10,2},{12,4},{14,6},{16,24},{18,... | collective-permute-start | bytes 392 | tf_op jit(solution)/shard_map/ppermute | solution.py:614
  17.4 1.4 %copy.18 = bf16[512,2,512]{2,0,1:T(8,128)(2,1)S(1)} copy(bf16[512,2,512]{2,1,0:T(2,128)(2,1)} %param.10) | data formatting | bytes 2097152 | tf_op jit(solution)/shard_map/optimization_barrier | solution.py:625
  18.8 14.2 %shard_map.84 = (f32[2048,512]{1,0:T(8,128)S(1)}, f32[2048,128]{1,0:T(8,128)S(1)}, bf16[16,512,128]{2,1,0:T(8,128)(2,1)S(1)}, bf16[16,128,512]{2,1,0:T(8,128)(2,...) custom-call(s32[2]{0:T(128)S(1)} %copy-done.5, s32[32,8]{1,0:T(8,128)S(1)} %copy.14.cols_ref, ...), custom_call_target="tpu_custom_call" | custom-call | flops 100000000 | bytes 100000 | tf_op jit(solution)/shard_map/pallas_call | solution.py:289
  33.1 3.4 %collective-permute-start.6 = (s32[1,32]{1,0:T(1,128)S(1)}, s32[1,32]{1,0:T(1,128)S(1)}, u32[]{:S(2)}, u32[]{:S(2)}) collective-permute-start(s32[1,32]{1,0:T(1,128)S(1)} %copy-done.11), channel_id=1, source_target_pairs={{0,16},{2,18},{4,20},{6,22},{8,24},{10,26},{12,28},{14,30},{16,0},... | collective-permute-start | bytes 392 | tf_op jit(solution)/shard_map/ppermute | solution.py:614
  36.5 1.1 pad_maximum_fusion
  37.6 0.3 collective-permute-start.10
  37.9 0.1 collective-permute-done.6.refs_3_
  38.0 2.5 %shard_map.85 = (bf16[1024,512]{1,0:T(8,128)(2,1)}, bf16[1024,512]{1,0:T(8,128)(2,1)S(1)}, bf16[1024,512]{1,0:T(8,128)(2,1)}) custom-call(s32[2]{0:T(128)S(1)} %copy-done.5, s32[1,32]{1,0:T(1,128)S(1)} %collective-permute-done.3.refs_0_, s32[1,32]{1,0:T(1,128)S(1)} %collective-permute-done.4.refs_1_, s32[1,32]{1,0:T(1,128)S(1)} %collective-permute-done.5.refs_2_, ...), custom_call_target="tpu_custom_call" | custom-call | tf_op jit(solution)/shard_map/pallas_call | solution.py:515
  40.5 2.9 %collective-permute-start.8 = (bf16[1024,512]{1,0:T(8,128)(2,1)}, bf16[1024,512]{1,0:T(8,128)(2,1)}, u32[]{:S(2)}, u32[]{:S(2)}) collective-permute-start(bf16[1024,512]{1,0:T(8,128)(2,1)} %get-tuple-element.93), channel_id=1, source_target_pairs={{0,16},{2,10},{4,20},{6,14},{8,24},{10,2},{12,28},{14,6},{16,0},{1... | collective-permute-start | bytes 3145736 | tf_op jit(solution)/shard_map/ppermute | solution.py:614
  43.4 12.7 %shard_map.86 = (f32[2048,512]{1,0:T(8,128)S(1)}, f32[2048,128]{1,0:T(8,128)S(1)}) custom-call(s32[2]{0:T(128)S(1)} %copy-done.5, s32[32,8]{1,0:T(8,128)S(1)} %copy.14.cols_ref, s32[2,36]{1,0:T(2,128)S(1)} %pad_add_fusion.1.where_ref, bf16[1024,512]{1,0:T(8,128)(2,1)S(1)} %collective-permute-done.1.refs_5_.refs_0_, ...), custom_call_target="tpu_custom_call", output_to_operand_aliasing={{0}: (8, {}), {1}: (9, {})} | custom-call | flops 999999995904 | bytes 100000 | tf_op jit(solution)/shard_map/pallas_call | solution.py:289
  56.1 11.0 %collective-permute-done.10.refs_6_.refs_1_ = bf16[1280,512]{1,0:T(8,128)(2,1)} collective-permute-done((bf16[1280,512]{1,0:T(8,128)(2,1)}, bf16[1280,512]{1,0:T(8,128)(2,1)}, u32[]{:S(2)}, u32[]{:S(2)}) %collective-permute-start.10) | collective-permute-done | bytes 1310752 | tf_op jit(solution)/shard_map/ppermute | solution.py:617
  67.1 2.3 %shard_map.87 = (bf16[1024,512]{1,0:T(8,128)(2,1)S(1)}, bf16[2048,512]{1,0:T(8,128)(2,1)S(1)}) custom-call(s32[2]{0:T(128)S(1)} %copy-done.5, s32[1,32]{1,0:T(1,128)S(1)} %collective-permute-done.3.refs_0_, s32[1,32]{1,0:T(1,128)S(1)} %collective-permute-done.4.refs_1_, s32[1,32]{1,0:T(1,128)S(1)} %collective-permute-done.5.refs_2_, ...), custom_call_target="tpu_custom_call" | custom-call | tf_op jit(solution)/shard_map/pallas_call | solution.py:515
  69.5 0.1 collective-permute-start.12
  69.6 0.9 collective-permute-start.7
  70.5 0.4 collective-permute-start.13
  70.9 1.8 %collective-permute-start.14 = (bf16[1024,512]{1,0:T(8,128)(2,1)}, bf16[1024,512]{1,0:T(8,128)(2,1)S(1)}, u32[]{:S(2)}, u32[]{:S(2)}) collective-permute-start(bf16[1024,512]{1,0:T(8,128)(2,1)} %collective-permute-done.8.refs_3_), channel_id=1, source_target_pairs={{0,1},{1,0},{2,3},{3,2},{4,5},{5,4},{6,7},{7,6},{8,9},{9,8},{10,11... | collective-permute-start | bytes 3145736 | tf_op jit(solution)/shard_map/ppermute | solution.py:617
  72.6 21.8 %shard_map.88 = (f32[2048,512]{1,0:T(8,128)S(1)}, f32[2048,128]{1,0:T(8,128)S(1)}) custom-call(s32[2]{0:T(128)S(1)} %copy-done.5, s32[32,8]{1,0:T(8,128)S(1)} %copy.14.cols_ref, s32[2,36]{1,0:T(2,128)S(1)} %pad_add_fusion.2.where_ref, bf16[1024,512]{1,0:T(8,128)(2,1)S(1)} %collective-permute-done.1.refs_5_.refs_0_, ...), custom_call_target="tpu_custom_call", output_to_operand_aliasing={{0}: (8, {}), {1}: (9, {})} | custom-call | flops 100000000 | bytes 100000 | tf_op jit(solution)/shard_map/pallas_call | solution.py:289
  94.5 2.0 %copy-done.1 = f32[2048,512]{1,0:T(8,128)} copy-done((f32[2048,512]{1,0:T(8,128)}, f32[2048,512]{1,0:T(8,128)S(1)}, u32[]{:S(2)}) %copy-start.1) | copy-done | bytes 4194328
  96.4 0.1 collective-permute-done.14.refs_5_
  96.5 18.1 %shard_map.89 = (f32[2048,512]{1,0:T(8,128)S(1)}, f32[2048,128]{1,0:T(8,128)S(1)}) custom-call(s32[2]{0:T(128)S(1)} %copy-done.5, s32[4,16]{1,0:T(4,128)S(1)} %bitcast.15, s32[4,16]{1,0:T(4,128)S(1)} %copy-done.8, bf16[2048,512]{1,0:T(8,128)(2,1)S(1)} %collective-permute-done.12.refs_0_, bf16[1024,512]{1,0:T(8,128)(2,1)} %collective-permute-done.9.refs_1_, ...), custom_call_target="tpu_custom_call" | custom-call | flops 268435456 | bytes 1048576 | tf_op jit(solution)/shard_map/pallas_call | solution.py:420
  114.6 7.2 %collective-permute-done.11.refs_0_ = bf16[1024,512]{1,0:T(8,128)(2,1)S(1)} collective-permute-done((bf16[1024,512]{1,0:T(8,128)(2,1)S(1)}, bf16[1024,512]{1,0:T(8,128)(2,1)S(1)}, u32[]{:S(2)}, u32[]{:S(2)}) %collective-permute-start.11) | collective-permute-done | bytes 1048608 | tf_op jit(solution)/shard_map/ppermute | solution.py:617
  121.8 9.5 %shard_map.90 = bf16[2048,512]{1,0:T(8,128)(2,1)} custom-call(s32[2]{0:T(128)S(1)} %copy-done.5, s32[4,16]{1,0:T(4,128)S(1)} %bitcast.16, s32[4,16]{1,0:T(4,128)S(1)} %copy-done.7, bf16[1024,512]{1,0:T(8,128)(2,1)S(1)} %collective-permute-done.11.refs_0_, bf16[2048,512]{1,0:T(8,128)(2,1)S(1)} %get-tuple-element.113.refs_6_.refs_1_, ...), custom_call_target="tpu_custom_call" | custom-call | flops 268435456 | bytes 1048576 | tf_op jit(solution)/shard_map/pallas_call | solution.py:420
  (44 shorter events, 0.2 us)
Async XLA Ops:
  0.0 4.6 %copy-start = (bf16[2048,512]{1,0:T(8,128)(2,1)S(1)}, bf16[2048,512]{1,0:T(8,128)(2,1)}, u32[]{:S(2)}) copy-start(bf16[2048,512]{1,0:T(8,128)(2,1)} %refs_4_.3) | copy-start | bytes 6291460
  0.9 4.8 %collective-permute-start = (f32[2,256]{1,0:T(2,128)S(1)}, f32[2,256]{1,0:T(2,128)S(1)}, u32[]{:S(2)}, u32[]{:S(2)}) collective-permute-start(f32[2,256]{1,0:T(2,128)S(1)} %pad_maximum_fusion.1), channel_id=1, source_target_pairs={{0,1},{1,0},{2,3},{3,2},{4,5},{5,4},{6,7},{7,6},{8,9},{9,8},{10,11... | collective-permute-start | bytes 6152 | tf_op jit(solution)/shard_map/ppermute | solution.py:617
  5.7 31.9 %collective-permute-start.1 = (bf16[1024,512]{1,0:T(8,128)(2,1)}, bf16[1024,512]{1,0:T(8,128)(2,1)S(1)}, u32[]{:S(2)}, u32[]{:S(2)}) collective-permute-start(bf16[1024,512]{1,0:T(8,128)(2,1)} %get-tuple-element.70), channel_id=1, source_target_pairs={{0,1},{1,0},{2,3},{3,2},{4,5},{5,4},{6,7},{7,6},{8,9},{9,8},{10,11... | collective-permute-start | bytes 3145736 | tf_op jit(solution)/shard_map/ppermute | solution.py:617
  8.1 5.0 %copy-start.9 = (f32[256]{0:T(256)S(1)}, f32[256]{0:T(256)}, u32[]{:S(2)}) copy-start(f32[256]{0:T(256)} %param.12) | copy-start | bytes 3076
  8.1 5.0 %copy-start.10 = (f32[256]{0:T(256)S(1)}, f32[256]{0:T(256)}, u32[]{:S(2)}) copy-start(f32[256]{0:T(256)} %param.11) | copy-start | bytes 3076
  11.5 7.3 %copy-start.5 = (s32[2]{0:T(128)S(1)}, s32[2]{0:T(128)}, u32[]{:S(2)}) copy-start(s32[2]{0:T(128)} %pad_add_fusion.3.place_ref) | copy-start | bytes 28
  11.6 7.2 %copy-start.4 = (bf16[512,512]{1,0:T(8,128)(2,1)S(1)}, bf16[512,512]{1,0:T(8,128)(2,1)}, u32[]{:S(2)}) copy-start(bf16[512,512]{1,0:T(8,128)(2,1)} %wq) | copy-start | bytes 1572868
  11.6 21.5 %collective-permute-start.2 = (bf16[256,512]{1,0:T(8,128)(2,1)S(1)}, bf16[256,512]{1,0:T(8,128)(2,1)S(1)}, u32[]{:S(2)}, u32[]{:S(2)}) collective-permute-start(bf16[256,512]{1,0:T(8,128)(2,1)S(1)} %get-tuple-element.76), channel_id=1, source_target_pairs={{2,0},{4,2},{6,4},{8,6},{10,8},{12,10},{14,12},{16,14},{18,16},{20... | collective-permute-start | bytes 786440 | tf_op jit(solution)/shard_map/ppermute | solution.py:659
  13.1 24.8 %collective-permute-start.3 = (s32[1,32]{1,0:T(1,128)}, s32[1,32]{1,0:T(1,128)S(1)}, u32[]{:S(2)}, u32[]{:S(2)}) collective-permute-start(s32[1,32]{1,0:T(1,128)} %get-tuple-element.83), channel_id=1, source_target_pairs={{0,2},{2,0},{4,6},{6,4},{8,10},{10,8},{12,14},{14,12},{16,18},{18,... | collective-permute-start | bytes 392 | tf_op jit(solution)/shard_map/ppermute | solution.py:614
  14.3 23.6 %collective-permute-start.4 = (s32[1,32]{1,0:T(1,128)}, s32[1,32]{1,0:T(1,128)S(1)}, u32[]{:S(2)}, u32[]{:S(2)}) collective-permute-start(s32[1,32]{1,0:T(1,128)} %get-tuple-element.84), channel_id=1, source_target_pairs={{0,4},{2,6},{4,0},{6,2},{8,12},{10,14},{12,8},{14,10},{16,20},{18,... | collective-permute-start | bytes 392 | tf_op jit(solution)/shard_map/ppermute | solution.py:614
  15.8 22.1 %collective-permute-start.5 = (s32[1,32]{1,0:T(1,128)}, s32[1,32]{1,0:T(1,128)S(1)}, u32[]{:S(2)}, u32[]{:S(2)}) collective-permute-start(s32[1,32]{1,0:T(1,128)} %get-tuple-element.85), channel_id=1, source_target_pairs={{0,8},{2,10},{4,12},{6,14},{8,0},{10,2},{12,4},{14,6},{16,24},{18,... | collective-permute-start | bytes 392 | tf_op jit(solution)/shard_map/ppermute | solution.py:614
  18.8 14.3 %copy-start.11 = (s32[1,32]{1,0:T(1,128)S(1)}, s32[1,32]{1,0:T(1,128)}, u32[]{:S(2)}) copy-start(s32[1,32]{1,0:T(1,128)} %get-tuple-element.86) | copy-start | bytes 388
  18.8 17.7 %slice-start = ((bf16[2048,512]{1,0:T(8,128)(2,1)}), bf16[1024,512]{1,0:T(8,128)(2,1)S(1)}, s32[]{:S(2)}) async-start(bf16[2048,512]{1,0:T(8,128)(2,1)} %refs_4_.3), calls=%async_computation | async-start | bytes 2097152 | tf_op jit(solution)/shard_map/slice | solution.py:661
  33.1 7.5 %copy-start.2 = (bf16[256,512]{1,0:T(8,128)(2,1)}, bf16[256,512]{1,0:T(8,128)(2,1)S(1)}, u32[]{:S(2)}) copy-start(bf16[256,512]{1,0:T(8,128)(2,1)S(1)} %collective-permute-done.2.refs_2_) | copy-start | bytes 786436
  33.1 4.9 %collective-permute-start.6 = (s32[1,32]{1,0:T(1,128)S(1)}, s32[1,32]{1,0:T(1,128)S(1)}, u32[]{:S(2)}, u32[]{:S(2)}) collective-permute-start(s32[1,32]{1,0:T(1,128)S(1)} %copy-done.11), channel_id=1, source_target_pairs={{0,16},{2,18},{4,20},{6,22},{8,24},{10,26},{12,28},{14,30},{16,0},... | collective-permute-start | bytes 392 | tf_op jit(solution)/shard_map/ppermute | solution.py:614
  37.6 29.5 %collective-permute-start.10 = (bf16[1280,512]{1,0:T(8,128)(2,1)}, bf16[1280,512]{1,0:T(8,128)(2,1)}, u32[]{:S(2)}, u32[]{:S(2)}) collective-permute-start(bf16[1280,512]{1,0:T(8,128)(2,1)} %pad_maximum_fusion), channel_id=1, source_target_pairs={{0,1},{1,0},{2,3},{3,2},{4,5},{5,4},{6,7},{7,6},{8,9},{9,8},{10,11... | collective-permute-start | bytes 3932168 | tf_op jit(solution)/shard_map/ppermute | solution.py:617
  40.5 28.9 %collective-permute-start.8 = (bf16[1024,512]{1,0:T(8,128)(2,1)}, bf16[1024,512]{1,0:T(8,128)(2,1)}, u32[]{:S(2)}, u32[]{:S(2)}) collective-permute-start(bf16[1024,512]{1,0:T(8,128)(2,1)} %get-tuple-element.93), channel_id=1, source_target_pairs={{0,16},{2,10},{4,20},{6,14},{8,24},{10,2},{12,28},{14,6},{16,0},{1... | collective-permute-start | bytes 3145736 | tf_op jit(solution)/shard_map/ppermute | solution.py:614
  43.4 26.0 %collective-permute-start.9 = (bf16[1024,512]{1,0:T(8,128)(2,1)}, bf16[1024,512]{1,0:T(8,128)(2,1)}, u32[]{:S(2)}, u32[]{:S(2)}) collective-permute-start(bf16[1024,512]{1,0:T(8,128)(2,1)} %get-tuple-element.94), channel_id=1, source_target_pairs={{0,4},{2,6},{4,0},{6,2},{8,12},{10,14},{12,8},{14,10},{16,20},{18,... | collective-permute-start | bytes 3145736 | tf_op jit(solution)/shard_map/ppermute | solution.py:614
  67.1 5.5 %copy-start.3 = (bf16[256,512]{1,0:T(8,128)(2,1)S(1)}, bf16[256,512]{1,0:T(8,128)(2,1)}, u32[]{:S(2)}) copy-start(bf16[256,512]{1,0:T(8,128)(2,1)} %copy-done.2) | copy-start | bytes 786436
  69.5 27.0 %copy-start.6 = (s32[1,4,16]{2,1,0:T(4,128)S(1)}, s32[1,4,16]{2,1,0:T(4,128)}, u32[]{:S(2)}) copy-start(s32[1,4,16]{2,1,0:T(4,128)} %param.14) | copy-start | bytes 772
  69.5 27.0 %copy-start.8 = (s32[4,16]{1,0:T(4,128)S(1)}, s32[4,16]{1,0:T(4,128)}, u32[]{:S(2)}) copy-start(s32[4,16]{1,0:T(4,128)} %get-tuple-element.114.spots_ref) | copy-start | bytes 772
  69.5 27.0 %collective-permute-start.12 = (bf16[2048,512]{1,0:T(8,128)(2,1)S(1)}, bf16[2048,512]{1,0:T(8,128)(2,1)S(1)}, u32[]{:S(2)}, u32[]{:S(2)}) collective-permute-start(bf16[2048,512]{1,0:T(8,128)(2,1)S(1)} %get-tuple-element.115), channel_id=1, source_target_pairs={{0,2},{2,0},{4,6},{6,4},{8,10},{10,8},{12,14},{14,12},{16,18},{18,... | collective-permute-start | bytes 6291464 | tf_op jit(solution)/shard_map/ppermute | solution.py:614
  69.6 26.9 %collective-permute-start.7 = (bf16[1024,512]{1,0:T(8,128)(2,1)S(1)}, bf16[1024,512]{1,0:T(8,128)(2,1)S(1)}, u32[]{:S(2)}, u32[]{:S(2)}) collective-permute-start(bf16[1024,512]{1,0:T(8,128)(2,1)S(1)} %get-tuple-element.91), channel_id=1, source_target_pairs={{0,8},{2,18},{4,12},{6,22},{8,0},{10,26},{12,4},{14,30},{16,24},{1... | collective-permute-start | bytes 3145736 | tf_op jit(solution)/shard_map/ppermute | solution.py:614
  70.5 26.0 %collective-permute-start.13 = (bf16[1024,512]{1,0:T(8,128)(2,1)S(1)}, bf16[1024,512]{1,0:T(8,128)(2,1)S(1)}, u32[]{:S(2)}, u32[]{:S(2)}) collective-permute-start(bf16[1024,512]{1,0:T(8,128)(2,1)S(1)} %get-tuple-element.117), channel_id=1, source_target_pairs={{0,4},{2,6},{4,0},{6,2},{8,12},{10,14},{12,8},{14,10},{16,20},{18,... | collective-permute-start | bytes 3145736 | tf_op jit(solution)/shard_map/ppermute | solution.py:614
  70.9 25.6 %collective-permute-start.14 = (bf16[1024,512]{1,0:T(8,128)(2,1)}, bf16[1024,512]{1,0:T(8,128)(2,1)S(1)}, u32[]{:S(2)}, u32[]{:S(2)}) collective-permute-start(bf16[1024,512]{1,0:T(8,128)(2,1)} %collective-permute-done.8.refs_3_), channel_id=1, source_target_pairs={{0,1},{1,0},{2,3},{3,2},{4,5},{5,4},{6,7},{7,6},{8,9},{9,8},{10,11... | collective-permute-start | bytes 3145736 | tf_op jit(solution)/shard_map/ppermute | solution.py:617
  94.5 2.0 %copy-start.1 = (f32[2048,512]{1,0:T(8,128)}, f32[2048,512]{1,0:T(8,128)S(1)}, u32[]{:S(2)}) copy-start(f32[2048,512]{1,0:T(8,128)S(1)} %get-tuple-element.119.refs_7_) | copy-start | bytes 12582916
  96.4 25.4 %collective-permute-start.11 = (bf16[1024,512]{1,0:T(8,128)(2,1)S(1)}, bf16[1024,512]{1,0:T(8,128)(2,1)S(1)}, u32[]{:S(2)}, u32[]{:S(2)}) collective-permute-start(bf16[1024,512]{1,0:T(8,128)(2,1)S(1)} %collective-permute-done.7.refs_4_), channel_id=1, source_target_pairs={{0,1},{1,0},{2,3},{3,2},{4,5},{5,4},{6,7},{7,6},{8,9},{9,8},{10,11... | collective-permute-start | bytes 3145736 | tf_op jit(solution)/shard_map/ppermute | solution.py:617
  96.5 25.3 %copy-start.7 = (s32[4,16]{1,0:T(4,128)S(1)}, s32[4,16]{1,0:T(4,128)}, u32[]{:S(2)}) copy-start(s32[4,16]{1,0:T(4,128)} %get-tuple-element.69.spots_ref) | copy-start | bytes 772

commit v2 on v1

--- a/solution.py
+++ b/solution.py
@@ -26,9 +26,11 @@
     copies = []
     start = 0
     for index, piece in enumerate(pieces):
-        size = piece.shape[0]
+        size = piece.shape[0] // TILE * TILE
         copies.append(
-            pltpu.make_async_copy(piece, target.at[pl.ds(start, size)], sems.at[index])
+            pltpu.make_async_copy(
+                piece.at[pl.ds(0, size)], target.at[pl.ds(start, size)], sems.at[index]
+            )
         )
         start += size
     return copies
@@ -145,16 +147,6 @@
         den[row, :] += pack_denominators(listed)
 
 
-def sums_copies(num, den, num_out, den_out, sems, inward):
-    rows = num_out.shape[0]
-    copies = []
-    for index, (here, there) in enumerate([(num, num_out), (den, den_out)]):
-        here = here.at[pl.ds(0, rows)]
-        source, target = (there, here) if inward else (here, there)
-        copies.append(pltpu.make_async_copy(source, target, sems.at[index]))
-    return copies
-
-
 def project_pieces(pieces, w, keys, values, at):
     for piece in pieces:
         tiles = piece.shape[0] // TILE
@@ -169,7 +161,7 @@
         at += tiles
 
 
-def attend_rows(span, fresh, place_ref, cols_ref, where_ref, local_ref, keys, values, sums, scratch):
+def attend_rows(fresh, place_ref, cols_ref, where_ref, local_ref, keys, values, sums, scratch):
     num, den, num_out, den_out = sums
     ones, list_ref, sems = scratch
     width = num.shape[1]
@@ -180,10 +172,9 @@
 
     def one_row(row, carry):
         target = pl.ds(pl.multiple_of(row * TILE, TILE), TILE)
-        half = row // (tiles_here // 2)
         found = jnp.int32(0)
         for slot in range(slots):
-            tile = where_ref[half, cols_ref[place_ref[0] * tiles_here + row, slot]]
+            tile = where_ref[cols_ref[place_ref[0] * tiles_here + row, slot]]
             list_ref[found] = tile
             found = found + (tile >= 0).astype(jnp.int32)
         list_ref[found] = 0
@@ -212,14 +203,12 @@
             pltpu.make_async_copy(here.at[target], there.at[target], sems.at[index]).start()
         return carry
 
-    lax.fori_loop(*span, one_row, 0)
-    every = pl.ds(span[0] * TILE, (span[1] - span[0]) * TILE)
+    lax.fori_loop(0, tiles_here, one_row, 0)
     for index, (here, there) in enumerate([(num, num_out), (den, den_out)]):
-        pltpu.make_async_copy(here.at[every], there.at[every], sems.at[index]).wait()
-
-
-def own_kernel(span, place_ref, cols_ref, where_ref, rows, w, wq, scales, *refs):
-    (num_out, den_out, keys, values, local_ref, expand_ref, num, den, *scratch) = refs
+        pltpu.make_async_copy(here, there, sems.at[index]).wait()
+
+
+def own_kernel(rows, w, wq, scales, keys, values, local_ref, expand_ref):
     width = rows.shape[1]
     tiles = rows.shape[0] // TILE
     size = min(GROUP, tiles)
@@ -235,19 +224,38 @@
         return carry
 
     lax.fori_loop(0, tiles // size, some_queries, 0)
-    sums = (num, den, num_out, den_out)
-    attend_rows(span, True, place_ref, cols_ref, where_ref, local_ref, keys, values, sums, scratch)
-
-
-def near_kernel(span, count, place_ref, cols_ref, where_ref, *refs):
+
+
+def project_own(rows, w, wq, scales):
+    width = rows.shape[1]
+    tiles = rows.shape[0] // TILE
+    shapes = [(tiles, width, TILE), (tiles, TILE, width), rows.shape, rows.shape]
+    return pl.pallas_call(
+        own_kernel,
+        in_specs=[VMEM] * 4,
+        out_specs=[VMEM] * 4,
+        out_shape=[jax.ShapeDtypeStruct(shape, jnp.bfloat16) for shape in shapes],
+        compiler_params=pltpu.CompilerParams(vmem_limit_bytes=24 * MIB),
+        cost_estimate=pl.CostEstimate(flops=10**8, bytes_accessed=10**5, transcendentals=0),
+    )(rows, w, wq, scales)
+
+
+def local_kernel(count, begins, place_ref, cols_ref, where_ref, *refs):
     pieces = refs[:count]
-    (w, local_ref, own_keys, own_values, _, _, num_out, den_out) = refs[count : count + 8]
-    (num, den, ones, list_ref, sems, keys, values, own_sems) = refs[count + 8 :]
-    tiles = own_keys.shape[0]
-    copies = [
-        pltpu.make_async_copy(own_keys, keys.at[pl.ds(0, tiles)], own_sems.at[0]),
-        pltpu.make_async_copy(own_values, values.at[pl.ds(0, tiles)], own_sems.at[1]),
-    ]
+    (w, local_ref, before, after, num_out, den_out) = refs[count : count + 6]
+    (num, den, ones, list_ref, sems, keys, values, more_sems) = refs[count + 6 :]
+    tiles = 0
+    if begins:
+        tiles = before.shape[0]
+        copies = [
+            pltpu.make_async_copy(before, keys.at[pl.ds(0, tiles)], more_sems.at[0]),
+            pltpu.make_async_copy(after, values.at[pl.ds(0, tiles)], more_sems.at[1]),
+        ]
+    else:
+        copies = [
+            pltpu.make_async_copy(before, num, more_sems.at[0]),
+            pltpu.make_async_copy(after, den, more_sems.at[1]),
+        ]
     for copy in copies:
         copy.start()
     project_pieces(pieces, w, keys, values, tiles)
@@ -255,42 +263,24 @@
         copy.wait()
     sums = (num, den, num_out, den_out)
     scratch = (ones, list_ref, sems)
-    attend_rows(span, True, place_ref, cols_ref, where_ref, local_ref, keys, values, sums, scratch)
-
-
-def rest_kernel(span, count, place_ref, cols_ref, where_ref, *refs):
-    pieces = refs[:count]
-    (w, local_ref, num_in, den_in, num_out, den_out) = refs[count : count + 6]
-    (num, den, ones, list_ref, sems, keys, values, sums_sems) = refs[count + 6 :]
-    incoming = sums_copies(num, den, num_in, den_in, sums_sems, True)
-    for copy in incoming:
-        copy.start()
-    project_pieces(pieces, w, keys, values, 0)
-    for copy in incoming:
-        copy.wait()
-    sums = (num, den, num_out, den_out)
-    scratch = (ones, list_ref, sems)
-    attend_rows(span, False, place_ref, cols_ref, where_ref, local_ref, keys, values, sums, scratch)
-
-
-def local_call(kernel, tables, pieces, extra, extra_specs, span, sums, more_outs, scratch, limit, flops):
-    own_rows, width = extra[1].shape if kernel is not own_kernel else pieces[0].shape
+    attend_rows(begins, place_ref, cols_ref, where_ref, local_ref, keys, values, sums, scratch)
+
+
+def local_attention(tables, pieces, w, local_q, before, begins):
+    own_rows, width = local_q.shape
     shapes = [
         jax.ShapeDtypeStruct((own_rows, width), jnp.float32),
         jax.ShapeDtypeStruct((own_rows, LANES), jnp.float32),
     ]
-    arguments = [*tables, *pieces, *extra, *(sums or ())]
-    aliases = {}
-    if sums:
-        aliases = {len(arguments) - 2: 0, len(arguments) - 1: 1}
-    bound = functools.partial(kernel, span)
-    if kernel is not own_kernel:
-        bound = functools.partial(kernel, span, len(pieces))
+    arguments = [*tables, *pieces, w, local_q, *before]
+    aliases = {} if begins else {len(arguments) - 2: 0, len(arguments) - 1: 1}
+    tiles = sum(piece.shape[0] // TILE for piece in pieces)
+    tiles += own_rows // TILE if begins else 0
     return pl.pallas_call(
-        bound,
-        in_specs=[SMEM] * 3 + [VMEM] * len(pieces) + extra_specs + [HBM] * len(sums or ()),
-        out_specs=[HBM, HBM] + [VMEM] * len(more_outs),
-        out_shape=shapes + more_outs,
+        functools.partial(local_kernel, len(pieces), begins),
+        in_specs=[SMEM] * 3 + [VMEM] * (len(pieces) + 2) + [HBM] * 2,
+        out_specs=[HBM, HBM],
+        out_shape=shapes,
         input_output_aliases=aliases,
         scratch_shapes=[
             pltpu.VMEM((own_rows, width), jnp.float32),
@@ -298,47 +288,15 @@
             pltpu.VMEM((2, TILE, LANES), jnp.bfloat16),
             pltpu.SMEM((tables[1].shape[1] + 1,), jnp.int32),
             pltpu.SemaphoreType.DMA((2,)),
-        ]
-        + scratch,
-        compiler_params=pltpu.CompilerParams(vmem_limit_bytes=limit * MIB),
-        cost_estimate=pl.CostEstimate(flops=flops, bytes_accessed=10**5, transcendentals=0),
+            pltpu.VMEM((tiles, width, TILE), jnp.bfloat16),
+            pltpu.VMEM((tiles, TILE, width), jnp.bfloat16),
+            pltpu.SemaphoreType.DMA((2,)),
+        ],
+        compiler_params=pltpu.CompilerParams(vmem_limit_bytes=24 * MIB),
+        cost_estimate=pl.CostEstimate(
+            flops=10**12 if begins else 10**8, bytes_accessed=10**5, transcendentals=0
+        ),
     )(*arguments)
-
-
-def key_scratch(tiles, width):
-    return [
-        pltpu.VMEM((tiles, width, TILE), jnp.bfloat16),
-        pltpu.VMEM((tiles, TILE, width), jnp.bfloat16),
-        pltpu.SemaphoreType.DMA((2,)),
-    ]
-
-
-def own_attention(tables, rows, w, wq, scales, span):
-    width = rows.shape[1]
-    tiles = rows.shape[0] // TILE
-    shapes = [(tiles, width, TILE), (tiles, TILE, width), rows.shape, rows.shape]
-    outs = [jax.ShapeDtypeStruct(shape, jnp.bfloat16) for shape in shapes]
-    return local_call(
-        own_kernel, tables, [rows], [w, wq, scales], [VMEM] * 3, span, None, outs, [], 24, 10**8
-    )
-
-
-def near_attention(tables, pieces, w, local_q, keys, values, num, den, span):
-    tiles = keys.shape[0] + sum(piece.shape[0] // TILE for piece in pieces)
-    scratch = key_scratch(tiles, local_q.shape[1])
-    extra = [w, local_q, keys, values]
-    specs = [VMEM, VMEM, ANY, ANY]
-    return local_call(
-        near_kernel, tables, pieces, extra, specs, span, (num, den), [], scratch, 24, 10**12
-    )
-
-
-def rest_attention(tables, pieces, w, local_q, num, den, span):
-    scratch = key_scratch(sum(piece.shape[0] // TILE for piece in pieces), local_q.shape[1])
-    extra = [w, local_q]
-    return local_call(
-        rest_kernel, tables, pieces, extra, [VMEM] * 2, span, (num, den), [], scratch, 24, 10**8
-    )
 
 
 def expand_kernel(count, last, place_ref, rows_ref, spots_ref, *refs):
@@ -346,23 +304,18 @@
     (expand_q, num_in, den_in, w) = refs[count : count + 4]
     refs = refs[count + 4 :]
     if last:
-        (out_ref, features, keys, values, num, den, row_list, tile_list, sems) = refs
+        (_, out_ref, features, keys, values, num, den, row_list, tile_list, mark, sems) = refs[:-2]
+        (results, result_sems) = refs[-2:]
     else:
-        (num_out, den_out, features, keys, values, num, den, row_list, tile_list, sems) = refs
-    own_rows, width = num_in.shape
+        (num, den, out_ref, features, keys, values, row_list, tile_list, mark, sems) = refs
+    own_rows, width = expand_q.shape
     tiles_here = own_rows // TILE
     matchings, edges = rows_ref.shape
     copies = piece_copies(sources, features, sems)
     for copy in copies:
         copy.start()
-
-    def clear(tile, carry):
-        target = pl.ds(pl.multiple_of(tile * TILE, TILE), TILE)
-        num[target, :] = jnp.zeros((TILE, width), jnp.float32)
-        den[target, :] = jnp.zeros((TILE, LANES), jnp.float32)
-        return carry
-
-    lax.fori_loop(0, tiles_here + 1, clear, 0)
+    for tile in range(tiles_here):
+        mark[tile] = 0 if last else 1
 
     def visit(edge, found):
         for matching in range(matchings):
@@ -372,12 +325,35 @@
             row_list[found] = row
             tile_list[found] = spot
             found = found + mine.astype(jnp.int32)
+            if last:
+
+                @pl.when(mine)
+                def _():
+                    mark[row] = 1
+
         return found
 
     found = lax.fori_loop(0, edges, visit, jnp.int32(0))
     for inner in range(GROUP):
         row_list[found + inner] = tiles_here
         tile_list[found + inner] = 0
+
+    def each_marked(action):
+        def visit_tile(tile, carry):
+            target = pl.ds(pl.multiple_of(tile * TILE, TILE), TILE)
+            pl.when(mark[tile] == 1)(lambda: action(tile, target))
+            return carry
+
+        lax.fori_loop(0, tiles_here, visit_tile, 0)
+
+    def begin(tile, target):
+        num[target, :] = num_in[target, :]
+        den[target, :] = den_in[target, :]
+
+    each_marked(begin)
+    spare = pl.ds(own_rows, TILE)
+    num[spare, :] = jnp.zeros((TILE, width), jnp.float32)
+    den[spare, :] = jnp.zeros((TILE, LANES), jnp.float32)
     for copy in copies:
         copy.wait()
 
@@ -397,54 +373,78 @@
 
     lax.fori_loop(0, (found + GROUP - 1) // GROUP, group, 0)
 
-    def finish(tile, carry):
-        target = pl.ds(pl.multiple_of(tile * TILE, TILE), TILE)
-        total = num_in[target, :] + num[target, :]
-        count = den_in[target, :] + den[target, :]
+    def finish(tile, target):
+        inverse = spread_denominators(den[target, :], width // LANES)
+        result = (num[target, :] * inverse).astype(jnp.bfloat16)
         if last:
-            inverse = spread_denominators(count, width // LANES)
-            out_ref[target, :] = (total * inverse).astype(jnp.bfloat16)
+            results[target, :] = result
+            copy_out(tile, target).start()
         else:
-            num_out[target, :] = total
-            den_out[target, :] = count
-        return carry
-
-    lax.fori_loop(0, tiles_here, finish, 0)
-
-
-def expand_attention(place, exp_rows, spots, sources, expand_q, num, den, w, last):
-    own_rows, width = num.shape
+            out_ref[target, :] = result
+
+    def copy_out(tile, target):
+        return pltpu.make_async_copy(results.at[target], out_ref.at[target], result_sems.at[tile])
+
+    each_marked(finish)
+    if last:
+        each_marked(lambda tile, target: copy_out(tile, target).wait())
+
+
+def expand_attention(place, exp_rows, spots, sources, expand_q, num, den, w, out):
+    width = w.shape[2]
+    own_rows = expand_q.shape[0]
+    last = out is not None
     most = exp_rows.shape[0] * exp_rows.shape[1] + GROUP
-    tiles = sum(source.shape[0] for source in sources) // TILE
-    sums = [jax.ShapeDtypeStruct(num.shape, num.dtype), jax.ShapeDtypeStruct(den.shape, den.dtype)]
+    tiles = sum(source.shape[0] // TILE for source in sources)
+    sums = [
+        jax.ShapeDtypeStruct((own_rows + TILE, width), jnp.float32),
+        jax.ShapeDtypeStruct((own_rows + TILE, LANES), jnp.float32),
+    ]
+    result = jax.ShapeDtypeStruct((own_rows, width), jnp.bfloat16)
+    sums_scratch = [pltpu.VMEM(array.shape, array.dtype) for array in sums]
+    arguments = [place, exp_rows, spots, *sources, expand_q, num, den, w]
     return pl.pallas_call(
         functools.partial(expand_kernel, len(sources), last),
-        in_specs=[SMEM] * 3 + [ANY] * len(sources) + [VMEM] * 4,
-        out_specs=VMEM if last else [VMEM, VMEM],
-        out_shape=jax.ShapeDtypeStruct((own_rows, width), jnp.bfloat16) if last else sums,
+        in_specs=[SMEM] * 3 + [ANY] * len(sources) + [VMEM] * 4 + [ANY] * last,
+        out_specs=ANY if last else [VMEM] * 3,
+        out_shape=result if last else sums + [result],
+        input_output_aliases={len(arguments): 0} if last else {},
         scratch_shapes=[
             pltpu.VMEM((tiles * TILE, width), jnp.bfloat16),
             pltpu.VMEM((GROUP, width, TILE), jnp.bfloat16),
             pltpu.VMEM((GROUP, TILE, width), jnp.bfloat16),
-            pltpu.VMEM((own_rows + TILE, width), jnp.float32),
-            pltpu.VMEM((own_rows + TILE, LANES), jnp.float32),
+        ]
+        + (sums_scratch if last else [])
+        + [
             pltpu.SMEM((most,), jnp.int32),
             pltpu.SMEM((most,), jnp.int32),
+            pltpu.SMEM((own_rows // TILE,), jnp.int32),
             pltpu.SemaphoreType.DMA((len(sources),)),
-        ],
-        compiler_params=pltpu.CompilerParams(vmem_limit_bytes=36 * MIB),
+        ]
+        + (
+            [
+                pltpu.VMEM((own_rows, width), jnp.bfloat16),
+                pltpu.SemaphoreType.DMA((own_rows // TILE,)),
+            ]
+            if last
+            else []
+        ),
+        compiler_params=pltpu.CompilerParams(vmem_limit_bytes=24 * MIB),
         cost_estimate=pl.CostEstimate(
             flops=own_rows * width * 256, bytes_accessed=own_rows * width, transcendentals=0
         ),
-    )(place, exp_rows, spots, *sources, expand_q, num, den, w)
-
-
-def cut_kernel(margin, here_ref, features, lower, edge, sems):
-    start = pl.multiple_of(here_ref[0] * (features.shape[0] - margin), TILE)
-    copies = [
-        pltpu.make_async_copy(features.at[pl.ds(0, lower.shape[0])], lower, sems.at[0]),
-        pltpu.make_async_copy(features.at[pl.ds(start, margin)], edge, sems.at[1]),
-    ]
+    )(*arguments, *([out] if last else []))
+
+
+def cut_kernel(here_ref, features, first, second, edge, sems):
+    here = here_ref[0]
+    half, margin = first.shape[0], edge.shape[0]
+    copies = []
+    for index, (start, target) in enumerate(
+        [(here * half, first), ((1 - here) * half, second), (here * (2 * half - margin), edge)]
+    ):
+        rows = pl.ds(pl.multiple_of(start, TILE), target.shape[0])
+        copies.append(pltpu.make_async_copy(features.at[rows], target, sems.at[index]))
     for copy in copies:
         copy.start()
     for copy in copies:
@@ -453,30 +453,31 @@
 
 def cut(here, features, margin):
     rows, width = features.shape
+    shapes = [(rows // 2, width), (rows // 2, width), (margin, width)]
     return pl.pallas_call(
-        functools.partial(cut_kernel, margin),
+        cut_kernel,
         in_specs=[SMEM, ANY],
-        out_specs=[VMEM, VMEM],
-        out_shape=[
-            jax.ShapeDtypeStruct((rows // 2, width), jnp.bfloat16),
-            jax.ShapeDtypeStruct((margin, width), jnp.bfloat16),
-        ],
-        scratch_shapes=[pltpu.SemaphoreType.DMA((2,))],
+        out_specs=[VMEM] * 3,
+        out_shape=[jax.ShapeDtypeStruct(shape, jnp.bfloat16) for shape in shapes],
+        scratch_shapes=[pltpu.SemaphoreType.DMA((3,))],
         compiler_params=pltpu.CompilerParams(vmem_limit_bytes=8 * MIB),
     )(here, features)
 
 
-def select_kernel(jobs, share, sources, place_ref, *refs):
-    matchings = len(refs) - sources - len(jobs)
+def select_kernel(jobs, share, sources, margin, place_ref, *refs):
+    matchings = len(refs) - sources - len(jobs) - (margin > 0)
     wanted = refs[:matchings]
     parts = refs[matchings : matchings + sources]
     outs = refs[matchings + sources :]
     here = place_ref[0]
     even = lax.rem(place_ref[1], 2) == 0
     quarter = parts[1].shape[0] // TILE
+    if margin:
+        start = pl.multiple_of((1 - here) * (quarter * TILE - margin), TILE)
+        outs[-1][...] = parts[1][pl.ds(start, margin), :]
     per_part = 2 * quarter
     flat = []
-    for (of_even, of_odd, lines), out in zip(jobs, outs):
+    for (of_even, of_odd, lines, _), out in zip(jobs, outs):
         at = 0
         for line in lines:
             start = (here if line == 0 else 1 - here) * share
@@ -488,7 +489,8 @@
                 at += 1
     for tile, out, slot in flat:
         own = tile // per_part == here
-        lower = lax.rem(tile // quarter, 2) == 0
+        place = tile // quarter
+        end = jnp.logical_or(place == 0, place == 3)
         target = slice(slot * TILE, (slot + 1) * TILE)
 
         @pl.when(own)
@@ -498,26 +500,28 @@
 
         start = pl.multiple_of(lax.rem(tile, quarter) * TILE, TILE)
 
-        @pl.when(jnp.logical_and(jnp.logical_not(own), lower))
+        @pl.when(jnp.logical_and(jnp.logical_not(own), end))
         def _():
             out[target, :] = parts[1][pl.ds(start, TILE), :]
 
         if sources > 2:
 
-            @pl.when(jnp.logical_not(jnp.logical_or(own, lower)))
+            @pl.when(jnp.logical_not(jnp.logical_or(own, end)))
             def _():
                 out[target, :] = parts[2][pl.ds(start, TILE), :]
 
 
-def select(place, jobs, share, wanted, parts):
+def select(place, jobs, share, wanted, parts, margin=0):
     width = parts[0].shape[1]
-    sizes = [share * len(lines) for _, _, lines in jobs]
+    sizes = [share * len(lines) * TILE + more for _, _, lines, more in jobs]
+    sizes += [margin] * (margin > 0)
     return pl.pallas_call(
-        functools.partial(select_kernel, jobs, share, len(parts)),
+        functools.partial(select_kernel, jobs, share, len(parts), margin),
         in_specs=[SMEM] * (1 + len(wanted)) + [VMEM] * len(parts),
-        out_specs=[VMEM] * len(jobs),
-        out_shape=[jax.ShapeDtypeStruct((size * TILE, width), jnp.bfloat16) for size in sizes],
+        out_specs=[VMEM] * len(sizes),
+        out_shape=[jax.ShapeDtypeStruct((size, width), jnp.bfloat16) for size in sizes],
         compiler_params=pltpu.CompilerParams(vmem_limit_bytes=16 * MIB),
+        cost_estimate=pl.CostEstimate(flops=1000, bytes_accessed=1000, transcendentals=0),
     )(place, *wanted, *parts)
 
 
@@ -545,7 +549,7 @@
 
     def place(at, carry):
         quarter = tiles // 4
-        tile = jnp.where(at < quarter, at + quarter, jnp.where(at < 2 * quarter, at - quarter, at))
+        tile = at + (quarter if at // quarter % 2 == 0 else -quarter)
         ranks, left = [], []
         for matching, (rank, missing) in enumerate(zip(*carry)):
             present = mark[matching, tile]
@@ -573,11 +577,16 @@
                 last_ref[matching, edge] = jnp.where(later, within, -1)
         return carry
 
-    zero = jnp.int32(0)
-    lax.fori_loop(0, tiles, clear, 0)
-    missing = lax.fori_loop(0, edges, count, (jnp.int32(edges),) * matchings)
-    lax.fori_loop(0, tiles, place, ((zero,) * matchings, missing))
-    lax.fori_loop(0, edges, look_up, 0)
+    for tile in range(tiles):
+        clear(tile, 0)
+    missing = (jnp.int32(edges),) * matchings
+    for edge in range(edges):
+        missing = count(edge, missing)
+    carry = ((jnp.int32(0),) * matchings, missing)
+    for at in range(tiles):
+        carry = place(at, carry)
+    for edge in range(edges):
+        look_up(edge, 0)
 
 
 def distinct_slots(place, cols, tiles, lines):
@@ -619,12 +628,10 @@
     scales = jnp.stack([edge_local, edge_expand])
     two = groups == 2 and min(flips[2:]) > 1
     if two:
-        lower, edge_rows = cut(jnp.reshape(here, (1,)).astype(jnp.int32), features, margin)
+        cuts = cut(jnp.reshape(here, (1,)).astype(jnp.int32), features, margin)
         beside = other(scales)
-        lower, edge_rows, exp_cols, beside, w_query, w_key_value, block, here = (
-            lax.optimization_barrier(
-                (lower, edge_rows, exp_cols, beside, w_query, w_key_value, block, here)
-            )
+        *cuts, exp_cols, beside, w_query, w_key_value, block, here = lax.optimization_barrier(
+            (*cuts, exp_cols, beside, w_query, w_key_value, block, here)
         )
     place = jnp.stack([here, block]).astype(jnp.int32)
     column = jnp.arange(tiles + 2 * HT, dtype=jnp.int32) - HT
@@ -632,85 +639,75 @@
     usable = jnp.logical_and(usable >= 0, usable < blocks * tiles)
     own = column // own_tiles == here
     own_place = column - here * own_tiles
-    split = own_tiles // 2
 
     if two:
-        half = own_rows // 2
         quarter = own_tiles // 2
-        lower_here = column // quarter % 2 == 0
+        end = jnp.logical_or(column // quarter == 0, column // quarter == 3)
         inside = jnp.logical_and(column >= 0, column < tiles)
         after = column >= tiles
         in_halo = jnp.where(after, column - tiles, column + HT)
-        in_halo += jnp.where(after == (here == 0), 2 * quarter + HT, 2 * quarter)
-        place_in = jnp.where(lower_here, column % quarter, quarter + column % quarter)
+        in_halo += jnp.where(after == (here == 0), 2 * quarter, 2 * quarter + HT)
+        place_in = jnp.where(end, column % quarter, quarter + column % quarter)
         rest = jnp.where(inside, place_in, in_halo)
         near = jnp.where(own, own_place, own_tiles + place_in)
-        near = jnp.where(jnp.logical_and(inside, jnp.logical_or(own, lower_here)), near, -1)
-        rest_low = jnp.where(jnp.logical_and(usable, jnp.logical_not(own)), rest, -1)
-        rest_high = jnp.where(jnp.logical_and(usable, near < 0), rest, -1)
-        where_own = jnp.where(own, own_place, -1)
-        tables = jnp.stack([where_own, where_own, near, near, rest_low, rest_high])
+        near = jnp.where(jnp.logical_and(inside, jnp.logical_or(own, end)), near, -1)
+        rest = jnp.where(jnp.logical_and(usable, near < 0), rest, -1)
         w = jnp.transpose(w_key_value, (1, 0, 2))
-        lower = other(lower)
+        first_half, second_half, edge_rows = cuts
+        first_half = other(first_half)
         near_spots, last_spots, wanted = distinct_slots(place, exp_cols, tiles, groups)
         edge_rows, *wanted = lax.optimization_barrier((edge_rows, *wanted))
-        route = [(2 * i, 2 * i - 2) for i in range(1, blocks)]
-        route += [(2 * i + 1, 2 * i + 3) for i in range(blocks - 1)]
-        halo = lax.ppermute(edge_rows, ("node", "head"), route)
         wanted = [swap(wanted[m], m) for m in range(MATCH)]
-        upper = jnp.concatenate([features[half:], halo], axis=0)
+        inward = [(2 * i, 2 * i - 2) for i in range(1, blocks)]
+        inward += [(2 * i + 1, 2 * i + 3) for i in range(blocks - 1)]
+        halo = lax.ppermute(edge_rows, ("node", "head"), inward)
         scales = jnp.where(
             here == 0,
             jnp.concatenate([scales, beside], axis=1),
             jnp.concatenate([beside, scales], axis=1),
         )
-        num, den, keys, values, local_q, expand_q = own_attention(
-            (place, local_cols, tables[:2]), features, w, w_query, scales, (0, split)
-        )
-        where_near, where_rest = tables[2:4], tables[4:]
-        lower, upper, num, den, where_near, where_rest = lax.optimization_barrier(
-            (lower, upper, num, den, where_near, where_rest)
-        )
-        upper = other(upper)
+        scales, halo, w, *wanted = lax.optimization_barrier((scales, halo, w, *wanted))
+        keys, values, local_q, expand_q = project_own(features, w, w_query, scales)
+        first_half, second_half, keys, near, rest = lax.optimization_barrier(
+            (first_half, second_half, keys, near, rest)
+        )
+        second_half = other(second_half)
         share = edges // groups
-        sources = [features, lower]
-        chosen = select(place, ((3, 2, (0,)), (2, 3, (0,)), (1, 1, (0,))), share, wanted, sources)
-        where_near, *chosen = lax.optimization_barrier((where_near, *chosen))
+        sources = [features, first_half]
+        jobs = ((3, 2, (0,), 0), (2, 3, (0,), 16), (1, 1, (0,), 0), (0, 0, (0,), 0))
+        *chosen, edge_rows = select(place, jobs, share, wanted, sources, margin)
+        near, edge_rows, *chosen = lax.optimization_barrier((near, edge_rows, *chosen))
+        outward = [(2 * i, 2 * i + 2) for i in range(blocks - 1)]
+        outward += [(2 * i + 1, 2 * i - 1) for i in range(1, blocks)]
+        other_halo = lax.ppermute(edge_rows, ("node", "head"), outward)
         first = swap(chosen[0], 3, 2)
         second = swap(chosen[1], 2, 3)
         early = swap(chosen[2], 1)
-        num, den = near_attention(
-            (place, local_cols, where_near),
-            [lower],
+        pair = swap(chosen[3], 0)
+        near, other_halo = lax.optimization_barrier((near, other_halo))
+        num, den = local_attention(
+            (place, local_cols, near), [first_half], w, local_q, (keys, values), True
+        )
+        second_half, num, den = lax.optimization_barrier((second_half, num, den))
+        sources = [features, first_half, second_half]
+        chosen = select(place, ((1, 1, (1,), 0), (0, 0, (1,), 0)), share, wanted, sources)
+        rest, first, early, pair, *chosen = lax.optimization_barrier(
+            (rest, first, early, pair, *chosen)
+        )
+        first_beside = other(first)
+        late = swap(chosen[0], 1)
+        late_pair = swap(chosen[1], 0)
+        num, den = local_attention(
+            (place, local_cols, rest),
+            [first_half, second_half, halo, other_halo],
             w,
             local_q,
-            keys,
-            values,
-            num,
-            den,
-            (split, own_tiles),
-        )
-        upper, num, den = lax.optimization_barrier((upper, num, den))
-        sources = [features, lower, upper]
-        chosen = select(place, ((1, 1, (1,)), (0, 0, (0, 1))), share, wanted, sources)
-        where_rest, first, early, *chosen = lax.optimization_barrier(
-            (where_rest, first, early, *chosen)
-        )
-        first_beside = other(first)
-        late = swap(chosen[0], 1)
-        pair = swap(chosen[1], 0)
-        num, den = rest_attention(
-            (place, local_cols, where_rest),
-            [lower, upper, halo],
-            w,
-            local_q,
-            num,
-            den,
-            (0, own_tiles),
+            (num, den),
+            False,
         )
         second, num, den = lax.optimization_barrier((second, num, den))
         last_sources = [other(second)]
-        near_sources = [pair, early, late, first, second, first_beside]
+        near_sources = [pair, late_pair, early, late, first, second, first_beside]
     else:
         w = jnp.transpose(w_key_value, (1, 0, 2))
         gather = lambda x: lax.all_gather(x, "head", axis=0, tiled=True)
@@ -724,26 +721,19 @@
         near_spots = jnp.where(matching < 2, matching * tiles + exp_cols, -1)
         last_spots = jnp.where(matching < 2, -1, (matching - 2) * tiles + exp_cols)
         where_own = jnp.where(own, own_place, -1)
-        where_own = jnp.stack([where_own, where_own])
         where_rest = jnp.where(jnp.logical_and(usable, jnp.logical_not(own)), column + HT, -1)
-        where_rest = jnp.stack([where_rest, where_rest])
-        num, den, keys, values, local_q, expand_q = own_attention(
-            (place, local_cols, where_own), features, w, w_query, scales, (0, own_tiles)
-        )
-        num, den = rest_attention(
-            (place, local_cols, where_rest),
-            [before, full, after],
-            w,
-            local_q,
-            num,
-            den,
-            (0, own_tiles),
-        )
-    num, den = expand_attention(
-        place, exp_rows, near_spots, near_sources, expand_q, num, den, w, False
+        keys, values, local_q, expand_q = project_own(features, w, w_query, scales)
+        num, den = local_attention(
+            (place, local_cols, where_own), [], w, local_q, (keys, values), True
+        )
+        num, den = local_attention(
+            (place, local_cols, where_rest), [before, full, after], w, local_q, (num, den), False
+        )
+    num, den, out = expand_attention(
+        place, exp_rows, near_spots, near_sources, expand_q, num, den, w, None
     )
     return expand_attention(
-        place, exp_rows, last_spots, last_sources, expand_q, num, den, w, True
+        place, exp_rows, last_spots, last_sources, expand_q, num, den, w, out
     )
 
 

time: 132 us -> 150 us (1.14)
  the two profiles are of different devices: /device:TPU:0 before, /device:TPU:25 now
where the time goes in v2:
time: 150 us; the launch traced here: 148 us
  Pallas kernels  84.1 us (56%)
  starting transfers between devices  30.4 us (20%)
  local copies, waits for them, and re-layouts  17.9 us (12%)
  waiting for transfers between devices  13.3 us (9%)
    pallas_call x2, Pallas kernels, local_attention(): pl.pallas_call(functools.partial(local_kernel, len(pieces), begins), in_s...  43.9 us
    pallas_call x2, Pallas kernels, expand_attention(): pl.pallas_call(functools.partial(expand_kernel, len(sources), last), in_s...  26.2 us
    ppermute x10, starting transfers between devices, swap(): lax.ppermute(x, 'node', [(i, i ^ flip[i % 2]) for i in range(blocks)])  18 us
    unnamed x65, local copies, waits for them, and re-layouts  16.5 us
    ppermute x10, waiting for transfers between devices, swap(): lax.ppermute(x, 'node', [(i, i ^ flip[i % 2]) for i in range(blocks)])  8.61 us
    pallas_call x2, Pallas kernels, select(): pl.pallas_call(functools.partial(select_kernel, jobs, share, len(parts),...  5.17 us
    pallas_call x1, Pallas kernels, project_own(): pl.pallas_call(own_kernel, in_specs=[VMEM] * 4, out_specs=[VMEM] * 4, out...  5 us
    ppermute x1, starting transfers between devices, local(): other_halo = lax.ppermute(edge_rows, ('node', 'head'), outward)  4.8 us
  transfers between devices with their start and end apart: 17, of which 9 were waited for; matrix products, arithmetic and copies ran while one was open for 1% of the time, Pallas kernels for 51%

profile of v2, /device:TPU:25, one launch (start us, length us, event | category | flops | bytes accessed | tf_op | source)
XLA Modules:
  0.0 147.6 jit_solution(16133642049133227145)
XLA Ops:
  0.7 1.2 collective-permute-start
  1.9 1.6 %copy-done = bf16[2048,512]{1,0:T(8,128)(2,1)S(1)} copy-done((bf16[2048,512]{1,0:T(8,128)(2,1)S(1)}, bf16[2048,512]{1,0:T(8,128)(2,1)}, u32[]{:S(2)}) %copy-start) | copy-done | bytes 2097176
  3.5 1.2 shard_map.82
  6.6 2.7 %shard_map.83 = (s32[4,16]{1,0:T(4,128)}, s32[4,16]{1,0:T(4,128)}, s32[1,32]{1,0:T(1,128)}, s32[1,32]{1,0:T(1,128)}, s32[1,32]{1,0:T(1,128)}, /*index=5*/s32[1,32]{1,0:T(1,128)}) custom-call(s32[2]{0:T(128)} %pad_add_fusion.place_ref, s32[4,16]{1,0:T(4,128)} %bitcast.21), custom_call_target="tpu_custom_call" | custom-call | flops 99999997952 | bytes 4096 | tf_op jit(solution)/shard_map/pallas_call | solution.py:596
  9.4 3.3 %collective-permute-start.2 = (bf16[256,512]{1,0:T(8,128)(2,1)}, bf16[256,512]{1,0:T(8,128)(2,1)S(1)}, u32[]{:S(2)}, u32[]{:S(2)}) collective-permute-start(bf16[256,512]{1,0:T(8,128)(2,1)} %get-tuple-element.93), channel_id=1, source_target_pairs={{2,0},{4,2},{6,4},{8,6},{10,8},{12,10},{14,12},{16,14},{18,16},{20... | collective-permute-start | bytes 786440 | tf_op jit(solution)/shard_map/ppermute | solution.py:663
  13.0 1.0 collective-permute-start.4
  14.2 1.4 copy.16
  16.9 2.2 %collective-permute-done.6.refs_3_ = s32[1,32]{1,0:T(1,128)S(1)} collective-permute-done((s32[1,32]{1,0:T(1,128)S(1)}, s32[1,32]{1,0:T(1,128)S(1)}, u32[]{:S(2)}, u32[]{:S(2)}) %collective-permute-start.6) | collective-permute-done | bytes 160 | tf_op jit(solution)/shard_map/ppermute | solution.py:623
  19.1 1.0 copy-done.6
  20.1 5.0 %shard_map.84 = (bf16[16,512,128]{2,1,0:T(8,128)(2,1)S(1)}, bf16[16,128,512]{2,1,0:T(8,128)(2,1)S(1)}, bf16[2048,512]{1,0:T(8,128)(2,1)S(1)}, bf16[2048,512]{1,0:T(8,128)(2,1)S(1)}) custom-call(bf16[2048,512]{1,0:T(8,128)(2,1)S(1)} %copy-done.1, bf16[2,512,512]{2,1,0:T(8,128)(2,1)S(1)} %bitcast.10, bf16[512,512]{1,0:T(8,128)(2,1)S(1)} %copy-done.6, ...), custom_call_target="tpu_custom_call" | custom-call | flops 100000000 | bytes 100000 | tf_op jit(solution)/shard_map/pallas_call | solution.py:233
  25.1 1.3 copy-done.2
  26.4 1.4 copy-done.4
  27.8 1.3 copy-done.21
  29.8 3.0 %shard_map.85 = (bf16[1024,512]{1,0:T(8,128)(2,1)S(1)}, bf16[1040,512]{1,0:T(8,128)(2,1)S(1)}, bf16[1024,512]{1,0:T(8,128)(2,1)S(1)}, bf16[1024,512]{1,0:T(8,128)(2,1)S(1)}, bf16[256,512]{1,0:T(8,128)(2,1)}) custom-call(s32[2]{0:T(128)S(1)} %copy-done.7, s32[1,32]{1,0:T(1,128)S(1)} %collective-permute-done.3.refs_0_, ...), custom_call_target="tpu_custom_call" | custom-call | flops 1000 | bytes 1000 | tf_op jit(solution)/shard_map/pallas_call | solution.py:518
  35.7 1.0 copy-done.27
  36.7 4.8 %collective-permute-start.12 = (bf16[256,512]{1,0:T(8,128)(2,1)}, bf16[256,512]{1,0:T(8,128)(2,1)}, u32[]{:S(2)}, u32[]{:S(2)}) collective-permute-start(bf16[256,512]{1,0:T(8,128)(2,1)} %get-tuple-element.121), channel_id=1, source_target_pairs={{0,2},{2,4},{4,6},{6,8},{8,10},{10,12},{12,14},{14,16},{16,18},{18... | collective-permute-start | bytes 786440 | tf_op jit(solution)/shard_map/ppermute | solution.py:682
  41.6 1.7 %collective-permute-start.11 = (bf16[1024,512]{1,0:T(8,128)(2,1)}, bf16[1024,512]{1,0:T(8,128)(2,1)}, u32[]{:S(2)}, u32[]{:S(2)}) collective-permute-start(bf16[1024,512]{1,0:T(8,128)(2,1)} %copy-done.24), channel_id=1, source_target_pairs={{0,1},{1,0},{2,3},{3,2},{4,5},{5,4},{6,7},{7,6},{8,9},{9,8},{10,11... | collective-permute-start | bytes 3145736 | tf_op jit(solution)/shard_map/ppermute | solution.py:626
  43.3 1.5 %collective-permute-start.9 = (bf16[1024,512]{1,0:T(8,128)(2,1)}, bf16[1024,512]{1,0:T(8,128)(2,1)}, u32[]{:S(2)}, u32[]{:S(2)}) collective-permute-start(bf16[1024,512]{1,0:T(8,128)(2,1)} %copy-done.26), channel_id=1, source_target_pairs={{0,4},{2,6},{4,0},{6,2},{8,12},{10,14},{12,8},{14,10},{16,20},{18,... | collective-permute-start | bytes 3145736 | tf_op jit(solution)/shard_map/ppermute | solution.py:623
  45.1 1.6 %collective-permute-start.7 = (bf16[1040,512]{1,0:T(8,128)(2,1)}, bf16[1040,512]{1,0:T(8,128)(2,1)}, u32[]{:S(2)}, u32[]{:S(2)}) collective-permute-start(bf16[1040,512]{1,0:T(8,128)(2,1)} %copy-done.23), channel_id=1, source_target_pairs={{0,8},{2,18},{4,12},{6,22},{8,0},{10,26},{12,4},{14,30},{16,24},{1... | collective-permute-start | bytes 3194888 | tf_op jit(solution)/shard_map/ppermute | solution.py:623
  46.7 1.6 %copy-done.5 = bf16[2048,512]{1,0:T(8,128)(2,1)S(1)} copy-done((bf16[2048,512]{1,0:T(8,128)(2,1)S(1)}, bf16[2048,512]{1,0:T(8,128)(2,1)}, u32[]{:S(2)}) %copy-start.5) | copy-done | bytes 2097176
  48.3 1.6 %copy-done.20 = bf16[16,512,128]{2,1,0:T(8,128)(2,1)S(1)} copy-done((bf16[16,512,128]{2,1,0:T(8,128)(2,1)S(1)}, bf16[16,512,128]{2,1,0:T(8,128)(2,1)}, u32[]{:S(2)}) %copy-start.20) | copy-done | bytes 2097176
  49.9 1.6 %copy-done.22 = bf16[16,128,512]{2,1,0:T(8,128)(2,1)S(1)} copy-done((bf16[16,128,512]{2,1,0:T(8,128)(2,1)S(1)}, bf16[16,128,512]{2,1,0:T(8,128)(2,1)}, u32[]{:S(2)}) %copy-start.22) | copy-done | bytes 2097176
  51.5 24.6 %shard_map.86 = (f32[2048,512]{1,0:T(8,128)S(1)}, f32[2048,128]{1,0:T(8,128)S(1)}) custom-call(s32[2]{0:T(128)S(1)} %copy-done.7, s32[32,8]{1,0:T(8,128)S(1)} %copy.14.cols_ref, s32[36]{0:T(128)S(1)} %get-tuple-element.122.where_ref, bf16[1024,512]{1,0:T(8,128)(2,1)} %collective-permute-done.1.refs_5_.refs_0_, bf16[2,512,512]{2,1,0:T(8,128)(2,1)S(1)} %bitcast.11, ...), custom_call_target="tpu_custom_call" | custom-call | flops 999999995904 | bytes 100000 | tf_op jit(solution)/shard_map/pallas_call | solution.py:279
  76.1 2.2 %shard_map.87 = (bf16[1024,512]{1,0:T(8,128)(2,1)S(1)}, bf16[1024,512]{1,0:T(8,128)(2,1)S(1)}) custom-call(s32[2]{0:T(128)S(1)} %copy-done.7, s32[1,32]{1,0:T(1,128)S(1)} %copy-done.12, s32[1,32]{1,0:T(1,128)S(1)} %copy-done.14, s32[1,32]{1,0:T(1,128)S(1)} %copy-done.16, s32[1,32]{1,0:T(1,128)S(1)} %copy-done.18, bf16[2048,512]{1,0:T(8,128)(2,1)S(1)} %copy-done.1, ...), custom_call_target="tpu_custom_call" | custom-call | flops 1000 | bytes 1000 | tf_op jit(solution)/shard_map/pallas_call | solution.py:518
  78.4 1.7 %collective-permute-done.8.refs_4_ = bf16[1024,512]{1,0:T(8,128)(2,1)} collective-permute-done((bf16[1024,512]{1,0:T(8,128)(2,1)}, bf16[1024,512]{1,0:T(8,128)(2,1)}, u32[]{:S(2)}, u32[]{:S(2)}) %collective-permute-start.8) | collective-permute-done | bytes 1048608 | tf_op jit(solution)/shard_map/ppermute | solution.py:623
  80.1 12.7 %collective-permute-start.14 = (bf16[1024,512]{1,0:T(8,128)(2,1)S(1)}, bf16[1024,512]{1,0:T(8,128)(2,1)S(1)}, u32[]{:S(2)}, u32[]{:S(2)}) collective-permute-start(bf16[1024,512]{1,0:T(8,128)(2,1)S(1)} %get-tuple-element.142), channel_id=1, source_target_pairs={{0,2},{2,0},{4,6},{6,4},{8,10},{10,8},{12,14},{14,12},{16,18},{18,... | collective-permute-start | bytes 3145736 | tf_op jit(solution)/shard_map/ppermute | solution.py:623
  93.4 19.3 %shard_map.88 = (f32[2048,512]{1,0:T(8,128)S(1)}, f32[2048,128]{1,0:T(8,128)S(1)}) custom-call(s32[2]{0:T(128)S(1)} %copy-done.7, s32[32,8]{1,0:T(8,128)S(1)} %copy.14.cols_ref, s32[36]{0:T(128)S(1)} %get-tuple-element.131.where_ref, bf16[1024,512]{1,0:T(8,128)(2,1)} %collective-permute-done.1.refs_5_.refs_0_, ...), custom_call_target="tpu_custom_call", output_to_operand_aliasing={{0}: (9, {}), {1}: (10, {})} | custom-call | flops 100000000 | bytes 100000 | tf_op jit(solution)/shard_map/pallas_call | solution.py:279
  112.7 1.2 collective-permute-start.13
  113.8 3.7 %collective-permute-done.15.refs_3_ = bf16[1024,512]{1,0:T(8,128)(2,1)S(1)} collective-permute-done((bf16[1024,512]{1,0:T(8,128)(2,1)S(1)}, bf16[1024,512]{1,0:T(8,128)(2,1)S(1)}, u32[]{:S(2)}, u32[]{:S(2)}) %collective-permute-start.15) | collective-permute-done | bytes 1048608 | tf_op jit(solution)/shard_map/ppermute | solution.py:623
  118.0 19.5 %shard_map.89 = (f32[2176,512]{1,0:T(8,128)S(1)}, f32[2176,128]{1,0:T(8,128)S(1)}, bf16[2048,512]{1,0:T(8,128)(2,1)}) custom-call(s32[2]{0:T(128)S(1)} %copy-done.7, s32[4,16]{1,0:T(4,128)S(1)} %bitcast.15, s32[4,16]{1,0:T(4,128)S(1)} %copy-done.10, bf16[1024,512]{1,0:T(8,128)(2,1)} %collective-permute-done.10.refs_0_, ...), custom_call_target="tpu_custom_call" | custom-call | flops 268435456 | bytes 1048576 | tf_op jit(solution)/shard_map/pallas_call | solution.py:406
  137.5 3.3 %collective-permute-done.13.refs_0_ = bf16[1040,512]{1,0:T(8,128)(2,1)S(1)} collective-permute-done((bf16[1040,512]{1,0:T(8,128)(2,1)}, bf16[1040,512]{1,0:T(8,128)(2,1)S(1)}, u32[]{:S(2)}, u32[]{:S(2)}) %collective-permute-start.13) | collective-permute-done | bytes 1064992 | tf_op jit(solution)/shard_map/ppermute | solution.py:626
  140.8 6.6 %shard_map.90 = bf16[2048,512]{1,0:T(8,128)(2,1)} custom-call(s32[2]{0:T(128)S(1)} %copy-done.7, s32[4,16]{1,0:T(4,128)S(1)} %bitcast.16, s32[4,16]{1,0:T(4,128)S(1)} %copy-done.9, bf16[1040,512]{1,0:T(8,128)(2,1)S(1)} %collective-permute-done.13.refs_0_, bf16[2048,512]{1,0:T(8,128)(2,1)S(1)} %copy-done.3, ...), custom_call_target="tpu_custom_call", output_to_operand_aliasing={{}: (8, {})} | custom-call | flops 268435456 | bytes 1048576 | tf_op jit(solution)/shard_map/pallas_call | solution.py:406
  (81 shorter events, 9.4 us)
Async XLA Ops:
  0.7 5.1 %collective-permute-start = (f32[2,256]{1,0:T(2,128)S(1)}, f32[2,256]{1,0:T(2,128)S(1)}, u32[]{:S(2)}, u32[]{:S(2)}) collective-permute-start(f32[2,256]{1,0:T(2,128)S(1)} %pad_maximum_fusion), channel_id=1, source_target_pairs={{0,1},{1,0},{2,3},{3,2},{4,5},{5,4},{6,7},{7,6},{8,9},{9,8},{10,11... | collective-permute-start | bytes 6152 | tf_op jit(solution)/shard_map/ppermute | solution.py:626
  5.8 24.0 %collective-permute-start.1 = (bf16[1024,512]{1,0:T(8,128)(2,1)}, bf16[1024,512]{1,0:T(8,128)(2,1)}, u32[]{:S(2)}, u32[]{:S(2)}) collective-permute-start(bf16[1024,512]{1,0:T(8,128)(2,1)} %get-tuple-element.85), channel_id=1, source_target_pairs={{0,1},{1,0},{2,3},{3,2},{4,5},{5,4},{6,7},{7,6},{8,9},{9,8},{10,11... | collective-permute-start | bytes 3145736 | tf_op jit(solution)/shard_map/ppermute | solution.py:626
  9.4 9.7 %copy-start.1 = (bf16[2048,512]{1,0:T(8,128)(2,1)S(1)}, bf16[2048,512]{1,0:T(8,128)(2,1)}, u32[]{:S(2)}) copy-start(bf16[2048,512]{1,0:T(8,128)(2,1)} %refs_4_.3) | copy-start | bytes 6291460
  9.4 9.7 %collective-permute-start.2 = (bf16[256,512]{1,0:T(8,128)(2,1)}, bf16[256,512]{1,0:T(8,128)(2,1)S(1)}, u32[]{:S(2)}, u32[]{:S(2)}) collective-permute-start(bf16[256,512]{1,0:T(8,128)(2,1)} %get-tuple-element.93), channel_id=1, source_target_pairs={{2,0},{4,2},{6,4},{8,6},{10,8},{12,10},{14,12},{16,14},{18,16},{20... | collective-permute-start | bytes 786440 | tf_op jit(solution)/shard_map/ppermute | solution.py:663
  12.7 3.0 %collective-permute-start.3 = (s32[1,32]{1,0:T(1,128)}, s32[1,32]{1,0:T(1,128)S(1)}, u32[]{:S(2)}, u32[]{:S(2)}) collective-permute-start(s32[1,32]{1,0:T(1,128)} %get-tuple-element.95), channel_id=1, source_target_pairs={{0,2},{2,0},{4,6},{6,4},{8,10},{10,8},{12,14},{14,12},{16,18},{18,... | collective-permute-start | bytes 392 | tf_op jit(solution)/shard_map/ppermute | solution.py:623
  13.0 3.0 %collective-permute-start.4 = (s32[1,32]{1,0:T(1,128)}, s32[1,32]{1,0:T(1,128)S(1)}, u32[]{:S(2)}, u32[]{:S(2)}) collective-permute-start(s32[1,32]{1,0:T(1,128)} %get-tuple-element.96), channel_id=1, source_target_pairs={{0,4},{2,6},{4,0},{6,2},{8,12},{10,14},{12,8},{14,10},{16,20},{18,... | collective-permute-start | bytes 392 | tf_op jit(solution)/shard_map/ppermute | solution.py:623
  14.0 2.8 %collective-permute-start.5 = (s32[1,32]{1,0:T(1,128)}, s32[1,32]{1,0:T(1,128)S(1)}, u32[]{:S(2)}, u32[]{:S(2)}) collective-permute-start(s32[1,32]{1,0:T(1,128)} %get-tuple-element.97), channel_id=1, source_target_pairs={{0,8},{2,10},{4,12},{6,14},{8,0},{10,2},{12,4},{14,6},{16,24},{18,... | collective-permute-start | bytes 392 | tf_op jit(solution)/shard_map/ppermute | solution.py:623
  15.6 14.1 %copy-start.7 = (s32[2]{0:T(128)S(1)}, s32[2]{0:T(128)}, u32[]{:S(2)}) copy-start(s32[2]{0:T(128)} %pad_add_fusion.place_ref) | copy-start | bytes 28
  15.7 17.1 %copy-start.11 = (s32[1,32]{1,0:T(1,128)}, s32[1,32]{1,0:T(1,128)S(1)}, u32[]{:S(2)}) copy-start(s32[1,32]{1,0:T(1,128)S(1)} %collective-permute-done.3.refs_0_) | copy-start | bytes 388
  15.7 3.4 %collective-permute-start.6 = (s32[1,32]{1,0:T(1,128)S(1)}, s32[1,32]{1,0:T(1,128)S(1)}, u32[]{:S(2)}, u32[]{:S(2)}) collective-permute-start(s32[1,32]{1,0:T(1,128)S(1)} %copy-done.31), channel_id=1, source_target_pairs={{0,16},{2,18},{4,20},{6,22},{8,24},{10,26},{12,28},{14,30},{16,0},... | collective-permute-start | bytes 392 | tf_op jit(solution)/shard_map/ppermute | solution.py:623
  16.0 16.8 %copy-start.13 = (s32[1,32]{1,0:T(1,128)}, s32[1,32]{1,0:T(1,128)S(1)}, u32[]{:S(2)}) copy-start(s32[1,32]{1,0:T(1,128)S(1)} %collective-permute-done.4.refs_1_) | copy-start | bytes 388
  16.9 15.9 %copy-start.15 = (s32[1,32]{1,0:T(1,128)}, s32[1,32]{1,0:T(1,128)S(1)}, u32[]{:S(2)}) copy-start(s32[1,32]{1,0:T(1,128)S(1)} %collective-permute-done.5.refs_2_) | copy-start | bytes 388
  19.0 13.7 %copy-start.17 = (s32[1,32]{1,0:T(1,128)}, s32[1,32]{1,0:T(1,128)S(1)}, u32[]{:S(2)}) copy-start(s32[1,32]{1,0:T(1,128)S(1)} %collective-permute-done.6.refs_3_) | copy-start | bytes 388
  29.1 12.4 %copy-start.28 = (s32[32,8]{0,1:T(8,128)S(1)}, s32[32,8]{0,1:T(8,128)}, u32[]{:S(2)}) copy-start(s32[32,8]{0,1:T(8,128)} %param.13) | copy-start | bytes 3076
  36.7 8.4 %collective-permute-start.12 = (bf16[256,512]{1,0:T(8,128)(2,1)}, bf16[256,512]{1,0:T(8,128)(2,1)}, u32[]{:S(2)}, u32[]{:S(2)}) collective-permute-start(bf16[256,512]{1,0:T(8,128)(2,1)} %get-tuple-element.121), channel_id=1, source_target_pairs={{0,2},{2,4},{4,6},{6,8},{8,10},{10,12},{12,14},{14,16},{16,18},{18... | collective-permute-start | bytes 786440 | tf_op jit(solution)/shard_map/ppermute | solution.py:682
  41.6 34.5 %collective-permute-start.11 = (bf16[1024,512]{1,0:T(8,128)(2,1)}, bf16[1024,512]{1,0:T(8,128)(2,1)}, u32[]{:S(2)}, u32[]{:S(2)}) collective-permute-start(bf16[1024,512]{1,0:T(8,128)(2,1)} %copy-done.24), channel_id=1, source_target_pairs={{0,1},{1,0},{2,3},{3,2},{4,5},{5,4},{6,7},{7,6},{8,9},{9,8},{10,11... | collective-permute-start | bytes 3145736 | tf_op jit(solution)/shard_map/ppermute | solution.py:626
  43.3 36.8 %collective-permute-start.8 = (bf16[1024,512]{1,0:T(8,128)(2,1)}, bf16[1024,512]{1,0:T(8,128)(2,1)}, u32[]{:S(2)}, u32[]{:S(2)}) collective-permute-start(bf16[1024,512]{1,0:T(8,128)(2,1)} %copy-done.27), channel_id=1, source_target_pairs={{0,16},{2,10},{4,20},{6,14},{8,24},{10,2},{12,28},{14,6},{16,0},{1... | collective-permute-start | bytes 3145736 | tf_op jit(solution)/shard_map/ppermute | solution.py:623
  43.3 36.8 %collective-permute-start.9 = (bf16[1024,512]{1,0:T(8,128)(2,1)}, bf16[1024,512]{1,0:T(8,128)(2,1)}, u32[]{:S(2)}, u32[]{:S(2)}) collective-permute-start(bf16[1024,512]{1,0:T(8,128)(2,1)} %copy-done.26), channel_id=1, source_target_pairs={{0,4},{2,6},{4,0},{6,2},{8,12},{10,14},{12,8},{14,10},{16,20},{18,... | collective-permute-start | bytes 3145736 | tf_op jit(solution)/shard_map/ppermute | solution.py:623
  44.8 35.3 %collective-permute-start.10 = (bf16[1024,512]{1,0:T(8,128)(2,1)}, bf16[1024,512]{1,0:T(8,128)(2,1)}, u32[]{:S(2)}, u32[]{:S(2)}) collective-permute-start(bf16[1024,512]{1,0:T(8,128)(2,1)} %copy-done.25), channel_id=1, source_target_pairs={{0,2},{2,0},{4,6},{6,4},{8,10},{10,8},{12,14},{14,12},{16,18},{18,... | collective-permute-start | bytes 3145736 | tf_op jit(solution)/shard_map/ppermute | solution.py:623
  45.1 67.5 %collective-permute-start.7 = (bf16[1040,512]{1,0:T(8,128)(2,1)}, bf16[1040,512]{1,0:T(8,128)(2,1)}, u32[]{:S(2)}, u32[]{:S(2)}) collective-permute-start(bf16[1040,512]{1,0:T(8,128)(2,1)} %copy-done.23), channel_id=1, source_target_pairs={{0,8},{2,18},{4,12},{6,22},{8,0},{10,26},{12,4},{14,30},{16,24},{1... | collective-permute-start | bytes 3194888 | tf_op jit(solution)/shard_map/ppermute | solution.py:623
  51.5 24.6 %copy-start.12 = (s32[1,32]{1,0:T(1,128)S(1)}, s32[1,32]{1,0:T(1,128)}, u32[]{:S(2)}) copy-start(s32[1,32]{1,0:T(1,128)} %copy-done.11) | copy-start | bytes 388
  51.5 24.6 %copy-start.14 = (s32[1,32]{1,0:T(1,128)S(1)}, s32[1,32]{1,0:T(1,128)}, u32[]{:S(2)}) copy-start(s32[1,32]{1,0:T(1,128)} %copy-done.13) | copy-start | bytes 388
  51.5 24.6 %copy-start.16 = (s32[1,32]{1,0:T(1,128)S(1)}, s32[1,32]{1,0:T(1,128)}, u32[]{:S(2)}) copy-start(s32[1,32]{1,0:T(1,128)} %copy-done.15) | copy-start | bytes 388
  51.5 24.6 %copy-start.18 = (s32[1,32]{1,0:T(1,128)S(1)}, s32[1,32]{1,0:T(1,128)}, u32[]{:S(2)}) copy-start(s32[1,32]{1,0:T(1,128)} %copy-done.17) | copy-start | bytes 388
  80.1 37.9 %copy-start.3 = (bf16[2048,512]{1,0:T(8,128)(2,1)S(1)}, bf16[2048,512]{1,0:T(8,128)(2,1)}, u32[]{:S(2)}) copy-start(bf16[2048,512]{1,0:T(8,128)(2,1)} %copy-done.2) | copy-start | bytes 6291460
  80.1 37.9 %copy-start.8 = (s32[1,4,16]{2,1,0:T(4,128)S(1)}, s32[1,4,16]{2,1,0:T(4,128)}, u32[]{:S(2)}) copy-start(s32[1,4,16]{2,1,0:T(4,128)} %param.14) | copy-start | bytes 772
  80.1 37.9 %copy-start.10 = (s32[4,16]{1,0:T(4,128)S(1)}, s32[4,16]{1,0:T(4,128)}, u32[]{:S(2)}) copy-start(s32[4,16]{1,0:T(4,128)} %get-tuple-element.140.spots_ref) | copy-start | bytes 772
  80.1 33.8 %collective-permute-start.14 = (bf16[1024,512]{1,0:T(8,128)(2,1)S(1)}, bf16[1024,512]{1,0:T(8,128)(2,1)S(1)}, u32[]{:S(2)}, u32[]{:S(2)}) collective-permute-start(bf16[1024,512]{1,0:T(8,128)(2,1)S(1)} %get-tuple-element.142), channel_id=1, source_target_pairs={{0,2},{2,0},{4,6},{6,4},{8,10},{10,8},{12,14},{14,12},{16,18},{18,... | collective-permute-start | bytes 3145736 | tf_op jit(solution)/shard_map/ppermute | solution.py:623
  92.8 24.7 %collective-permute-start.15 = (bf16[1024,512]{1,0:T(8,128)(2,1)S(1)}, bf16[1024,512]{1,0:T(8,128)(2,1)S(1)}, u32[]{:S(2)}, u32[]{:S(2)}) collective-permute-start(bf16[1024,512]{1,0:T(8,128)(2,1)S(1)} %get-tuple-element.144), channel_id=1, source_target_pairs={{0,4},{2,6},{4,0},{6,2},{8,12},{10,14},{12,8},{14,10},{16,20},{18,... | collective-permute-start | bytes 3145736 | tf_op jit(solution)/shard_map/ppermute | solution.py:623
  93.4 24.6 %collective-permute-start.16 = (bf16[1024,512]{1,0:T(8,128)(2,1)}, bf16[1024,512]{1,0:T(8,128)(2,1)S(1)}, u32[]{:S(2)}, u32[]{:S(2)}) collective-permute-start(bf16[1024,512]{1,0:T(8,128)(2,1)} %collective-permute-done.8.refs_4_), channel_id=1, source_target_pairs={{0,1},{1,0},{2,3},{3,2},{4,5},{5,4},{6,7},{7,6},{8,9},{9,8},{10,11... | collective-permute-start | bytes 3145736 | tf_op jit(solution)/shard_map/ppermute | solution.py:626
  112.7 28.1 %collective-permute-start.13 = (bf16[1040,512]{1,0:T(8,128)(2,1)}, bf16[1040,512]{1,0:T(8,128)(2,1)S(1)}, u32[]{:S(2)}, u32[]{:S(2)}) collective-permute-start(bf16[1040,512]{1,0:T(8,128)(2,1)} %collective-permute-done.7.refs_5_), channel_id=1, source_target_pairs={{0,1},{1,0},{2,3},{3,2},{4,5},{5,4},{6,7},{7,6},{8,9},{9,8},{10,11... | collective-permute-start | bytes 3194888 | tf_op jit(solution)/shard_map/ppermute | solution.py:626
  118.0 22.8 %copy-start.9 = (s32[4,16]{1,0:T(4,128)S(1)}, s32[4,16]{1,0:T(4,128)}, u32[]{:S(2)}) copy-start(s32[4,16]{1,0:T(4,128)} %get-tuple-element.84.spots_ref) | copy-start | bytes 772
  (17 other events, 45.5 us)

commit v3 on v2

v3 whole, which is shorter than its diff:
```python
import functools
import math

import jax
import jax.numpy as jnp
from jax import lax
from jax.experimental import pallas as pl
from jax.experimental.pallas import tpu as pltpu
from jax.sharding import PartitionSpec as P

HEADS = 8
TILE = 128
HT = 2
MATCH = 4
LANES = 128
GROUP = 4
MIB = 1024 * 1024

ANY = pl.BlockSpec(memory_space=pl.ANY)
SMEM = pl.BlockSpec(memory_space=pltpu.SMEM)
VMEM = pl.BlockSpec(memory_space=pltpu.VMEM)
HBM = pl.BlockSpec(memory_space=pltpu.HBM)


def lane_masks():
    lane = lax.broadcasted_iota(jnp.int32, (TILE, LANES), 1)
    return lane < LANES // 2, lane % (LANES // 2)


def pack_denominators(pieces):
    _, within = lane_masks()
    size = LANES // 2 // len(pieces)
    packed = pieces[-1]
    for pair in range(len(pieces) - 2, -1, -1):
        packed = jnp.where(within < (pair + 1) * size, pieces[pair], packed)
    return packed


def denominator_chooser(pairs):
    size = LANES // 2 // pairs
    shape = (2 * LANES, pairs * LANES)
    source = lax.broadcasted_iota(jnp.int32, shape, 0) % LANES
    target = lax.broadcasted_iota(jnp.int32, shape, 1)
    wanted = target // LANES * size + (target % LANES) // (LANES // 2) * (LANES // 2)
    return jnp.where(source == wanted, 1.0, 0.0).astype(jnp.bfloat16)


def spread_reciprocals(packed, chooser):
    inverse = 1.0 / packed
    coarse = inverse.astype(jnp.bfloat16)
    fine = (inverse - coarse.astype(jnp.float32)).astype(jnp.bfloat16)
    return jnp.dot(
        jnp.concatenate([coarse, fine], axis=1), chooser, preferred_element_type=jnp.float32
    )


def project(rows, w, keys, values, first):
    new_keys = jnp.dot(rows, w[0], preferred_element_type=jnp.float32).astype(jnp.bfloat16).T
    new_values = jnp.dot(rows, w[1], preferred_element_type=jnp.float32).astype(jnp.bfloat16)
    for index in range(rows.shape[0] // TILE):
        span = slice(index * TILE, (index + 1) * TILE)
        keys[first + index] = new_keys[:, span]
        values[first + index] = new_values[span, :]


def attend_chunks(queries, keys, values, ones, num, den, units):
    low, _ = lane_masks()
    low_mask = jnp.where(low, 1.0, 0.0).astype(jnp.bfloat16)
    high_mask = jnp.where(low, 0.0, 1.0).astype(jnp.bfloat16)
    rows = [pl.ds(pl.multiple_of(unit[0] * TILE, TILE), TILE) for unit in units]
    last = queries.shape[0] // TILE - 1
    query_rows = [
        pl.ds(pl.multiple_of(jnp.minimum(unit[0], last) * TILE, TILE), TILE) for unit in units
    ]
    denominators = [[] for _ in units]
    for pair in range(queries.shape[1] // LANES):
        part = slice(pair * LANES, (pair + 1) * LANES)
        weights = []
        for row, (_, one, two, _) in zip(query_rows, units):
            some = queries[row, part]
            scores = jnp.dot(
                jnp.concatenate([some * low_mask, some * high_mask], axis=0),
                jnp.concatenate([keys[one, part, :], keys[two, part, :]], axis=1),
                preferred_element_type=jnp.float32,
            )
            weights.append(jnp.exp(jnp.clip(scores, -5.0, 5.0)).astype(jnp.bfloat16))
        sums = []
        for weight, (_, one, two, fills) in zip(weights, units):
            counts = ones[fills]
            wide = [
                jnp.concatenate([values[one, :, part], ones[0]], axis=1),
                jnp.concatenate([values[two, :, part] * counts, counts], axis=1),
            ]
            sums.append(
                jnp.dot(
                    weight, jnp.concatenate(wide, axis=0), preferred_element_type=jnp.float32
                )
            )
        for row, both, listed in zip(rows, sums, denominators):
            num[row, part] += jnp.where(low, both[:TILE, :LANES], both[TILE:, :LANES])
            listed.append(jnp.where(low, both[:TILE, LANES:], both[TILE:, LANES:]))
    for row, listed in zip(rows, denominators):
        den[row, :] += pack_denominators(listed)


def attend_units(queries, keys, values, num, den, units):
    low_lanes, _ = lane_masks()
    low = jnp.where(low_lanes, 1.0, 0.0).astype(jnp.bfloat16)
    high = jnp.where(low_lanes, 0.0, 1.0).astype(jnp.bfloat16)
    nothing = jnp.zeros((LANES // 2, TILE), jnp.bfloat16)
    rows = [pl.ds(pl.multiple_of(row * TILE, TILE), TILE) for row, _ in units]
    last = queries.shape[0] // TILE - 1
    query_rows = [
        pl.ds(pl.multiple_of(jnp.minimum(row, last) * TILE, TILE), TILE) for row, _ in units
    ]
    denominators = [[] for _ in units]
    for pair in range(queries.shape[1] // LANES):
        part = slice(pair * LANES, (pair + 1) * LANES)
        middle = pair * LANES + LANES // 2
        weights = []
        for row, (_, tile) in zip(query_rows, units):
            first = jnp.concatenate([keys[tile, pair * LANES : middle, :], nothing], axis=0)
            second = jnp.concatenate([nothing, keys[tile, middle : (pair + 1) * LANES, :]], axis=0)
            scores = jnp.dot(
                queries[row, part],
                jnp.concatenate([first, second], axis=1),
                preferred_element_type=jnp.float32,
            )
            weights.append(jnp.exp(jnp.clip(scores, -5.0, 5.0)).astype(jnp.bfloat16))
        sums = []
        for weight, (_, tile) in zip(weights, units):
            value = values[tile, :, part]
            wide = jnp.concatenate(
                [
                    jnp.concatenate([value * low, low], axis=1),
                    jnp.concatenate([value * high, high], axis=1),
                ],
                axis=0,
            )
            sums.append(jnp.dot(weight, wide, preferred_element_type=jnp.float32))
        for row, both, listed in zip(rows, sums, denominators):
            num[row, part] += both[:, :LANES]
            listed.append(both[:, LANES:])
    for row, listed in zip(rows, denominators):
        den[row, :] += pack_denominators(listed)


def project_pieces(pieces, w, keys, values, at):
    for piece in pieces:
        tiles = piece.shape[0] // TILE
        size = math.gcd(tiles, GROUP)

        def some_tiles(index, carry, piece=piece, at=at, size=size):
            some = piece[pl.ds(pl.multiple_of(index * size * TILE, TILE), size * TILE), :]
            project(some, w, keys, values, at + index * size)
            return carry

        lax.fori_loop(0, tiles // size, some_tiles, 0)
        at += tiles


def attend_listed(
    steps, split, place_ref, cols_ref, where_ref, queries, keys, values, num, den, scratch
):
    ones, row_list, tile_list, fill_list = scratch
    tiles_here = queries.shape[0] // TILE
    slots = tile_list.shape[0] - 2 * row_list.shape[0]
    ones[0] = jnp.ones(ones.shape[1:], ones.dtype)
    ones[1] = jnp.zeros(ones.shape[1:], ones.dtype)

    def visit(row, found):
        part = jnp.where(row < split, 0, 1)
        at = 2 * found
        for slot in range(slots):
            tile = where_ref[part, cols_ref[(place_ref[0] * tiles_here + row) * slots + slot]]
            tile_list[at] = tile
            at = at + (tile >= 0).astype(jnp.int32)
        tile_list[at] = 0
        units = (at - 2 * found + 1) // 2
        odd = lax.rem(at, 2)
        for unit in range(slots // 2):
            row_list[found + unit] = row
            fill_list[found + unit] = jnp.where(unit == units - 1, odd, 0)
        return found + units

    found = lax.fori_loop(0, steps, visit, jnp.int32(0))
    for inner in range(GROUP):
        row_list[found + inner] = tiles_here
        fill_list[found + inner] = 0
        tile_list[2 * (found + inner)] = 0
        tile_list[2 * (found + inner) + 1] = 0

    def group(index, carry):
        units = []
        for inner in range(GROUP):
            unit = index * GROUP + inner
            units.append(
                (row_list[unit], tile_list[2 * unit], tile_list[2 * unit + 1], fill_list[unit])
            )
        attend_chunks(queries, keys, values, ones, num, den, units)
        return carry

    lax.fori_loop(0, (found + GROUP - 1) // GROUP, group, 0)


def each_tile(tiles, action):
    def visit(tile, carry):
        action(pl.ds(pl.multiple_of(tile * TILE, TILE), TILE))
        return carry

    lax.fori_loop(0, tiles, visit, 0)


def own_kernel(split, place_ref, cols_ref, where_ref, rows, w, wq, scales, *refs):
    (num, den, keys, values, local_ref, expand_ref) = refs[:6]
    width = rows.shape[1]
    tiles = rows.shape[0] // TILE
    size = min(GROUP, tiles)
    project_pieces([rows], w, keys, values, 0)

    def some_queries(index, carry):
        target = pl.ds(pl.multiple_of(index * size * TILE, TILE), size * TILE)
        queries = jnp.dot(rows[target, :], wq[...], preferred_element_type=jnp.float32)
        queries = queries.astype(jnp.bfloat16).astype(jnp.float32)
        scale = 1.0 / math.sqrt(width // HEADS)
        local_ref[target, :] = (queries * scales[0:1, :] * scale).astype(jnp.bfloat16)
        expand_ref[target, :] = (queries * scales[1:2, :] * scale).astype(jnp.bfloat16)
        return carry

    lax.fori_loop(0, tiles // size, some_queries, 0)

    def clear(target):
        num[target, :] = jnp.zeros((TILE, width), jnp.float32)
        den[target, :] = jnp.zeros((TILE, LANES), jnp.float32)

    each_tile(tiles + 1, clear)
    attend_listed(
        split, split, place_ref, cols_ref, where_ref, local_ref, keys, values, num, den, refs[6:]
    )


def more_kernel(count, from_own, split, place_ref, cols_ref, where_ref, *refs):
    pieces = refs[:count]
    (w, local_ref, num_in, den_in) = refs[count : count + 4]
    refs = refs[count + 4 :]
    if from_own:
        (own_keys, own_values, num, den, *scratch, keys, values) = refs
        first = own_keys.shape[0]

        def bring(tile, carry):
            keys[tile] = own_keys[tile]
            values[tile] = own_values[tile]
            return carry

        lax.fori_loop(0, first, bring, 0)
    else:
        (num, den, *scratch, keys, values) = refs
        first = 0
    project_pieces(pieces, w, keys, values, first)

    def begin(target):
        num[target, :] = num_in[target, :]
        den[target, :] = den_in[target, :]

    tiles = local_ref.shape[0] // TILE
    each_tile(tiles + 1, begin)
    attend_listed(
        tiles, split, place_ref, cols_ref, where_ref, local_ref, keys, values, num, den, scratch
    )


def sums_shapes(own_rows, width):
    return [
        jax.ShapeDtypeStruct((own_rows + TILE, width), jnp.float32),
        jax.ShapeDtypeStruct((own_rows + TILE, LANES), jnp.float32),
    ]


def list_scratch(own_rows, slots):
    units = own_rows // TILE * (slots // 2) + GROUP
    return [
        pltpu.VMEM((2, TILE, LANES), jnp.bfloat16),
        pltpu.SMEM((units,), jnp.int32),
        pltpu.SMEM((2 * units + slots,), jnp.int32),
        pltpu.SMEM((units,), jnp.int32),
    ]


def own_attention(tables, rows, w, wq, scales, split, slots):
    own_rows, width = rows.shape
    tiles = own_rows // TILE
    shapes = [(tiles, width, TILE), (tiles, TILE, width), rows.shape, rows.shape]
    return pl.pallas_call(
        functools.partial(own_kernel, split),
        in_specs=[SMEM] * 3 + [VMEM] * 4,
        out_specs=[VMEM] * 6,
        out_shape=sums_shapes(own_rows, width)
        + [jax.ShapeDtypeStruct(shape, jnp.bfloat16) for shape in shapes],
        scratch_shapes=list_scratch(own_rows, slots),
        compiler_params=pltpu.CompilerParams(vmem_limit_bytes=24 * MIB),
        cost_estimate=pl.CostEstimate(flops=10**8, bytes_accessed=10**5, transcendentals=0),
    )(*tables, rows, w, wq, scales)


def more_attention(tables, pieces, w, local_q, num, den, own, split, slots):
    own_rows, width = local_q.shape
    tiles = sum(piece.shape[0] // TILE for piece in pieces) + (own_rows // TILE if own else 0)
    return pl.pallas_call(
        functools.partial(more_kernel, len(pieces), bool(own), split),
        in_specs=[SMEM] * 3 + [VMEM] * (len(pieces) + 4 + len(own)),
        out_specs=[VMEM] * 2,
        out_shape=sums_shapes(own_rows, width),
        scratch_shapes=list_scratch(own_rows, slots)
        + [
            pltpu.VMEM((tiles, width, TILE), jnp.bfloat16),
            pltpu.VMEM((tiles, TILE, width), jnp.bfloat16),
        ],
        compiler_params=pltpu.CompilerParams(vmem_limit_bytes=24 * MIB),
        cost_estimate=pl.CostEstimate(
            flops=10**12 if own else 10**8, bytes_accessed=10**5, transcendentals=0
        ),
    )(*tables, *pieces, w, local_q, num, den, *own)


def expand_kernel(count, gives_out, last, place_ref, rows_ref, spots_ref, *refs):
    sources = refs[:count]
    (expand_q, num_in, den_in, w) = refs[count : count + 4]
    refs = refs[count + 4 :]
    if last:
        (_, out_ref, features, keys, values, num, den, row_list, tile_list, mark) = refs[:-3]
        (results, result_sems) = refs[-3:-1]
    else:
        if gives_out:
            (num, den, out_ref) = refs[:3]
        else:
            (num, den) = refs[:2]
        (features, keys, values, row_list, tile_list, mark) = refs[-7:-1]
    chooser = refs[-1]
    own_rows, width = expand_q.shape
    tiles_here = own_rows // TILE
    matchings, edges = rows_ref.shape
    if gives_out:
        chooser[...] = denominator_chooser(width // LANES)
    for tile in range(tiles_here):
        mark[tile] = 0 if last else 1

    def visit(edge, found):
        for matching in range(matchings):
            row = rows_ref[matching, edge] - place_ref[0] * tiles_here
            spot = spots_ref[matching, edge]
            mine = jnp.logical_and(jnp.logical_and(row >= 0, row < tiles_here), spot >= 0)
            row_list[found] = row
            tile_list[found] = spot
            found = found + mine.astype(jnp.int32)
            if last:

                @pl.when(mine)
                def _():
                    mark[row] = 1

        return found

    found = lax.fori_loop(0, edges, visit, jnp.int32(0))
    for inner in range(GROUP):
        row_list[found + inner] = tiles_here
        tile_list[found + inner] = 0

    def each_marked(action):
        def visit_tile(tile, carry):
            target = pl.ds(pl.multiple_of(tile * TILE, TILE), TILE)
            pl.when(mark[tile] == 1)(lambda: action(tile, target))
            return carry

        lax.fori_loop(0, tiles_here, visit_tile, 0)

    def begin(tile, target):
        num[target, :] = num_in[target, :]
        den[target, :] = den_in[target, :]

    each_marked(begin)
    spare = pl.ds(own_rows, TILE)
    num[spare, :] = jnp.zeros((TILE, width), jnp.float32)
    den[spare, :] = jnp.zeros((TILE, LANES), jnp.float32)

    def group(index, carry):
        first = index * GROUP
        for i in range(GROUP):
            spot = tile_list[first + i]
            for source in sources:
                tiles = source.shape[0] // TILE

                @pl.when(jnp.logical_and(spot >= 0, spot < tiles))
                def _(source=source, spot=spot):
                    rows = pl.ds(pl.multiple_of(spot * TILE, TILE), TILE)
                    features[i * TILE : (i + 1) * TILE, :] = source[rows, :]

                spot = spot - tiles
        project(features[...], w, keys, values, 0)
        units = [(row_list[first + i], i) for i in range(GROUP)]
        attend_units(expand_q, keys, values, num, den, units)
        return carry

    lax.fori_loop(0, (found + GROUP - 1) // GROUP, group, 0)

    def finish(tile, target):
        inverse = spread_reciprocals(den[target, :], chooser[...])
        result = (num[target, :] * inverse).astype(jnp.bfloat16)
        if last:
            results[target, :] = result
            copy_out(tile, target).start()
        else:
            out_ref[target, :] = result

    def copy_out(tile, target):
        return pltpu.make_async_copy(results.at[target], out_ref.at[target], result_sems.at[tile])

    if gives_out:
        each_marked(finish)
    if last:
        each_marked(lambda tile, target: copy_out(tile, target).wait())


def expand_attention(place, exp_rows, spots, sources, expand_q, num, den, w, gives_out, out):
    width = w.shape[2]
    own_rows = expand_q.shape[0]
    last = out is not None
    most = exp_rows.shape[0] * exp_rows.shape[1] + GROUP
    sums = sums_shapes(own_rows, width)
    result = jax.ShapeDtypeStruct((own_rows, width), jnp.bfloat16)
    sums_scratch = [pltpu.VMEM(array.shape, array.dtype) for array in sums]
    arguments = [place, exp_rows, spots, *sources, expand_q, num, den, w]
    return pl.pallas_call(
        functools.partial(expand_kernel, len(sources), gives_out, last),
        in_specs=[SMEM] * 3 + [VMEM] * (len(sources) + 4) + [ANY] * last,
        out_specs=ANY if last else [VMEM] * (2 + gives_out),
        out_shape=result if last else sums + [result] * gives_out,
        input_output_aliases={len(arguments): 0} if last else {},
        scratch_shapes=[
            pltpu.VMEM((GROUP * TILE, width), jnp.bfloat16),
            pltpu.VMEM((GROUP, width, TILE), jnp.bfloat16),
            pltpu.VMEM((GROUP, TILE, width), jnp.bfloat16),
        ]
        + (sums_scratch if last else [])
        + [
            pltpu.SMEM((most,), jnp.int32),
            pltpu.SMEM((most,), jnp.int32),
            pltpu.SMEM((own_rows // TILE,), jnp.int32),
        ]
        + (
            [
                pltpu.VMEM((own_rows, width), jnp.bfloat16),
                pltpu.SemaphoreType.DMA((own_rows // TILE,)),
            ]
            if last
            else []
        )
        + [pltpu.VMEM((2 * LANES, width), jnp.bfloat16)],
        compiler_params=pltpu.CompilerParams(vmem_limit_bytes=24 * MIB),
        cost_estimate=pl.CostEstimate(
            flops=own_rows * width * 256, bytes_accessed=own_rows * width, transcendentals=0
        ),
    )(*arguments, *([out] if last else []))


def cut_half_kernel(here_ref, features, half_ref, buffer, sem):
    rows = half_ref.shape[0]
    start = pl.multiple_of(here_ref[0] * rows, TILE)
    inward = pltpu.make_async_copy(features.at[pl.ds(start, rows)], buffer, sem)
    inward.start()
    inward.wait()
    outward = pltpu.make_async_copy(buffer, half_ref, sem)
    outward.start()
    outward.wait()


def cut_half(here, features):
    half = (features.shape[0] // 2, features.shape[1])
    return pl.pallas_call(
        cut_half_kernel,
        in_specs=[SMEM, ANY],
        out_specs=ANY,
        out_shape=jax.ShapeDtypeStruct(half, jnp.bfloat16),
        scratch_shapes=[pltpu.VMEM(half, jnp.bfloat16), pltpu.SemaphoreType.DMA],
        compiler_params=pltpu.CompilerParams(vmem_limit_bytes=60 * MIB),
    )(here, features)


def cut_rest_kernel(here_ref, features, half_ref, edge_ref, sems):
    here = here_ref[0]
    half, margin = half_ref.shape[0], edge_ref.shape[0]
    copies = []
    for index, (start, target) in enumerate(
        [((1 - here) * half, half_ref), (here * (2 * half - margin), edge_ref)]
    ):
        rows = pl.ds(pl.multiple_of(start, TILE), target.shape[0])
        copies.append(pltpu.make_async_copy(features.at[rows], target, sems.at[index]))
    for copy in copies:
        copy.start()
    for copy in copies:
        copy.wait()


def cut_rest(here, features, margin):
    rows, width = features.shape
    return pl.pallas_call(
        cut_rest_kernel,
        in_specs=[SMEM, ANY],
        out_specs=[VMEM] * 2,
        out_shape=[
            jax.ShapeDtypeStruct((rows // 2, width), jnp.bfloat16),
            jax.ShapeDtypeStruct((margin, width), jnp.bfloat16),
        ],
        scratch_shapes=[pltpu.SemaphoreType.DMA((2,))],
        compiler_params=pltpu.CompilerParams(vmem_limit_bytes=8 * MIB),
        cost_estimate=pl.CostEstimate(flops=10**11, bytes_accessed=4096, transcendentals=0),
    )(here, features)


def select_kernel(jobs, share, sources, margin, place_ref, *refs):
    matchings = len(refs) - sources - len(jobs) - (margin > 0)
    wanted = refs[:matchings]
    parts = refs[matchings : matchings + sources]
    outs = refs[matchings + sources :]
    here = place_ref[0]
    even = lax.rem(place_ref[1], 2) == 0
    quarter = parts[1].shape[0] // TILE
    if margin:
        start = pl.multiple_of((1 - here) * (quarter * TILE - margin), TILE)
        outs[-1][...] = parts[1][pl.ds(start, margin), :]
    per_part = 2 * quarter
    flat = []
    for (of_even, of_odd, lines), out in zip(jobs, outs):
        at = 0
        for line in lines:
            start = (here if line == 0 else 1 - here) * share
            for slot in range(share):
                tile = wanted[of_even][0, start + slot]
                if of_odd != of_even:
                    tile = jnp.where(even, tile, wanted[of_odd][0, start + slot])
                flat.append((tile, out, at))
                at += 1
    for tile, out, slot in flat:
        own = tile // per_part == here
        place = tile // quarter
        end = jnp.logical_or(place == 0, place == 3)
        target = slice(slot * TILE, (slot + 1) * TILE)

        @pl.when(own)
        def _():
            start = pl.multiple_of(lax.rem(tile, per_part) * TILE, TILE)
            out[target, :] = parts[0][pl.ds(start, TILE), :]

        start = pl.multiple_of(lax.rem(tile, quarter) * TILE, TILE)

        @pl.when(jnp.logical_and(jnp.logical_not(own), end))
        def _():
            out[target, :] = parts[1][pl.ds(start, TILE), :]

        if sources > 2:

            @pl.when(jnp.logical_not(jnp.logical_or(own, end)))
            def _():
                out[target, :] = parts[2][pl.ds(start, TILE), :]


def select(place, jobs, share, wanted, parts, margin=0):
    width = parts[0].shape[1]
    sizes = [share * len(lines) * TILE for _, _, lines in jobs]
    sizes += [margin] * (margin > 0)
    return pl.pallas_call(
        functools.partial(select_kernel, jobs, share, len(parts), margin),
        in_specs=[SMEM] * (1 + len(wanted)) + [VMEM] * len(parts),
        out_specs=[VMEM] * len(sizes),
        out_shape=[jax.ShapeDtypeStruct((size, width), jnp.bfloat16) for size in sizes],
        compiler_params=pltpu.CompilerParams(vmem_limit_bytes=16 * MIB),
        cost_estimate=pl.CostEstimate(flops=1000, bytes_accessed=1000, transcendentals=0),
    )(place, *wanted, *parts)


def rank_tiles(tiles, edges, column_of, mark, on_tile):
    every = range(mark.shape[0])
    quarter = tiles // 4
    for tile in range(tiles):
        for matching in every:
            mark[matching, tile] = 0
    missing = [jnp.int32(edges)] * len(every)
    for edge in range(edges):
        for matching in every:
            tile = column_of(matching, edge)
            missing[matching] = missing[matching] - (1 - mark[matching, tile])
            mark[matching, tile] = 1
    rank = [jnp.int32(0)] * len(every)
    for at in range(tiles):
        tile = at + (quarter if at // quarter % 2 == 0 else -quarter)
        for matching in every:
            present = mark[matching, tile]
            added = jnp.where(jnp.logical_and(present == 0, missing[matching] > 0), 1, 0)
            on_tile(matching, tile, rank[matching])
            rank[matching] = rank[matching] + present + added
            missing[matching] = missing[matching] - added


def spots_kernel(tiles, lines, blocks, here_ref, block_ref, cols_ref, *refs):
    (place_ref, own_ref, near_table, rest_table) = refs[:4]
    spots_refs = refs[4:7]
    wanted_refs = refs[7:-2]
    mark, rank_of = refs[-2:]
    matchings, edges = cols_ref.shape
    share = edges // lines
    here, block = here_ref[0], block_ref[0]
    odd = lax.rem(block, 2)
    place_ref[0] = here
    place_ref[1] = block
    per_part = tiles // lines
    quarter = per_part // 2
    for index in range(tiles + 2 * HT):
        column = index - HT
        if 0 <= column < tiles:
            own = here == column // per_part
            own_place = jnp.where(own, column % per_part, -1)
            within = column % quarter
            end = column // quarter in (0, 3)
            near = jnp.where(own, -1, per_part + within if end else -1)
            rest = jnp.where(own, -1, -1 if end else within)
        else:
            after = column >= tiles
            own_place = near = jnp.int32(-1)
            ours = here == (0 if after else 1)
            rest = (column - tiles if after else column + HT) + jnp.where(ours, quarter + HT, quarter)
            rest = jnp.where(block < blocks - 1 if after else block > 0, rest, -1)
        own_ref[0, index] = own_place
        own_ref[1, index] = -1
        near_table[0, index] = near
        near_table[1, index] = jnp.maximum(near, own_place)
        rest_table[0, index] = rest
        rest_table[1, index] = rest

    def on_tile(matching, tile, slot):
        rank_of[matching, tile] = slot
        wanted_refs[matching][0, slot] = tile

    rank_tiles(tiles, edges, lambda matching, edge: cols_ref[matching, edge], mark, on_tile)
    for edge in range(edges):
        for matching in range(matchings):
            slot = rank_of[matching, cols_ref[matching, edge]]
            away = jnp.where(slot // share == here, 0, 1)
            within = lax.rem(slot, share)
            if matching == 0:
                when, spot = 0, away * share + within
            elif matching == 1:
                when, spot = away, within + jnp.where(away == 0, 3 * share, 0)
            else:
                second = odd if matching == matchings - 1 else 1 - odd
                when = jnp.where(away == 0, second, 1 + second)
                spot = within + share * jnp.where(second == 0, 2, jnp.where(away == 0, 1, odd))
            for index, spots_ref in enumerate(spots_refs):
                spots_ref[matching, edge] = jnp.where(when == index, spot, -1)


def arrival_spots(here, block, blocks, cols, tiles, lines):
    wanted = jax.ShapeDtypeStruct((1, 2 * cols.shape[1]), jnp.int32)
    spots = jax.ShapeDtypeStruct(cols.shape, jnp.int32)
    table = jax.ShapeDtypeStruct((2, tiles + 2 * HT), jnp.int32)
    place = jax.ShapeDtypeStruct((2,), jnp.int32)
    place, *rest = pl.pallas_call(
        functools.partial(spots_kernel, tiles, lines, blocks),
        in_specs=[SMEM] * 3,
        out_specs=[SMEM] * (7 + cols.shape[0]),
        out_shape=[place] + [table] * 3 + [spots] * 3 + [wanted] * cols.shape[0],
        scratch_shapes=[pltpu.SMEM((cols.shape[0], tiles), jnp.int32)] * 2,
        compiler_params=pltpu.CompilerParams(vmem_limit_bytes=8 * MIB),
        cost_estimate=pl.CostEstimate(flops=10**11, bytes_accessed=4096, transcendentals=0),
    )(here, block, cols)
    return place, rest[:3], rest[3:6], rest[6:]


def local(features, w_query, w_key_value, edge_local, edge_expand, local_cols, exp_rows, exp_cols):
    groups = lax.axis_size("head")
    blocks = lax.axis_size("node")
    own_rows, width = features.shape
    here = lax.axis_index("head")
    block = lax.axis_index("node")
    edges = exp_cols.shape[2]
    tiles = local_cols.shape[0]
    own_tiles = own_rows // TILE
    margin = HT * TILE
    exp_rows, exp_cols = exp_rows[0], exp_cols[0]
    log_count = blocks.bit_length() - 1
    flips = [1 << matching * log_count // MATCH for matching in range(MATCH)]

    def swap(x, matching, of_odd=None):
        flip = [flips[matching], flips[matching if of_odd is None else of_odd]]
        return lax.ppermute(x, "node", [(i, i ^ flip[i % 2]) for i in range(blocks)])

    def other(x):
        return lax.ppermute(x, "head", [(0, 1), (1, 0)])

    scales = jnp.stack([edge_local, edge_expand])
    listed = local_cols.shape[1]
    split = own_tiles
    two = groups == 2 and min(flips[2:]) > 1

    if two:
        split = own_tiles // 4
        here_array = jnp.reshape(here, (1,)).astype(jnp.int32)
        block_array = jnp.reshape(block, (1,)).astype(jnp.int32)
        first_half = cut_half(here_array, features)
        beside = other(scales)
        first_half, features, exp_cols, local_cols, beside, w_query, w_key_value = (
            lax.optimization_barrier(
                (first_half, features, exp_cols, local_cols, beside, w_query, w_key_value)
            )
        )
        local_cols = local_cols.reshape(-1)
        w = jnp.transpose(w_key_value, (1, 0, 2))
        first_half = other(first_half)
        second_half, edge_rows = cut_rest(here_array, features, margin)
        place, tables, spots, wanted = arrival_spots(
            here_array, block_array, blocks, exp_cols, tiles, groups
        )
        edge_rows, *wanted = lax.optimization_barrier((edge_rows, *wanted))
        wanted_pair, *wanted = wanted
        wanted = [swap(wanted[m - 1], m) for m in range(1, MATCH)]
        inward = [(2 * i, 2 * i - 2) for i in range(1, blocks)]
        inward += [(2 * i + 1, 2 * i + 3) for i in range(blocks - 1)]
        halo = lax.ppermute(edge_rows, ("node", "head"), inward)
        scales = jnp.where(
            here == 0,
            jnp.concatenate([scales, beside], axis=1),
            jnp.concatenate([beside, scales], axis=1),
        )
        scales, w, local_cols, halo, *wanted = lax.optimization_barrier(
            (scales, w, local_cols, halo, *wanted)
        )
        num, den, keys, values, local_q, expand_q = own_attention(
            (place, local_cols, tables[0]), features, w, w_query, scales, split, listed
        )
        first_half, second_half, num = lax.optimization_barrier((first_half, second_half, num))
        second_half = other(second_half)
        share = edges // groups
        sources = [features, first_half]
        jobs = ((2, 1, (0,)), (1, 2, (0,)), (0, 0, (0,)))
        *chosen, edge_rows = select(place, jobs, share, wanted, sources, margin)
        num, *chosen = lax.optimization_barrier((num, *chosen))
        first = swap(chosen[0], 3, 2)
        early = swap(chosen[2], 1)
        num, den = more_attention(
            (place, local_cols, tables[1]),
            [first_half],
            w,
            local_q,
            num,
            den,
            (keys, values),
            split,
            listed,
        )
        second_half, num, den, edge_rows, wanted_pair, second = lax.optimization_barrier(
            (second_half, num, den, edge_rows, wanted_pair, chosen[1])
        )
        outward = [(2 * i, 2 * i + 2) for i in range(blocks - 1)]
        outward += [(2 * i + 1, 2 * i - 1) for i in range(1, blocks)]
        other_halo = lax.ppermute(edge_rows, ("node", "head"), outward)
        wanted_pair = swap(wanted_pair, 0)
        sources = [features, first_half, second_half]
        late, direct = select(place, ((0, 0, (1,)), (1, 1, (1,))), share, wanted, sources)
        num, first, early, late = lax.optimization_barrier((num, first, early, late))
        second = swap(second, 2, 3)
        first_beside = other(first)
        late = swap(late, 1)
        (pair,) = select(place, ((0, 0, (0, 1)),), share, [wanted_pair], sources)
        num, pair, other_halo = lax.optimization_barrier((num, pair, other_halo))
        pair = swap(pair, 0)
        num, den = more_attention(
            (place, local_cols, tables[2]),
            [second_half, other_halo, halo],
            w,
            local_q,
            num,
            den,
            (),
            split,
            listed,
        )
        num, den = expand_attention(
            place, exp_rows, spots[0], [pair, first, early], expand_q, num, den, w, False, None
        )
        second, direct, num, den = lax.optimization_barrier((second, direct, num, den))
        direct = lax.ppermute(direct, "node", [(i, i ^ flips[2]) for i in range(0, blocks, 2)])
        sides = [(4 * i + 2 + side, 4 * i + 3 - side) for i in range(blocks // 2) for side in (0, 1)]
        second_beside = lax.ppermute(second, ("node", "head"), sides)
        sources = [None, [late, second, first_beside], [direct, second_beside]]
    else:
        place = jnp.stack([here, block]).astype(jnp.int32)
        column = jnp.arange(tiles + 2 * HT, dtype=jnp.int32) - HT
        usable = block * tiles + column
        usable = jnp.logical_and(usable >= 0, usable < blocks * tiles)
        own = column // own_tiles == here
        w = jnp.transpose(w_key_value, (1, 0, 2))
        gather = lambda x: lax.all_gather(x, "head", axis=0, tiled=True)
        scales = lax.all_gather(scales, "head", axis=1, tiled=True)
        full = gather(features)
        before = lax.ppermute(full[-margin:], "node", [(i, i + 1) for i in range(blocks - 1)])
        after = lax.ppermute(full[:margin], "node", [(i + 1, i) for i in range(blocks - 1)])
        received = [gather(swap(features, m)) for m in range(MATCH)]
        sources = [None, received[:2], received[2:]]
        matching = jnp.arange(MATCH, dtype=jnp.int32)[:, None]
        spots = [
            None,
            jnp.where(matching < 2, matching * tiles + exp_cols, -1),
            jnp.where(matching < 2, -1, (matching - 2) * tiles + exp_cols),
        ]
        where_own = jnp.where(own, column - here * own_tiles, -1)
        where_rest = jnp.where(jnp.logical_and(usable, jnp.logical_not(own)), column + HT, -1)
        local_cols = local_cols.reshape(-1)
        num, den, keys, values, local_q, expand_q = own_attention(
            (place, local_cols, jnp.stack([where_own] * 2)),
            features,
            w,
            w_query,
            scales,
            split,
            listed,
        )
        num, den = more_attention(
            (place, local_cols, jnp.stack([where_rest] * 2)),
            [before, full, after],
            w,
            local_q,
            num,
            den,
            (),
            split,
            listed,
        )
    num, den, out = expand_attention(
        place, exp_rows, spots[1], sources[1], expand_q, num, den, w, True, None
    )
    return expand_attention(
        place, exp_rows, spots[2], sources[2], expand_q, num, den, w, True, out
    )


def solution(mesh):
    return jax.shard_map(
        local,
        mesh=mesh,
        in_specs=(
            P(("node", "head"), None),
            P(),
            P(),
            P("head"),
            P("head"),
            P("node", None),
            P("node", None, None),
            P("node", None, None),
        ),
        out_specs=P(("node", "head"), None),
        check_vma=False,
    )
```

time: 150 us -> 119 us (0.79)
  local copies, waits for them, and re-layouts: 17.9 us -> 1.63 us
  starting transfers between devices: 30.4 us -> 25.4 us
  waiting for transfers between devices: 13.3 us -> 8.82 us
  Pallas kernels: 84.1 us -> 80.1 us
    unnamed x65 -> x30, local copies, waits for them, and re-layouts: 16.5 us -> 0.07 us
    ppermute x10 -> x9, starting transfers between devices: 18 us -> 6.95 us  [swap(): lax.ppermute(x, 'node', [(i, i ^ flip[i % 2]) for i in range(blocks)])]
    ppermute x0 -> x2, starting transfers between devices: none -> 7.22 us  [the longest x1 6.5 us: local(): second_beside = lax.ppermute(second, ('node', 'head'), sides)]
    pallas_call x7 -> x9, Pallas kernels: 79 us -> 72.8 us  [the longest x2 31.7 us: more_attention(): pl.pallas_call(functools.partial(more_kernel, len(pieces), bool(own), spl...]
    ppermute x5 -> x4, waiting for transfers between devices: 4.37 us -> 1.2 us  [other(): return lax.ppermute(x, 'head', [(0, 1), (1, 0)])]
    pallas_call x2 -> x3, Pallas kernels: 5.17 us -> 7.37 us  [select(): pl.pallas_call(functools.partial(select_kernel, jobs, share, len(parts),...]
    ppermute x10 -> x9, waiting for transfers between devices: 8.61 us -> 6.88 us  [swap(): lax.ppermute(x, 'node', [(i, i ^ flip[i % 2]) for i in range(blocks)])]
    ppermute x1, starting transfers between devices: 4.8 us -> 3.2 us  [local(): other_halo = lax.ppermute(edge_rows, ('node', 'head'), outward)]
  transfers between devices with their start and end apart: 17 -> 17, of which waited for: 9 -> 7; matrix products, arithmetic and copies ran while one was open for 1% -> 1% of each run, Pallas kernels for 51% -> 62%
where the time goes in v3:
time: 119 us; the launch traced here: 117 us
  Pallas kernels  80.1 us (67%)
  starting transfers between devices  25.4 us (21%)
  waiting for transfers between devices  8.82 us (7%)
  local copies, waits for them, and re-layouts  1.63 us (1%)
    pallas_call x2, Pallas kernels, more_attention(): pl.pallas_call(functools.partial(more_kernel, len(pieces), bool(own), spl...  31.7 us
    pallas_call x3, Pallas kernels, expand_attention(): pl.pallas_call(functools.partial(expand_kernel, len(sources), gives_out,...  26.2 us
    pallas_call x1, Pallas kernels, own_attention(): pl.pallas_call(functools.partial(own_kernel, split), in_specs=[SMEM] * 3...  8.85 us
    pallas_call x3, Pallas kernels, select(): pl.pallas_call(functools.partial(select_kernel, jobs, share, len(parts),...  7.37 us
    ppermute x9, starting transfers between devices, swap(): lax.ppermute(x, 'node', [(i, i ^ flip[i % 2]) for i in range(blocks)])  6.95 us
    ppermute x9, waiting for transfers between devices, swap(): lax.ppermute(x, 'node', [(i, i ^ flip[i % 2]) for i in range(blocks)])  6.88 us
    ppermute x1, starting transfers between devices, local(): second_beside = lax.ppermute(second, ('node', 'head'), sides)  6.5 us
    ppermute x1, starting transfers between devices, local(): halo = lax.ppermute(edge_rows, ('node', 'head'), inward)  4.05 us
  transfers between devices with their start and end apart: 17, of which 7 were waited for; matrix products, arithmetic and copies ran while one was open for 1% of the time, Pallas kernels for 62%

profile of v3, /device:TPU:25, one launch (start us, length us, event | category | flops | bytes accessed | tf_op | source)
XLA Modules:
  0.0 117.4 jit_solution(1306570636522345197)
XLA Ops:
  0.0 0.9 pad_maximum_fusion
  0.9 1.2 %collective-permute-start = (f32[2,256]{1,0:T(2,128)S(1)}, f32[2,256]{1,0:T(2,128)S(1)}, u32[]{:S(2)}, u32[]{:S(2)}) collective-permute-start(f32[2,256]{1,0:T(2,128)S(1)} %pad_maximum_fusion), channel_id=1, source_target_pairs={{0,1},{1,0},{2,3},{3,2},{4,5},{5,4},{6,7},{7,6},{8,9},{9,8},{10,11... | collective-permute-start | bytes 6152 | tf_op jit(solution)/shard_map/ppermute | solution.py:696
  2.1 2.2 %shard_map.82 = bf16[1024,512]{1,0:T(8,128)(2,1)} custom-call(s32[1]{0:T(128)} %bitcast.here_ref, bf16[2048,512]{1,0:T(8,128)(2,1)} %refs_1_), custom_call_target="tpu_custom_call" | custom-call | tf_op jit(solution)/shard_map/pallas_call | solution.py:478
  4.3 0.3 collective-permute-start.1
  4.6 1.1 shard_map.84
  5.8 2.7 %shard_map.83 = (s32[2]{0:T(128)S(1)}, s32[2,36]{1,0:T(2,128)S(1)}, s32[2,36]{1,0:T(2,128)S(1)}, s32[2,36]{1,0:T(2,128)S(1)}, s32[4,16]{1,0:T(4,128)S(1)}, /*ind...) custom-call(s32[1]{0:T(128)} %bitcast.here_ref, ...), custom_call_target="tpu_custom_call" | custom-call | flops 99999997952 | bytes 4096 | tf_op jit(solution)/shard_map/pallas_call | solution.py:665
  8.5 4.1 %collective-permute-start.2 = (bf16[256,512]{1,0:T(8,128)(2,1)S(1)}, bf16[256,512]{1,0:T(8,128)(2,1)S(1)}, u32[]{:S(2)}, u32[]{:S(2)}) collective-permute-start(bf16[256,512]{1,0:T(8,128)(2,1)S(1)} %get-tuple-element.96), channel_id=1, source_target_pairs={{2,0},{4,2},{6,4},{8,6},{10,8},{12,10},{14,12},{16,14},{18,16},{20... | collective-permute-start | bytes 786440 | tf_op jit(solution)/shard_map/ppermute | solution.py:726
  12.8 1.4 %copy.14 = bf16[512,2,512]{2,0,1:T(8,128)(2,1)S(1)} copy(bf16[512,2,512]{2,1,0:T(2,128)(2,1)} %param.10) | data formatting | bytes 2097152 | tf_op jit(solution)/shard_map/optimization_barrier | solution.py:710
  14.2 1.3 %collective-permute-start.3 = (s32[1,32]{1,0:T(1,128)S(1)}, s32[1,32]{1,0:T(1,128)S(1)}, u32[]{:S(2)}, u32[]{:S(2)}) collective-permute-start(s32[1,32]{1,0:T(1,128)S(1)} %get-tuple-element.97), channel_id=1, source_target_pairs={{0,4},{2,6},{4,0},{6,2},{8,12},{10,14},{12,8},{14,10},{16,20},{18,... | collective-permute-start | bytes 392 | tf_op jit(solution)/shard_map/ppermute | solution.py:693
  15.8 1.3 %collective-permute-done.3.refs_0_ = s32[1,32]{1,0:T(1,128)S(1)} collective-permute-done((s32[1,32]{1,0:T(1,128)S(1)}, s32[1,32]{1,0:T(1,128)S(1)}, u32[]{:S(2)}, u32[]{:S(2)}) %collective-permute-start.3) | collective-permute-done | bytes 160 | tf_op jit(solution)/shard_map/ppermute | solution.py:693
  17.1 1.2 collective-permute-done.4.refs_1_
  18.3 0.7 collective-permute-done.5.refs_2_
  19.0 8.9 %shard_map.85 = (f32[2176,512]{1,0:T(8,128)S(1)}, f32[2176,128]{1,0:T(8,128)S(1)}, bf16[16,512,128]{2,1,0:T(8,128)(2,1)S(1)}, bf16[16,128,512]{2,1,0:T(8,128)(2,...) custom-call(s32[2]{0:T(128)S(1)} %get-tuple-element.83.place_ref, s32[256]{0:T(256)S(1)} %reshape.11.cols_ref, ...), custom_call_target="tpu_custom_call" | custom-call | flops 100000000 | bytes 100000 | tf_op jit(solution)/shard_map/pallas_call | solution.py:293
  27.9 0.6 collective-permute-done.1.refs_4_.refs_0_.refs_2_
  28.4 2.5 %collective-permute-start.6 = (bf16[1024,512]{1,0:T(8,128)(2,1)}, bf16[1024,512]{1,0:T(8,128)(2,1)}, u32[]{:S(2)}, u32[]{:S(2)}) collective-permute-start(bf16[1024,512]{1,0:T(8,128)(2,1)} %get-tuple-element.106), channel_id=1, source_target_pairs={{0,1},{1,0},{2,3},{3,2},{4,5},{5,4},{6,7},{7,6},{8,9},{9,8},{10,11... | collective-permute-start | bytes 3145736 | tf_op jit(solution)/shard_map/ppermute | solution.py:696
  30.9 3.3 %shard_map.86 = (bf16[1024,512]{1,0:T(8,128)(2,1)}, bf16[1024,512]{1,0:T(8,128)(2,1)S(1)}, bf16[1024,512]{1,0:T(8,128)(2,1)}, bf16[256,512]{1,0:T(8,128)(2,1)S(1)}) custom-call(s32[2]{0:T(128)S(1)} %get-tuple-element.83.place_ref, s32[1,32]{1,0:T(1,128)S(1)} %collective-permute-done.3.refs_0_, s32[1,32]{1,0:T(1,128)S(1)} %collective-permute-done.4.refs_1_, ...), custom_call_target="tpu_custom_call" | custom-call | flops 1000 | bytes 1000 | tf_op jit(solution)/shard_map/pallas_call | solution.py:570
  34.6 18.9 %shard_map.87 = (f32[2176,512]{1,0:T(8,128)S(1)}, f32[2176,128]{1,0:T(8,128)S(1)}) custom-call(s32[2]{0:T(128)S(1)} %get-tuple-element.83.place_ref, s32[256]{0:T(256)S(1)} %reshape.11.cols_ref, s32[2,36]{1,0:T(2,128)S(1)} %get-tuple-element.107.where_ref, bf16[1024,512]{1,0:T(8,128)(2,1)} %collective-permute-done.1.refs_4_.refs_0_.refs_2_, ...), custom_call_target="tpu_custom_call" | custom-call | flops 999999995904 | bytes 100000 | tf_op jit(solution)/shard_map/pallas_call | solution.py:308
  53.5 0.6 collective-permute-done.6.refs_5_.refs_3_.refs_0_
  54.1 3.2 %collective-permute-start.11 = (bf16[256,512]{1,0:T(8,128)(2,1)S(1)}, bf16[256,512]{1,0:T(8,128)(2,1)S(1)}, u32[]{:S(2)}, u32[]{:S(2)}) collective-permute-start(bf16[256,512]{1,0:T(8,128)(2,1)S(1)} %get-tuple-element.136), channel_id=1, source_target_pairs={{0,2},{2,4},{4,6},{6,8},{8,10},{10,12},{12,14},{14,16},{16,18},{18... | collective-permute-start | bytes 786440 | tf_op jit(solution)/shard_map/ppermute | solution.py:763
  57.4 2.0 %shard_map.88 = (bf16[1024,512]{1,0:T(8,128)(2,1)S(1)}, bf16[1024,512]{1,0:T(8,128)(2,1)S(1)}) custom-call(s32[2]{0:T(128)S(1)} %get-tuple-element.83.place_ref, s32[1,32]{1,0:T(1,128)S(1)} %copy-done.4, s32[1,32]{1,0:T(1,128)S(1)} %copy-done.6, s32[1,32]{1,0:T(1,128)S(1)} %copy-done.8, bf16[2048,512]{1,0:T(8,128)(2,1)S(1)} %copy-done, ...), custom_call_target="tpu_custom_call" | custom-call | flops 1000 | bytes 1000 | tf_op jit(solution)/shard_map/pallas_call | solution.py:570
  59.5 2.0 %shard_map.89 = bf16[2048,512]{1,0:T(8,128)(2,1)S(1)} custom-call(s32[2]{0:T(128)S(1)} %get-tuple-element.83.place_ref, s32[1,32]{1,0:T(1,128)S(1)} %collective-permute-done.10.refs_0_, bf16[2048,512]{1,0:T(8,128)(2,1)S(1)} %copy-done, bf16[1024,512]{1,0:T(8,128)(2,1)} %collective-permute-done.1.refs_4_.refs_0_.refs_2_, ...), custom_call_target="tpu_custom_call" | custom-call | flops 1000 | bytes 1000 | tf_op jit(solution)/shard_map/pallas_call | solution.py:570
  61.5 3.6 %collective-permute-start.12 = (bf16[2048,512]{1,0:T(8,128)(2,1)S(1)}, bf16[2048,512]{1,0:T(8,128)(2,1)S(1)}, u32[]{:S(2)}, u32[]{:S(2)}) collective-permute-start(bf16[2048,512]{1,0:T(8,128)(2,1)S(1)} %shard_map.89), channel_id=1, source_target_pairs={{0,2},{2,0},{4,6},{6,4},{8,10},{10,8},{12,14},{14,12},{16,18},{18,... | collective-permute-start | bytes 6291464 | tf_op jit(solution)/shard_map/ppermute | solution.py:693
  65.1 0.7 collective-permute-start.7
  65.8 0.7 collective-permute-start.15
  66.5 12.8 %shard_map.90 = (f32[2176,512]{1,0:T(8,128)S(1)}, f32[2176,128]{1,0:T(8,128)S(1)}) custom-call(s32[2]{0:T(128)S(1)} %get-tuple-element.83.place_ref, s32[256]{0:T(256)S(1)} %reshape.11.cols_ref, s32[2,36]{1,0:T(2,128)S(1)} %get-tuple-element.141.where_ref, bf16[1024,512]{1,0:T(8,128)(2,1)} %collective-permute-done.6.refs_5_.refs_3_.refs_0_, ...), custom_call_target="tpu_custom_call" | custom-call | flops 100000000 | bytes 100000 | tf_op jit(solution)/shard_map/pallas_call | solution.py:308
  79.4 7.9 %shard_map.91 = (f32[2176,512]{1,0:T(8,128)S(1)}, f32[2176,128]{1,0:T(8,128)S(1)}) custom-call(s32[2]{0:T(128)S(1)} %get-tuple-element.83.place_ref, s32[4,16]{1,0:T(4,128)S(1)} %bitcast.15, s32[4,16]{1,0:T(4,128)S(1)} %get-tuple-element.129.spots_ref, bf16[2048,512]{1,0:T(8,128)(2,1)S(1)} %collective-permute-done.12.refs_0_, ...), custom_call_target="tpu_custom_call" | custom-call | flops 268435456 | bytes 1048576 | tf_op jit(solution)/shard_map/pallas_call | solution.py:432
  87.3 3.6 %collective-permute-done.7.refs_1_ = bf16[1024,512]{1,0:T(8,128)(2,1)S(1)} collective-permute-done((bf16[1024,512]{1,0:T(8,128)(2,1)S(1)}, bf16[1024,512]{1,0:T(8,128)(2,1)S(1)}, u32[]{:S(2)}, u32[]{:S(2)}) %collective-permute-start.7) | collective-permute-done | bytes 1048608 | tf_op jit(solution)/shard_map/ppermute | solution.py:693
  90.9 0.7 collective-permute-start.13
  91.6 6.5 %collective-permute-start.14 = (bf16[1024,512]{1,0:T(8,128)(2,1)S(1)}, bf16[1024,512]{1,0:T(8,128)(2,1)S(1)}, u32[]{:S(2)}, u32[]{:S(2)}) collective-permute-start(bf16[1024,512]{1,0:T(8,128)(2,1)S(1)} %collective-permute-done.7.refs_1_), channel_id=1, source_target_pairs={{2,3},{3,2},{6,7},{7,6},{10,11},{11,10},{14,15},{15,14},{18,19},{1... | collective-permute-start | bytes 3145736 | tf_op jit(solution)/shard_map/ppermute | solution.py:791
  98.2 11.4 %shard_map.92 = (f32[2176,512]{1,0:T(8,128)S(1)}, f32[2176,128]{1,0:T(8,128)S(1)}, bf16[2048,512]{1,0:T(8,128)(2,1)}) custom-call(s32[2]{0:T(128)S(1)} %get-tuple-element.83.place_ref, s32[4,16]{1,0:T(4,128)S(1)} %bitcast.16, s32[4,16]{1,0:T(4,128)S(1)} %get-tuple-element.152.spots_ref, bf16[1024,512]{1,0:T(8,128)(2,1)S(1)} %collective-permute-done.15.refs_0_, ...), custom_call_target="tpu_custom_call" | custom-call | flops 268435456 | bytes 1048576 | tf_op jit(solution)/shard_map/pallas_call | solution.py:432
  109.6 0.7 collective-permute-done.14.refs_1_
  110.3 6.9 %shard_map.93 = bf16[2048,512]{1,0:T(8,128)(2,1)} custom-call(s32[2]{0:T(128)S(1)} %get-tuple-element.83.place_ref, s32[4,16]{1,0:T(4,128)S(1)} %bitcast.17, s32[4,16]{1,0:T(4,128)S(1)} %get-tuple-element.84.spots_ref, bf16[1024,512]{1,0:T(8,128)(2,1)S(1)} %collective-permute-done.13.refs_0_, ...), custom_call_target="tpu_custom_call", output_to_operand_aliasing={{}: (9, {})} | custom-call | flops 268435456 | bytes 1048576 | tf_op jit(solution)/shard_map/pallas_call | solution.py:432
  (49 shorter events, 1.0 us)
Async XLA Ops:
  0.0 4.6 %copy-start = (bf16[2048,512]{1,0:T(8,128)(2,1)S(1)}, bf16[2048,512]{1,0:T(8,128)(2,1)}, u32[]{:S(2)}) copy-start(bf16[2048,512]{1,0:T(8,128)(2,1)} %refs_1_) | copy-start | bytes 6291460
  0.9 3.5 %collective-permute-start = (f32[2,256]{1,0:T(2,128)S(1)}, f32[2,256]{1,0:T(2,128)S(1)}, u32[]{:S(2)}, u32[]{:S(2)}) collective-permute-start(f32[2,256]{1,0:T(2,128)S(1)} %pad_maximum_fusion), channel_id=1, source_target_pairs={{0,1},{1,0},{2,3},{3,2},{4,5},{5,4},{6,7},{7,6},{8,9},{9,8},{10,11... | collective-permute-start | bytes 6152 | tf_op jit(solution)/shard_map/ppermute | solution.py:696
  4.3 1.4 %copy-start.13 = (f32[2,256]{1,0:T(2,128)}, f32[2,256]{1,0:T(2,128)S(1)}, u32[]{:S(2)}) copy-start(f32[2,256]{1,0:T(2,128)S(1)} %collective-permute-done) | copy-start | bytes 6148
  4.3 1.4 %copy-start.9 = (s32[1,4,16]{2,1,0:T(4,128)S(1)}, s32[1,4,16]{2,1,0:T(4,128)}, u32[]{:S(2)}) copy-start(s32[1,4,16]{2,1,0:T(4,128)} %param.15) | copy-start | bytes 772
  4.3 24.1 %collective-permute-start.1 = (bf16[1024,512]{1,0:T(8,128)(2,1)}, bf16[1024,512]{1,0:T(8,128)(2,1)}, u32[]{:S(2)}, u32[]{:S(2)}) collective-permute-start(bf16[1024,512]{1,0:T(8,128)(2,1)} %shard_map.82), channel_id=1, source_target_pairs={{0,1},{1,0},{2,3},{3,2},{4,5},{5,4},{6,7},{7,6},{8,9},{9,8},{10,11... | collective-permute-start | bytes 3145736 | tf_op jit(solution)/shard_map/ppermute | solution.py:696
  5.7 6.9 %copy-start.10 = (s32[32,8]{0,1:T(8,128)S(1)}, s32[32,8]{0,1:T(8,128)}, u32[]{:S(2)}) copy-start(s32[32,8]{0,1:T(8,128)} %param.13) | copy-start | bytes 3076
  8.5 7.1 %copy-start.11 = (f32[256]{0:T(256)S(1)}, f32[256]{0:T(256)}, u32[]{:S(2)}) copy-start(f32[256]{0:T(256)} %param.12) | copy-start | bytes 3076
  8.5 7.1 %copy-start.12 = (f32[256]{0:T(256)S(1)}, f32[256]{0:T(256)}, u32[]{:S(2)}) copy-start(f32[256]{0:T(256)} %param.11) | copy-start | bytes 3076
  8.5 7.1 %copy-start.14 = (f32[2,256]{1,0:T(2,128)S(1)}, f32[2,256]{1,0:T(2,128)}, u32[]{:S(2)}) copy-start(f32[2,256]{1,0:T(2,128)} %copy-done.13) | copy-start | bytes 6148
  8.5 10.5 %copy-start.1 = (bf16[512,512]{1,0:T(8,128)(2,1)S(1)}, bf16[512,512]{1,0:T(8,128)(2,1)}, u32[]{:S(2)}) copy-start(bf16[512,512]{1,0:T(8,128)(2,1)} %wq) | copy-start | bytes 1572868
  8.5 10.5 %collective-permute-start.2 = (bf16[256,512]{1,0:T(8,128)(2,1)S(1)}, bf16[256,512]{1,0:T(8,128)(2,1)S(1)}, u32[]{:S(2)}, u32[]{:S(2)}) collective-permute-start(bf16[256,512]{1,0:T(8,128)(2,1)S(1)} %get-tuple-element.96), channel_id=1, source_target_pairs={{2,0},{4,2},{6,4},{8,6},{10,8},{12,10},{14,12},{16,14},{18,16},{20... | collective-permute-start | bytes 786440 | tf_op jit(solution)/shard_map/ppermute | solution.py:726
  14.2 2.9 %collective-permute-start.3 = (s32[1,32]{1,0:T(1,128)S(1)}, s32[1,32]{1,0:T(1,128)S(1)}, u32[]{:S(2)}, u32[]{:S(2)}) collective-permute-start(s32[1,32]{1,0:T(1,128)S(1)} %get-tuple-element.97), channel_id=1, source_target_pairs={{0,4},{2,6},{4,0},{6,2},{8,12},{10,14},{12,8},{14,10},{16,20},{18,... | collective-permute-start | bytes 392 | tf_op jit(solution)/shard_map/ppermute | solution.py:693
  15.5 2.8 %collective-permute-start.4 = (s32[1,32]{1,0:T(1,128)S(1)}, s32[1,32]{1,0:T(1,128)S(1)}, u32[]{:S(2)}, u32[]{:S(2)}) collective-permute-start(s32[1,32]{1,0:T(1,128)S(1)} %get-tuple-element.98), channel_id=1, source_target_pairs={{0,8},{2,10},{4,12},{6,14},{8,0},{10,2},{12,4},{14,6},{16,24},{18,... | collective-permute-start | bytes 392 | tf_op jit(solution)/shard_map/ppermute | solution.py:693
  15.6 3.4 %collective-permute-start.5 = (s32[1,32]{1,0:T(1,128)S(1)}, s32[1,32]{1,0:T(1,128)S(1)}, u32[]{:S(2)}, u32[]{:S(2)}) collective-permute-start(s32[1,32]{1,0:T(1,128)S(1)} %get-tuple-element.99), channel_id=1, source_target_pairs={{0,16},{2,18},{4,20},{6,22},{8,24},{10,26},{12,28},{14,30},{16,0},... | collective-permute-start | bytes 392 | tf_op jit(solution)/shard_map/ppermute | solution.py:693
  17.1 17.1 %copy-start.3 = (s32[1,32]{1,0:T(1,128)}, s32[1,32]{1,0:T(1,128)S(1)}, u32[]{:S(2)}) copy-start(s32[1,32]{1,0:T(1,128)S(1)} %collective-permute-done.3.refs_0_) | copy-start | bytes 388
  18.3 16.0 %copy-start.5 = (s32[1,32]{1,0:T(1,128)}, s32[1,32]{1,0:T(1,128)S(1)}, u32[]{:S(2)}) copy-start(s32[1,32]{1,0:T(1,128)S(1)} %collective-permute-done.4.refs_1_) | copy-start | bytes 388
  19.0 15.2 %copy-start.7 = (s32[1,32]{1,0:T(1,128)}, s32[1,32]{1,0:T(1,128)S(1)}, u32[]{:S(2)}) copy-start(s32[1,32]{1,0:T(1,128)S(1)} %collective-permute-done.5.refs_2_) | copy-start | bytes 388
  28.4 25.7 %collective-permute-start.6 = (bf16[1024,512]{1,0:T(8,128)(2,1)}, bf16[1024,512]{1,0:T(8,128)(2,1)}, u32[]{:S(2)}, u32[]{:S(2)}) collective-permute-start(bf16[1024,512]{1,0:T(8,128)(2,1)} %get-tuple-element.106), channel_id=1, source_target_pairs={{0,1},{1,0},{2,3},{3,2},{4,5},{5,4},{6,7},{7,6},{8,9},{9,8},{10,11... | collective-permute-start | bytes 3145736 | tf_op jit(solution)/shard_map/ppermute | solution.py:696
  34.2 25.2 %collective-permute-start.8 = (bf16[1024,512]{1,0:T(8,128)(2,1)}, bf16[1024,512]{1,0:T(8,128)(2,1)}, u32[]{:S(2)}, u32[]{:S(2)}) collective-permute-start(bf16[1024,512]{1,0:T(8,128)(2,1)} %get-tuple-element.131), channel_id=1, source_target_pairs={{0,16},{2,10},{4,20},{6,14},{8,24},{10,2},{12,28},{14,6},{16,0},{1... | collective-permute-start | bytes 3145736 | tf_op jit(solution)/shard_map/ppermute | solution.py:693
  34.3 25.2 %collective-permute-start.9 = (bf16[1024,512]{1,0:T(8,128)(2,1)}, bf16[1024,512]{1,0:T(8,128)(2,1)}, u32[]{:S(2)}, u32[]{:S(2)}) collective-permute-start(bf16[1024,512]{1,0:T(8,128)(2,1)} %get-tuple-element.132), channel_id=1, source_target_pairs={{0,4},{2,6},{4,0},{6,2},{8,12},{10,14},{12,8},{14,10},{16,20},{18,... | collective-permute-start | bytes 3145736 | tf_op jit(solution)/shard_map/ppermute | solution.py:693
  34.6 22.8 %copy-start.4 = (s32[1,32]{1,0:T(1,128)S(1)}, s32[1,32]{1,0:T(1,128)}, u32[]{:S(2)}) copy-start(s32[1,32]{1,0:T(1,128)} %copy-done.3) | copy-start | bytes 388
  34.6 22.8 %copy-start.6 = (s32[1,32]{1,0:T(1,128)S(1)}, s32[1,32]{1,0:T(1,128)}, u32[]{:S(2)}) copy-start(s32[1,32]{1,0:T(1,128)} %copy-done.5) | copy-start | bytes 388
  34.6 22.8 %copy-start.8 = (s32[1,32]{1,0:T(1,128)S(1)}, s32[1,32]{1,0:T(1,128)}, u32[]{:S(2)}) copy-start(s32[1,32]{1,0:T(1,128)} %copy-done.7) | copy-start | bytes 388
  54.1 7.4 %collective-permute-start.11 = (bf16[256,512]{1,0:T(8,128)(2,1)S(1)}, bf16[256,512]{1,0:T(8,128)(2,1)S(1)}, u32[]{:S(2)}, u32[]{:S(2)}) collective-permute-start(bf16[256,512]{1,0:T(8,128)(2,1)S(1)} %get-tuple-element.136), channel_id=1, source_target_pairs={{0,2},{2,4},{4,6},{6,8},{8,10},{10,12},{12,14},{14,16},{16,18},{18... | collective-permute-start | bytes 786440 | tf_op jit(solution)/shard_map/ppermute | solution.py:763
  57.3 2.2 %collective-permute-start.10 = (s32[1,32]{1,0:T(1,128)S(1)}, s32[1,32]{1,0:T(1,128)S(1)}, u32[]{:S(2)}, u32[]{:S(2)}) collective-permute-start(s32[1,32]{1,0:T(1,128)S(1)} %get-tuple-element.135), channel_id=1, source_target_pairs={{0,2},{2,0},{4,6},{6,4},{8,10},{10,8},{12,14},{14,12},{16,18},{18,... | collective-permute-start | bytes 392 | tf_op jit(solution)/shard_map/ppermute | solution.py:693
  61.5 17.8 %collective-permute-start.12 = (bf16[2048,512]{1,0:T(8,128)(2,1)S(1)}, bf16[2048,512]{1,0:T(8,128)(2,1)S(1)}, u32[]{:S(2)}, u32[]{:S(2)}) collective-permute-start(bf16[2048,512]{1,0:T(8,128)(2,1)S(1)} %shard_map.89), channel_id=1, source_target_pairs={{0,2},{2,0},{4,6},{6,4},{8,10},{10,8},{12,14},{14,12},{16,18},{18,... | collective-permute-start | bytes 6291464 | tf_op jit(solution)/shard_map/ppermute | solution.py:693
  65.1 25.8 %collective-permute-start.7 = (bf16[1024,512]{1,0:T(8,128)(2,1)S(1)}, bf16[1024,512]{1,0:T(8,128)(2,1)S(1)}, u32[]{:S(2)}, u32[]{:S(2)}) collective-permute-start(bf16[1024,512]{1,0:T(8,128)(2,1)S(1)} %get-tuple-element.126), channel_id=1, source_target_pairs={{0,8},{2,18},{4,12},{6,22},{8,0},{10,26},{12,4},{14,30},{16,24},{1... | collective-permute-start | bytes 3145736 | tf_op jit(solution)/shard_map/ppermute | solution.py:693
  65.8 32.3 %collective-permute-start.15 = (bf16[1024,512]{1,0:T(8,128)(2,1)S(1)}, bf16[1024,512]{1,0:T(8,128)(2,1)S(1)}, u32[]{:S(2)}, u32[]{:S(2)}) collective-permute-start(bf16[1024,512]{1,0:T(8,128)(2,1)S(1)} %get-tuple-element.153), channel_id=1, source_target_pairs={{0,4},{2,6},{4,0},{6,2},{8,12},{10,14},{12,8},{14,10},{16,20},{18,... | collective-permute-start | bytes 3145736 | tf_op jit(solution)/shard_map/ppermute | solution.py:693
  66.5 31.6 %collective-permute-start.16 = (bf16[1024,512]{1,0:T(8,128)(2,1)}, bf16[1024,512]{1,0:T(8,128)(2,1)S(1)}, u32[]{:S(2)}, u32[]{:S(2)}) collective-permute-start(bf16[1024,512]{1,0:T(8,128)(2,1)} %collective-permute-done.8.refs_1_), channel_id=1, source_target_pairs={{0,1},{1,0},{2,3},{3,2},{4,5},{5,4},{6,7},{7,6},{8,9},{9,8},{10,11... | collective-permute-start | bytes 3145736 | tf_op jit(solution)/shard_map/ppermute | solution.py:696
  66.5 12.8 %copy-start.2 = (s32[1,4,16]{2,1,0:T(4,128)S(1)}, s32[1,4,16]{2,1,0:T(4,128)}, u32[]{:S(2)}) copy-start(s32[1,4,16]{2,1,0:T(4,128)} %param.14) | copy-start | bytes 772
  90.9 18.7 %collective-permute-start.13 = (bf16[1024,512]{1,0:T(8,128)(2,1)S(1)}, bf16[1024,512]{1,0:T(8,128)(2,1)S(1)}, u32[]{:S(2)}, u32[]{:S(2)}) collective-permute-start(bf16[1024,512]{1,0:T(8,128)(2,1)S(1)} %get-tuple-element.150), channel_id=1, source_target_pairs={{0,8},{4,12},{8,0},{12,4},{16,24},{20,28},{24,16},{28,20},{1,9},{5... | collective-permute-start | bytes 3145736 | tf_op jit(solution)/shard_map/ppermute | solution.py:789
  91.6 18.7 %collective-permute-start.14 = (bf16[1024,512]{1,0:T(8,128)(2,1)S(1)}, bf16[1024,512]{1,0:T(8,128)(2,1)S(1)}, u32[]{:S(2)}, u32[]{:S(2)}) collective-permute-start(bf16[1024,512]{1,0:T(8,128)(2,1)S(1)} %collective-permute-done.7.refs_1_), channel_id=1, source_target_pairs={{2,3},{3,2},{6,7},{7,6},{10,11},{11,10},{14,15},{15,14},{18,19},{1... | collective-permute-start | bytes 3145736 | tf_op jit(solution)/shard_map/ppermute | solution.py:791

commit v4 on v3

--- a/solution.py
+++ b/solution.py
@@ -103,33 +103,34 @@
         den[row, :] += pack_denominators(listed)
 
 
-def attend_units(queries, keys, values, num, den, units):
+def attend_units(queries, rows_here, w, num, den, rows):
+    keys = jnp.dot(rows_here, w[0], preferred_element_type=jnp.float32).astype(jnp.bfloat16)
+    values = jnp.dot(rows_here, w[1], preferred_element_type=jnp.float32).astype(jnp.bfloat16)
     low_lanes, _ = lane_masks()
     low = jnp.where(low_lanes, 1.0, 0.0).astype(jnp.bfloat16)
     high = jnp.where(low_lanes, 0.0, 1.0).astype(jnp.bfloat16)
-    nothing = jnp.zeros((LANES // 2, TILE), jnp.bfloat16)
-    rows = [pl.ds(pl.multiple_of(row * TILE, TILE), TILE) for row, _ in units]
     last = queries.shape[0] // TILE - 1
     query_rows = [
-        pl.ds(pl.multiple_of(jnp.minimum(row, last) * TILE, TILE), TILE) for row, _ in units
+        pl.ds(pl.multiple_of(jnp.minimum(row, last) * TILE, TILE), TILE) for row in rows
     ]
-    denominators = [[] for _ in units]
+    rows = [pl.ds(pl.multiple_of(row * TILE, TILE), TILE) for row in rows]
+    spans = [slice(index * TILE, (index + 1) * TILE) for index in range(len(rows))]
+    denominators = [[] for _ in rows]
     for pair in range(queries.shape[1] // LANES):
         part = slice(pair * LANES, (pair + 1) * LANES)
-        middle = pair * LANES + LANES // 2
         weights = []
-        for row, (_, tile) in zip(query_rows, units):
-            first = jnp.concatenate([keys[tile, pair * LANES : middle, :], nothing], axis=0)
-            second = jnp.concatenate([nothing, keys[tile, middle : (pair + 1) * LANES, :]], axis=0)
-            scores = jnp.dot(
+        for row, span in zip(query_rows, spans):
+            key = keys[span, part]
+            scores = lax.dot_general(
                 queries[row, part],
-                jnp.concatenate([first, second], axis=1),
+                jnp.concatenate([key * low, key * high], axis=0),
+                (((1,), (1,)), ((), ())),
                 preferred_element_type=jnp.float32,
             )
             weights.append(jnp.exp(jnp.clip(scores, -5.0, 5.0)).astype(jnp.bfloat16))
         sums = []
-        for weight, (_, tile) in zip(weights, units):
-            value = values[tile, :, part]
+        for weight, span in zip(weights, spans):
+            value = values[span, part]
             wide = jnp.concatenate(
                 [
                     jnp.concatenate([value * low, low], axis=1),
@@ -190,17 +191,30 @@
         tile_list[2 * (found + inner)] = 0
         tile_list[2 * (found + inner) + 1] = 0
 
-    def group(index, carry):
+    def group(first, size):
         units = []
-        for inner in range(GROUP):
-            unit = index * GROUP + inner
+        for inner in range(size):
+            unit = first + inner
             units.append(
                 (row_list[unit], tile_list[2 * unit], tile_list[2 * unit + 1], fill_list[unit])
             )
         attend_chunks(queries, keys, values, ones, num, den, units)
+
+    in_groups(found, group)
+
+
+def in_groups(found, group):
+    whole = found // GROUP
+
+    def visit(index, carry):
+        group(index * GROUP, GROUP)
         return carry
 
-    lax.fori_loop(0, (found + GROUP - 1) // GROUP, group, 0)
+    lax.fori_loop(0, whole, visit, 0)
+    left = found - whole * GROUP
+    half = GROUP // 2
+    pl.when(left > half)(lambda: group(whole * GROUP, GROUP))
+    pl.when(jnp.logical_and(left > 0, left <= half))(lambda: group(whole * GROUP, half))
 
 
 def each_tile(tiles, action):
@@ -327,14 +341,14 @@
     (expand_q, num_in, den_in, w) = refs[count : count + 4]
     refs = refs[count + 4 :]
     if last:
-        (_, out_ref, features, keys, values, num, den, row_list, tile_list, mark) = refs[:-3]
+        (_, out_ref, features, num, den, row_list, tile_list, mark) = refs[:-3]
         (results, result_sems) = refs[-3:-1]
     else:
         if gives_out:
             (num, den, out_ref) = refs[:3]
         else:
             (num, den) = refs[:2]
-        (features, keys, values, row_list, tile_list, mark) = refs[-7:-1]
+        (features, row_list, tile_list, mark) = refs[-5:-1]
     chooser = refs[-1]
     own_rows, width = expand_q.shape
     tiles_here = own_rows // TILE
@@ -382,9 +396,8 @@
     num[spare, :] = jnp.zeros((TILE, width), jnp.float32)
     den[spare, :] = jnp.zeros((TILE, LANES), jnp.float32)
 
-    def group(index, carry):
-        first = index * GROUP
-        for i in range(GROUP):
+    def group(first, size):
+        for i in range(size):
             spot = tile_list[first + i]
             for source in sources:
                 tiles = source.shape[0] // TILE
@@ -395,12 +408,10 @@
                     features[i * TILE : (i + 1) * TILE, :] = source[rows, :]
 
                 spot = spot - tiles
-        project(features[...], w, keys, values, 0)
-        units = [(row_list[first + i], i) for i in range(GROUP)]
-        attend_units(expand_q, keys, values, num, den, units)
-        return carry
-
-    lax.fori_loop(0, (found + GROUP - 1) // GROUP, group, 0)
+        rows = [row_list[first + i] for i in range(size)]
+        attend_units(expand_q, features[: size * TILE, :], w, num, den, rows)
+
+    in_groups(found, group)
 
     def finish(tile, target):
         inverse = spread_reciprocals(den[target, :], chooser[...])
@@ -437,8 +448,6 @@
         input_output_aliases={len(arguments): 0} if last else {},
         scratch_shapes=[
             pltpu.VMEM((GROUP * TILE, width), jnp.bfloat16),
-            pltpu.VMEM((GROUP, width, TILE), jnp.bfloat16),
-            pltpu.VMEM((GROUP, TILE, width), jnp.bfloat16),
         ]
         + (sums_scratch if last else [])
         + [

time: 119 us -> 118 us (level)
  the two profiles are of different devices: /device:TPU:25 before, /device:TPU:0 now
where the time goes in v4:
time: 118 us; the launch traced here: 116 us
  Pallas kernels  81.3 us (69%)
  starting transfers between devices  27 us (23%)
  waiting for transfers between devices  4.4 us (4%)
  local copies, waits for them, and re-layouts  1.63 us (1%)
    pallas_call x2, Pallas kernels, more_attention(): pl.pallas_call(functools.partial(more_kernel, len(pieces), bool(own), spl...  30.4 us
    pallas_call x3, Pallas kernels, expand_attention(): pl.pallas_call(functools.partial(expand_kernel, len(sources), gives_out,...  28.9 us
    ppermute x9, starting transfers between devices, swap(): lax.ppermute(x, 'node', [(i, i ^ flip[i % 2]) for i in range(blocks)])  15.3 us
    pallas_call x1, Pallas kernels, own_attention(): pl.pallas_call(functools.partial(own_kernel, split), in_specs=[SMEM] * 3...  8.58 us
    pallas_call x3, Pallas kernels, select(): pl.pallas_call(functools.partial(select_kernel, jobs, share, len(parts),...  7.38 us
    ppermute x4, starting transfers between devices, other(): return lax.ppermute(x, 'head', [(0, 1), (1, 0)])  6.29 us
    pallas_call x1, Pallas kernels, arrival_spots(): pl.pallas_call(functools.partial(spots_kernel, tiles, lines, blocks), in_...  2.73 us
    ppermute x1, waiting for transfers between devices, local(): lax.ppermute(direct, 'node', [(i, i ^ flips[2]) for i in range(0, blocks,...  2.53 us
  transfers between devices with their start and end apart: 17, of which 2 were waited for; matrix products, arithmetic and copies ran while one was open for 1% of the time, Pallas kernels for 65%

profile of v4, /device:TPU:0, one launch (start us, length us, event | category | flops | bytes accessed | tf_op | source)
XLA Modules:
  0.0 115.7 jit_solution(12252441375334023784)
XLA Ops:
  0.0 0.9 pad_maximum_fusion
  0.9 3.0 %collective-permute-start = (f32[2,256]{1,0:T(2,128)S(1)}, f32[2,256]{1,0:T(2,128)S(1)}, u32[]{:S(2)}, u32[]{:S(2)}) collective-permute-start(f32[2,256]{1,0:T(2,128)S(1)} %pad_maximum_fusion), channel_id=1, source_target_pairs={{0,1},{1,0},{2,3},{3,2},{4,5},{5,4},{6,7},{7,6},{8,9},{9,8},{10,11... | collective-permute-start | bytes 6152 | tf_op jit(solution)/shard_map/ppermute | solution.py:705
  3.8 2.2 %shard_map.82 = bf16[1024,512]{1,0:T(8,128)(2,1)} custom-call(s32[1]{0:T(128)} %bitcast.here_ref, bf16[2048,512]{1,0:T(8,128)(2,1)} %refs_1_), custom_call_target="tpu_custom_call" | custom-call | tf_op jit(solution)/shard_map/pallas_call | solution.py:487
  6.1 1.3 %collective-permute-start.1 = (bf16[1024,512]{1,0:T(8,128)(2,1)}, bf16[1024,512]{1,0:T(8,128)(2,1)}, u32[]{:S(2)}, u32[]{:S(2)}) collective-permute-start(bf16[1024,512]{1,0:T(8,128)(2,1)} %shard_map.82), channel_id=1, source_target_pairs={{0,1},{1,0},{2,3},{3,2},{4,5},{5,4},{6,7},{7,6},{8,9},{9,8},{10,11... | collective-permute-start | bytes 3145736 | tf_op jit(solution)/shard_map/ppermute | solution.py:705
  7.4 1.1 shard_map.84
  8.5 2.7 %shard_map.83 = (s32[2]{0:T(128)S(1)}, s32[2,36]{1,0:T(2,128)S(1)}, s32[2,36]{1,0:T(2,128)S(1)}, s32[2,36]{1,0:T(2,128)S(1)}, s32[4,16]{1,0:T(4,128)S(1)}, /*ind...) custom-call(s32[1]{0:T(128)} %bitcast.here_ref, ...), custom_call_target="tpu_custom_call" | custom-call | flops 99999997952 | bytes 4096 | tf_op jit(solution)/shard_map/pallas_call | solution.py:674
  11.3 1.4 %collective-permute-start.2 = (bf16[256,512]{1,0:T(8,128)(2,1)S(1)}, bf16[256,512]{1,0:T(8,128)(2,1)S(1)}, u32[]{:S(2)}, u32[]{:S(2)}) collective-permute-start(bf16[256,512]{1,0:T(8,128)(2,1)S(1)} %get-tuple-element.96), channel_id=1, source_target_pairs={{2,0},{4,2},{6,4},{8,6},{10,8},{12,10},{14,12},{16,14},{18,16},{20... | collective-permute-start | bytes 786440 | tf_op jit(solution)/shard_map/ppermute | solution.py:735
  12.9 1.4 %copy.14 = bf16[512,2,512]{2,0,1:T(8,128)(2,1)S(1)} copy(bf16[512,2,512]{2,1,0:T(2,128)(2,1)} %param.10) | data formatting | bytes 2097152 | tf_op jit(solution)/shard_map/optimization_barrier | solution.py:719
  14.3 2.2 %collective-permute-start.3 = (s32[1,32]{1,0:T(1,128)S(1)}, s32[1,32]{1,0:T(1,128)S(1)}, u32[]{:S(2)}, u32[]{:S(2)}) collective-permute-start(s32[1,32]{1,0:T(1,128)S(1)} %get-tuple-element.97), channel_id=1, source_target_pairs={{0,4},{2,6},{4,0},{6,2},{8,12},{10,14},{12,8},{14,10},{16,20},{18,... | collective-permute-start | bytes 392 | tf_op jit(solution)/shard_map/ppermute | solution.py:702
  16.5 1.6 %collective-permute-start.4 = (s32[1,32]{1,0:T(1,128)S(1)}, s32[1,32]{1,0:T(1,128)S(1)}, u32[]{:S(2)}, u32[]{:S(2)}) collective-permute-start(s32[1,32]{1,0:T(1,128)S(1)} %get-tuple-element.98), channel_id=1, source_target_pairs={{0,8},{2,10},{4,12},{6,14},{8,0},{10,2},{12,4},{14,6},{16,24},{18,... | collective-permute-start | bytes 392 | tf_op jit(solution)/shard_map/ppermute | solution.py:702
  18.1 2.7 %collective-permute-start.5 = (s32[1,32]{1,0:T(1,128)S(1)}, s32[1,32]{1,0:T(1,128)S(1)}, u32[]{:S(2)}, u32[]{:S(2)}) collective-permute-start(s32[1,32]{1,0:T(1,128)S(1)} %get-tuple-element.99), channel_id=1, source_target_pairs={{0,16},{2,18},{4,20},{6,22},{8,24},{10,26},{12,28},{14,30},{16,0},... | collective-permute-start | bytes 392 | tf_op jit(solution)/shard_map/ppermute | solution.py:702
  20.8 1.8 %collective-permute-done.5.refs_2_ = s32[1,32]{1,0:T(1,128)S(1)} collective-permute-done((s32[1,32]{1,0:T(1,128)S(1)}, s32[1,32]{1,0:T(1,128)S(1)}, u32[]{:S(2)}, u32[]{:S(2)}) %collective-permute-start.5) | collective-permute-done | bytes 160 | tf_op jit(solution)/shard_map/ppermute | solution.py:702
  22.6 8.6 %shard_map.85 = (f32[2176,512]{1,0:T(8,128)S(1)}, f32[2176,128]{1,0:T(8,128)S(1)}, bf16[16,512,128]{2,1,0:T(8,128)(2,1)S(1)}, bf16[16,128,512]{2,1,0:T(8,128)(2,...) custom-call(s32[2]{0:T(128)S(1)} %get-tuple-element.83.place_ref, s32[256]{0:T(256)S(1)} %reshape.11.cols_ref, ...), custom_call_target="tpu_custom_call" | custom-call | flops 100000000 | bytes 100000 | tf_op jit(solution)/shard_map/pallas_call | solution.py:307
  31.2 1.1 collective-permute-start.6
  32.3 3.3 %shard_map.86 = (bf16[1024,512]{1,0:T(8,128)(2,1)}, bf16[1024,512]{1,0:T(8,128)(2,1)S(1)}, bf16[1024,512]{1,0:T(8,128)(2,1)}, bf16[256,512]{1,0:T(8,128)(2,1)S(1)}) custom-call(s32[2]{0:T(128)S(1)} %get-tuple-element.83.place_ref, s32[1,32]{1,0:T(1,128)S(1)} %collective-permute-done.3.refs_0_, s32[1,32]{1,0:T(1,128)S(1)} %collective-permute-done.4.refs_1_, ...), custom_call_target="tpu_custom_call" | custom-call | flops 1000 | bytes 1000 | tf_op jit(solution)/shard_map/pallas_call | solution.py:579
  35.6 2.7 %collective-permute-start.8 = (bf16[1024,512]{1,0:T(8,128)(2,1)}, bf16[1024,512]{1,0:T(8,128)(2,1)}, u32[]{:S(2)}, u32[]{:S(2)}) collective-permute-start(bf16[1024,512]{1,0:T(8,128)(2,1)} %get-tuple-element.131), channel_id=1, source_target_pairs={{0,16},{2,10},{4,20},{6,14},{8,24},{10,2},{12,28},{14,6},{16,0},{1... | collective-permute-start | bytes 3145736 | tf_op jit(solution)/shard_map/ppermute | solution.py:702
  38.3 1.2 collective-permute-start.9
  39.5 17.7 %shard_map.87 = (f32[2176,512]{1,0:T(8,128)S(1)}, f32[2176,128]{1,0:T(8,128)S(1)}) custom-call(s32[2]{0:T(128)S(1)} %get-tuple-element.83.place_ref, s32[256]{0:T(256)S(1)} %reshape.11.cols_ref, s32[2,36]{1,0:T(2,128)S(1)} %get-tuple-element.107.where_ref, bf16[1024,512]{1,0:T(8,128)(2,1)} %collective-permute-done.1.refs_4_.refs_0_.refs_2_, ...), custom_call_target="tpu_custom_call" | custom-call | flops 999999995904 | bytes 100000 | tf_op jit(solution)/shard_map/pallas_call | solution.py:322
  57.2 1.3 %collective-permute-start.11 = (bf16[256,512]{1,0:T(8,128)(2,1)S(1)}, bf16[256,512]{1,0:T(8,128)(2,1)S(1)}, u32[]{:S(2)}, u32[]{:S(2)}) collective-permute-start(bf16[256,512]{1,0:T(8,128)(2,1)S(1)} %get-tuple-element.136), channel_id=1, source_target_pairs={{0,2},{2,4},{4,6},{6,8},{8,10},{10,12},{12,14},{14,16},{16,18},{18... | collective-permute-start | bytes 786440 | tf_op jit(solution)/shard_map/ppermute | solution.py:772
  58.5 2.7 %collective-permute-start.10 = (s32[1,32]{1,0:T(1,128)S(1)}, s32[1,32]{1,0:T(1,128)S(1)}, u32[]{:S(2)}, u32[]{:S(2)}) collective-permute-start(s32[1,32]{1,0:T(1,128)S(1)} %get-tuple-element.135), channel_id=1, source_target_pairs={{0,2},{2,0},{4,6},{6,4},{8,10},{10,8},{12,14},{14,12},{16,18},{18,... | collective-permute-start | bytes 392 | tf_op jit(solution)/shard_map/ppermute | solution.py:702
  61.3 2.0 %shard_map.88 = (bf16[1024,512]{1,0:T(8,128)(2,1)S(1)}, bf16[1024,512]{1,0:T(8,128)(2,1)S(1)}) custom-call(s32[2]{0:T(128)S(1)} %get-tuple-element.83.place_ref, s32[1,32]{1,0:T(1,128)S(1)} %copy-done.4, s32[1,32]{1,0:T(1,128)S(1)} %copy-done.6, s32[1,32]{1,0:T(1,128)S(1)} %copy-done.8, bf16[2048,512]{1,0:T(8,128)(2,1)S(1)} %copy-done, ...), custom_call_target="tpu_custom_call" | custom-call | flops 1000 | bytes 1000 | tf_op jit(solution)/shard_map/pallas_call | solution.py:579
  63.3 2.0 %shard_map.89 = bf16[2048,512]{1,0:T(8,128)(2,1)S(1)} custom-call(s32[2]{0:T(128)S(1)} %get-tuple-element.83.place_ref, s32[1,32]{1,0:T(1,128)S(1)} %collective-permute-done.10.refs_0_, bf16[2048,512]{1,0:T(8,128)(2,1)S(1)} %copy-done, bf16[1024,512]{1,0:T(8,128)(2,1)} %collective-permute-done.1.refs_4_.refs_0_.refs_2_, ...), custom_call_target="tpu_custom_call" | custom-call | flops 1000 | bytes 1000 | tf_op jit(solution)/shard_map/pallas_call | solution.py:579
  65.5 1.2 %collective-permute-start.7 = (bf16[1024,512]{1,0:T(8,128)(2,1)S(1)}, bf16[1024,512]{1,0:T(8,128)(2,1)S(1)}, u32[]{:S(2)}, u32[]{:S(2)}) collective-permute-start(bf16[1024,512]{1,0:T(8,128)(2,1)S(1)} %get-tuple-element.126), channel_id=1, source_target_pairs={{0,8},{2,18},{4,12},{6,22},{8,0},{10,26},{12,4},{14,30},{16,24},{1... | collective-permute-start | bytes 3145736 | tf_op jit(solution)/shard_map/ppermute | solution.py:702
  66.7 1.1 collective-permute-start.15
  67.8 0.9 collective-permute-start.16
  68.7 12.6 %shard_map.90 = (f32[2176,512]{1,0:T(8,128)S(1)}, f32[2176,128]{1,0:T(8,128)S(1)}) custom-call(s32[2]{0:T(128)S(1)} %get-tuple-element.83.place_ref, s32[256]{0:T(256)S(1)} %reshape.11.cols_ref, s32[2,36]{1,0:T(2,128)S(1)} %get-tuple-element.141.where_ref, bf16[1024,512]{1,0:T(8,128)(2,1)} %collective-permute-done.6.refs_5_.refs_3_.refs_0_, ...), custom_call_target="tpu_custom_call" | custom-call | flops 100000000 | bytes 100000 | tf_op jit(solution)/shard_map/pallas_call | solution.py:322
  81.3 11.2 %shard_map.91 = (f32[2176,512]{1,0:T(8,128)S(1)}, f32[2176,128]{1,0:T(8,128)S(1)}) custom-call(s32[2]{0:T(128)S(1)} %get-tuple-element.83.place_ref, s32[4,16]{1,0:T(4,128)S(1)} %bitcast.15, s32[4,16]{1,0:T(4,128)S(1)} %get-tuple-element.129.spots_ref, bf16[2048,512]{1,0:T(8,128)(2,1)S(1)} %collective-permute-done.12.refs_0_, ...), custom_call_target="tpu_custom_call" | custom-call | flops 268435456 | bytes 1048576 | tf_op jit(solution)/shard_map/pallas_call | solution.py:443
  92.6 1.9 %collective-permute-start.13 = (bf16[1024,512]{1,0:T(8,128)(2,1)S(1)}, bf16[1024,512]{1,0:T(8,128)(2,1)S(1)}, u32[]{:S(2)}, u32[]{:S(2)}) collective-permute-start(bf16[1024,512]{1,0:T(8,128)(2,1)S(1)} %get-tuple-element.150), channel_id=1, source_target_pairs={{0,8},{4,12},{8,0},{12,4},{16,24},{20,28},{24,16},{28,20},{1,9},{5... | collective-permute-start | bytes 3145736 | tf_op jit(solution)/shard_map/ppermute | solution.py:798
  94.5 0.7 collective-permute-start.14
  95.3 11.5 %shard_map.92 = (f32[2176,512]{1,0:T(8,128)S(1)}, f32[2176,128]{1,0:T(8,128)S(1)}, bf16[2048,512]{1,0:T(8,128)(2,1)}) custom-call(s32[2]{0:T(128)S(1)} %get-tuple-element.83.place_ref, s32[4,16]{1,0:T(4,128)S(1)} %bitcast.16, s32[4,16]{1,0:T(4,128)S(1)} %get-tuple-element.152.spots_ref, bf16[1024,512]{1,0:T(8,128)(2,1)S(1)} %collective-permute-done.15.refs_0_, ...), custom_call_target="tpu_custom_call" | custom-call | flops 268435456 | bytes 1048576 | tf_op jit(solution)/shard_map/pallas_call | solution.py:443
  106.7 2.5 %collective-permute-done.13.refs_0_ = bf16[1024,512]{1,0:T(8,128)(2,1)S(1)} collective-permute-done((bf16[1024,512]{1,0:T(8,128)(2,1)S(1)}, bf16[1024,512]{1,0:T(8,128)(2,1)S(1)}, u32[]{:S(2)}, u32[]{:S(2)}) %collective-permute-start.13) | collective-permute-done | bytes 1048608 | tf_op jit(solution)/shard_map/ppermute | solution.py:798
  109.3 6.3 %shard_map.93 = bf16[2048,512]{1,0:T(8,128)(2,1)} custom-call(s32[2]{0:T(128)S(1)} %get-tuple-element.83.place_ref, s32[4,16]{1,0:T(4,128)S(1)} %bitcast.17, s32[4,16]{1,0:T(4,128)S(1)} %get-tuple-element.84.spots_ref, bf16[1024,512]{1,0:T(8,128)(2,1)S(1)} %collective-permute-done.13.refs_0_, ...), custom_call_target="tpu_custom_call", output_to_operand_aliasing={{}: (9, {})} | custom-call | flops 268435456 | bytes 1048576 | tf_op jit(solution)/shard_map/pallas_call | solution.py:443
  (49 shorter events, 0.4 us)
Async XLA Ops:
  0.0 7.4 %copy-start = (bf16[2048,512]{1,0:T(8,128)(2,1)S(1)}, bf16[2048,512]{1,0:T(8,128)(2,1)}, u32[]{:S(2)}) copy-start(bf16[2048,512]{1,0:T(8,128)(2,1)} %refs_1_) | copy-start | bytes 6291460
  0.9 5.2 %collective-permute-start = (f32[2,256]{1,0:T(2,128)S(1)}, f32[2,256]{1,0:T(2,128)S(1)}, u32[]{:S(2)}, u32[]{:S(2)}) collective-permute-start(f32[2,256]{1,0:T(2,128)S(1)} %pad_maximum_fusion), channel_id=1, source_target_pairs={{0,1},{1,0},{2,3},{3,2},{4,5},{5,4},{6,7},{7,6},{8,9},{9,8},{10,11... | collective-permute-start | bytes 6152 | tf_op jit(solution)/shard_map/ppermute | solution.py:705
  6.0 2.5 %copy-start.13 = (f32[2,256]{1,0:T(2,128)}, f32[2,256]{1,0:T(2,128)S(1)}, u32[]{:S(2)}) copy-start(f32[2,256]{1,0:T(2,128)S(1)} %collective-permute-done) | copy-start | bytes 6148
  6.1 2.5 %copy-start.9 = (s32[1,4,16]{2,1,0:T(4,128)S(1)}, s32[1,4,16]{2,1,0:T(4,128)}, u32[]{:S(2)}) copy-start(s32[1,4,16]{2,1,0:T(4,128)} %param.15) | copy-start | bytes 772
  6.1 25.2 %collective-permute-start.1 = (bf16[1024,512]{1,0:T(8,128)(2,1)}, bf16[1024,512]{1,0:T(8,128)(2,1)}, u32[]{:S(2)}, u32[]{:S(2)}) collective-permute-start(bf16[1024,512]{1,0:T(8,128)(2,1)} %shard_map.82), channel_id=1, source_target_pairs={{0,1},{1,0},{2,3},{3,2},{4,5},{5,4},{6,7},{7,6},{8,9},{9,8},{10,11... | collective-permute-start | bytes 3145736 | tf_op jit(solution)/shard_map/ppermute | solution.py:705
  8.5 4.2 %copy-start.10 = (s32[32,8]{0,1:T(8,128)S(1)}, s32[32,8]{0,1:T(8,128)}, u32[]{:S(2)}) copy-start(s32[32,8]{0,1:T(8,128)} %param.13) | copy-start | bytes 3076
  11.3 6.8 %copy-start.11 = (f32[256]{0:T(256)S(1)}, f32[256]{0:T(256)}, u32[]{:S(2)}) copy-start(f32[256]{0:T(256)} %param.12) | copy-start | bytes 3076
  11.3 6.8 %copy-start.12 = (f32[256]{0:T(256)S(1)}, f32[256]{0:T(256)}, u32[]{:S(2)}) copy-start(f32[256]{0:T(256)} %param.11) | copy-start | bytes 3076
  11.3 6.8 %copy-start.14 = (f32[2,256]{1,0:T(2,128)S(1)}, f32[2,256]{1,0:T(2,128)}, u32[]{:S(2)}) copy-start(f32[2,256]{1,0:T(2,128)} %copy-done.13) | copy-start | bytes 6148
  11.3 11.3 %copy-start.1 = (bf16[512,512]{1,0:T(8,128)(2,1)S(1)}, bf16[512,512]{1,0:T(8,128)(2,1)}, u32[]{:S(2)}) copy-start(bf16[512,512]{1,0:T(8,128)(2,1)} %wq) | copy-start | bytes 1572868
  11.3 11.3 %collective-permute-start.2 = (bf16[256,512]{1,0:T(8,128)(2,1)S(1)}, bf16[256,512]{1,0:T(8,128)(2,1)S(1)}, u32[]{:S(2)}, u32[]{:S(2)}) collective-permute-start(bf16[256,512]{1,0:T(8,128)(2,1)S(1)} %get-tuple-element.96), channel_id=1, source_target_pairs={{2,0},{4,2},{6,4},{8,6},{10,8},{12,10},{14,12},{16,14},{18,16},{20... | collective-permute-start | bytes 786440 | tf_op jit(solution)/shard_map/ppermute | solution.py:735
  14.3 6.4 %collective-permute-start.3 = (s32[1,32]{1,0:T(1,128)S(1)}, s32[1,32]{1,0:T(1,128)S(1)}, u32[]{:S(2)}, u32[]{:S(2)}) collective-permute-start(s32[1,32]{1,0:T(1,128)S(1)} %get-tuple-element.97), channel_id=1, source_target_pairs={{0,4},{2,6},{4,0},{6,2},{8,12},{10,14},{12,8},{14,10},{16,20},{18,... | collective-permute-start | bytes 392 | tf_op jit(solution)/shard_map/ppermute | solution.py:702
  16.5 4.3 %collective-permute-start.4 = (s32[1,32]{1,0:T(1,128)S(1)}, s32[1,32]{1,0:T(1,128)S(1)}, u32[]{:S(2)}, u32[]{:S(2)}) collective-permute-start(s32[1,32]{1,0:T(1,128)S(1)} %get-tuple-element.98), channel_id=1, source_target_pairs={{0,8},{2,10},{4,12},{6,14},{8,0},{10,2},{12,4},{14,6},{16,24},{18,... | collective-permute-start | bytes 392 | tf_op jit(solution)/shard_map/ppermute | solution.py:702
  18.1 4.5 %collective-permute-start.5 = (s32[1,32]{1,0:T(1,128)S(1)}, s32[1,32]{1,0:T(1,128)S(1)}, u32[]{:S(2)}, u32[]{:S(2)}) collective-permute-start(s32[1,32]{1,0:T(1,128)S(1)} %get-tuple-element.99), channel_id=1, source_target_pairs={{0,16},{2,18},{4,20},{6,22},{8,24},{10,26},{12,28},{14,30},{16,0},... | collective-permute-start | bytes 392 | tf_op jit(solution)/shard_map/ppermute | solution.py:702
  20.8 14.9 %copy-start.3 = (s32[1,32]{1,0:T(1,128)}, s32[1,32]{1,0:T(1,128)S(1)}, u32[]{:S(2)}) copy-start(s32[1,32]{1,0:T(1,128)S(1)} %collective-permute-done.3.refs_0_) | copy-start | bytes 388
  20.8 14.9 %copy-start.5 = (s32[1,32]{1,0:T(1,128)}, s32[1,32]{1,0:T(1,128)S(1)}, u32[]{:S(2)}) copy-start(s32[1,32]{1,0:T(1,128)S(1)} %collective-permute-done.4.refs_1_) | copy-start | bytes 388
  22.6 13.0 %copy-start.7 = (s32[1,32]{1,0:T(1,128)}, s32[1,32]{1,0:T(1,128)S(1)}, u32[]{:S(2)}) copy-start(s32[1,32]{1,0:T(1,128)S(1)} %collective-permute-done.5.refs_2_) | copy-start | bytes 388
  31.2 26.0 %collective-permute-start.6 = (bf16[1024,512]{1,0:T(8,128)(2,1)}, bf16[1024,512]{1,0:T(8,128)(2,1)}, u32[]{:S(2)}, u32[]{:S(2)}) collective-permute-start(bf16[1024,512]{1,0:T(8,128)(2,1)} %get-tuple-element.106), channel_id=1, source_target_pairs={{0,1},{1,0},{2,3},{3,2},{4,5},{5,4},{6,7},{7,6},{8,9},{9,8},{10,11... | collective-permute-start | bytes 3145736 | tf_op jit(solution)/shard_map/ppermute | solution.py:705
  35.6 27.7 %collective-permute-start.8 = (bf16[1024,512]{1,0:T(8,128)(2,1)}, bf16[1024,512]{1,0:T(8,128)(2,1)}, u32[]{:S(2)}, u32[]{:S(2)}) collective-permute-start(bf16[1024,512]{1,0:T(8,128)(2,1)} %get-tuple-element.131), channel_id=1, source_target_pairs={{0,16},{2,10},{4,20},{6,14},{8,24},{10,2},{12,28},{14,6},{16,0},{1... | collective-permute-start | bytes 3145736 | tf_op jit(solution)/shard_map/ppermute | solution.py:702
  38.3 25.0 %collective-permute-start.9 = (bf16[1024,512]{1,0:T(8,128)(2,1)}, bf16[1024,512]{1,0:T(8,128)(2,1)}, u32[]{:S(2)}, u32[]{:S(2)}) collective-permute-start(bf16[1024,512]{1,0:T(8,128)(2,1)} %get-tuple-element.132), channel_id=1, source_target_pairs={{0,4},{2,6},{4,0},{6,2},{8,12},{10,14},{12,8},{14,10},{16,20},{18,... | collective-permute-start | bytes 3145736 | tf_op jit(solution)/shard_map/ppermute | solution.py:702
  39.5 21.8 %copy-start.4 = (s32[1,32]{1,0:T(1,128)S(1)}, s32[1,32]{1,0:T(1,128)}, u32[]{:S(2)}) copy-start(s32[1,32]{1,0:T(1,128)} %copy-done.3) | copy-start | bytes 388
  39.5 21.8 %copy-start.6 = (s32[1,32]{1,0:T(1,128)S(1)}, s32[1,32]{1,0:T(1,128)}, u32[]{:S(2)}) copy-start(s32[1,32]{1,0:T(1,128)} %copy-done.5) | copy-start | bytes 388
  39.5 21.8 %copy-start.8 = (s32[1,32]{1,0:T(1,128)S(1)}, s32[1,32]{1,0:T(1,128)}, u32[]{:S(2)}) copy-start(s32[1,32]{1,0:T(1,128)} %copy-done.7) | copy-start | bytes 388
  57.2 8.2 %collective-permute-start.11 = (bf16[256,512]{1,0:T(8,128)(2,1)S(1)}, bf16[256,512]{1,0:T(8,128)(2,1)S(1)}, u32[]{:S(2)}, u32[]{:S(2)}) collective-permute-start(bf16[256,512]{1,0:T(8,128)(2,1)S(1)} %get-tuple-element.136), channel_id=1, source_target_pairs={{0,2},{2,4},{4,6},{6,8},{8,10},{10,12},{12,14},{14,16},{16,18},{18... | collective-permute-start | bytes 786440 | tf_op jit(solution)/shard_map/ppermute | solution.py:772
  58.5 4.8 %collective-permute-start.10 = (s32[1,32]{1,0:T(1,128)S(1)}, s32[1,32]{1,0:T(1,128)S(1)}, u32[]{:S(2)}, u32[]{:S(2)}) collective-permute-start(s32[1,32]{1,0:T(1,128)S(1)} %get-tuple-element.135), channel_id=1, source_target_pairs={{0,2},{2,0},{4,6},{6,4},{8,10},{10,8},{12,14},{14,12},{16,18},{18,... | collective-permute-start | bytes 392 | tf_op jit(solution)/shard_map/ppermute | solution.py:702
  65.4 15.9 %collective-permute-start.12 = (bf16[2048,512]{1,0:T(8,128)(2,1)S(1)}, bf16[2048,512]{1,0:T(8,128)(2,1)S(1)}, u32[]{:S(2)}, u32[]{:S(2)}) collective-permute-start(bf16[2048,512]{1,0:T(8,128)(2,1)S(1)} %shard_map.89), channel_id=1, source_target_pairs={{0,2},{2,0},{4,6},{6,4},{8,10},{10,8},{12,14},{14,12},{16,18},{18,... | collective-permute-start | bytes 6291464 | tf_op jit(solution)/shard_map/ppermute | solution.py:702
  65.5 27.1 %collective-permute-start.7 = (bf16[1024,512]{1,0:T(8,128)(2,1)S(1)}, bf16[1024,512]{1,0:T(8,128)(2,1)S(1)}, u32[]{:S(2)}, u32[]{:S(2)}) collective-permute-start(bf16[1024,512]{1,0:T(8,128)(2,1)S(1)} %get-tuple-element.126), channel_id=1, source_target_pairs={{0,8},{2,18},{4,12},{6,22},{8,0},{10,26},{12,4},{14,30},{16,24},{1... | collective-permute-start | bytes 3145736 | tf_op jit(solution)/shard_map/ppermute | solution.py:702
  66.7 28.6 %collective-permute-start.15 = (bf16[1024,512]{1,0:T(8,128)(2,1)S(1)}, bf16[1024,512]{1,0:T(8,128)(2,1)S(1)}, u32[]{:S(2)}, u32[]{:S(2)}) collective-permute-start(bf16[1024,512]{1,0:T(8,128)(2,1)S(1)} %get-tuple-element.153), channel_id=1, source_target_pairs={{0,4},{2,6},{4,0},{6,2},{8,12},{10,14},{12,8},{14,10},{16,20},{18,... | collective-permute-start | bytes 3145736 | tf_op jit(solution)/shard_map/ppermute | solution.py:702
  67.8 27.5 %collective-permute-start.16 = (bf16[1024,512]{1,0:T(8,128)(2,1)}, bf16[1024,512]{1,0:T(8,128)(2,1)S(1)}, u32[]{:S(2)}, u32[]{:S(2)}) collective-permute-start(bf16[1024,512]{1,0:T(8,128)(2,1)} %collective-permute-done.8.refs_1_), channel_id=1, source_target_pairs={{0,1},{1,0},{2,3},{3,2},{4,5},{5,4},{6,7},{7,6},{8,9},{9,8},{10,11... | collective-permute-start | bytes 3145736 | tf_op jit(solution)/shard_map/ppermute | solution.py:705
  68.7 12.7 %copy-start.2 = (s32[1,4,16]{2,1,0:T(4,128)S(1)}, s32[1,4,16]{2,1,0:T(4,128)}, u32[]{:S(2)}) copy-start(s32[1,4,16]{2,1,0:T(4,128)} %param.14) | copy-start | bytes 772
  92.6 16.7 %collective-permute-start.13 = (bf16[1024,512]{1,0:T(8,128)(2,1)S(1)}, bf16[1024,512]{1,0:T(8,128)(2,1)S(1)}, u32[]{:S(2)}, u32[]{:S(2)}) collective-permute-start(bf16[1024,512]{1,0:T(8,128)(2,1)S(1)} %get-tuple-element.150), channel_id=1, source_target_pairs={{0,8},{4,12},{8,0},{12,4},{16,24},{20,28},{24,16},{28,20},{1,9},{5... | collective-permute-start | bytes 3145736 | tf_op jit(solution)/shard_map/ppermute | solution.py:798
  94.5 14.8 %collective-permute-start.14 = (bf16[1024,512]{1,0:T(8,128)(2,1)S(1)}, bf16[1024,512]{1,0:T(8,128)(2,1)S(1)}, u32[]{:S(2)}, u32[]{:S(2)}) collective-permute-start(bf16[1024,512]{1,0:T(8,128)(2,1)S(1)} %collective-permute-done.7.refs_1_), channel_id=1, source_target_pairs={{2,3},{3,2},{6,7},{7,6},{10,11},{11,10},{14,15},{15,14},{18,19},{1... | collective-permute-start | bytes 3145736 | tf_op jit(solution)/shard_map/ppermute | solution.py:800

commit v5 on v4

--- a/solution.py
+++ b/solution.py
@@ -331,7 +331,7 @@
         ],
         compiler_params=pltpu.CompilerParams(vmem_limit_bytes=24 * MIB),
         cost_estimate=pl.CostEstimate(
-            flops=10**12 if own else 10**8, bytes_accessed=10**5, transcendentals=0
+            flops=10**12, bytes_accessed=10**5, transcendentals=0
         ),
     )(*tables, *pieces, w, local_q, num, den, *own)
 
@@ -413,20 +413,27 @@
 
     in_groups(found, group)
 
+    def outputs(target):
+        inverse = spread_reciprocals(den[target, :], chooser[...])
+        return (num[target, :] * inverse).astype(jnp.bfloat16)
+
     def finish(tile, target):
-        inverse = spread_reciprocals(den[target, :], chooser[...])
-        result = (num[target, :] * inverse).astype(jnp.bfloat16)
-        if last:
-            results[target, :] = result
-            copy_out(tile, target).start()
-        else:
-            out_ref[target, :] = result
+        results[target, :] = outputs(target)
+        copy_out(tile, target).start()
+
+    def finish_some(index, carry):
+        size = math.gcd(GROUP, tiles_here) * TILE
+        target = pl.ds(pl.multiple_of(index * size, TILE), size)
+        out_ref[target, :] = outputs(target)
+        return carry
 
     def copy_out(tile, target):
         return pltpu.make_async_copy(results.at[target], out_ref.at[target], result_sems.at[tile])
 
-    if gives_out:
+    if last:
         each_marked(finish)
+    elif gives_out:
+        lax.fori_loop(0, tiles_here // math.gcd(GROUP, tiles_here), finish_some, 0)
     if last:
         each_marked(lambda tile, target: copy_out(tile, target).wait())
 
@@ -466,20 +473,33 @@
         + [pltpu.VMEM((2 * LANES, width), jnp.bfloat16)],
         compiler_params=pltpu.CompilerParams(vmem_limit_bytes=24 * MIB),
         cost_estimate=pl.CostEstimate(
-            flops=own_rows * width * 256, bytes_accessed=own_rows * width, transcendentals=0
+            flops=10**8 if gives_out else 10**12, bytes_accessed=own_rows * width, transcendentals=0
         ),
     )(*arguments, *([out] if last else []))
 
 
-def cut_half_kernel(here_ref, features, half_ref, buffer, sem):
+def cut_half_kernel(here_ref, features, half_ref, buffer, sems):
     rows = half_ref.shape[0]
-    start = pl.multiple_of(here_ref[0] * rows, TILE)
-    inward = pltpu.make_async_copy(features.at[pl.ds(start, rows)], buffer, sem)
-    inward.start()
-    inward.wait()
-    outward = pltpu.make_async_copy(buffer, half_ref, sem)
-    outward.start()
-    outward.wait()
+    start = here_ref[0] * rows
+    pieces = sems.shape[1]
+    size = rows // pieces
+    inward, outward = [], []
+    for index in range(pieces):
+        source = pl.ds(pl.multiple_of(start + index * size, TILE), size)
+        target = pl.ds(index * size, size)
+        inward.append(
+            pltpu.make_async_copy(features.at[source], buffer.at[target], sems.at[0, index])
+        )
+        outward.append(
+            pltpu.make_async_copy(buffer.at[target], half_ref.at[target], sems.at[1, index])
+        )
+    for copy in inward:
+        copy.start()
+    for first, second in zip(inward, outward):
+        first.wait()
+        second.start()
+    for copy in outward:
+        copy.wait()
 
 
 def cut_half(here, features):
@@ -489,7 +509,7 @@
         in_specs=[SMEM, ANY],
         out_specs=ANY,
         out_shape=jax.ShapeDtypeStruct(half, jnp.bfloat16),
-        scratch_shapes=[pltpu.VMEM(half, jnp.bfloat16), pltpu.SemaphoreType.DMA],
+        scratch_shapes=[pltpu.VMEM(half, jnp.bfloat16), pltpu.SemaphoreType.DMA((2, 4))],
         compiler_params=pltpu.CompilerParams(vmem_limit_bytes=60 * MIB),
     )(here, features)
 

time: 118 us -> 120 us (1.017)
  the two profiles are of different devices: /device:TPU:0 before, /device:TPU:25 now
where the time goes in v5:
time: 120 us; the launch traced here: 119 us
  Pallas kernels  85.1 us (71%)
  starting transfers between devices  24 us (20%)
  waiting for transfers between devices  6.74 us (6%)
  local copies, waits for them, and re-layouts  1.63 us (1%)
    pallas_call x2, Pallas kernels, more_attention(): pl.pallas_call(functools.partial(more_kernel, len(pieces), bool(own), spl...  30.4 us
    pallas_call x3, Pallas kernels, expand_attention(): pl.pallas_call(functools.partial(expand_kernel, len(sources), gives_out,...  28.5 us
    ppermute x9, starting transfers between devices, swap(): lax.ppermute(x, 'node', [(i, i ^ flip[i % 2]) for i in range(blocks)])  11 us
    pallas_call x1, Pallas kernels, own_attention(): pl.pallas_call(functools.partial(own_kernel, split), in_specs=[SMEM] * 3...  10.2 us
    pallas_call x3, Pallas kernels, select(): pl.pallas_call(functools.partial(select_kernel, jobs, share, len(parts),...  10.1 us
    ppermute x1, starting transfers between devices, local(): halo = lax.ppermute(edge_rows, ('node', 'head'), inward)  4.14 us
    ppermute x1, starting transfers between devices, local(): other_halo = lax.ppermute(edge_rows, ('node', 'head'), outward)  3.54 us
    ppermute x9, waiting for transfers between devices, swap(): lax.ppermute(x, 'node', [(i, i ^ flip[i % 2]) for i in range(blocks)])  3.24 us
  transfers between devices with their start and end apart: 17, of which 5 were waited for; matrix products, arithmetic and copies ran while one was open for 1% of the time, Pallas kernels for 66%

profile of v5, /device:TPU:25, one launch (start us, length us, event | category | flops | bytes accessed | tf_op | source)
XLA Modules:
  0.0 118.8 jit_solution(4393931836528144929)
XLA Ops:
  0.0 0.9 pad_maximum_fusion
  0.9 1.2 %collective-permute-start = (f32[2,256]{1,0:T(2,128)S(1)}, f32[2,256]{1,0:T(2,128)S(1)}, u32[]{:S(2)}, u32[]{:S(2)}) collective-permute-start(f32[2,256]{1,0:T(2,128)S(1)} %pad_maximum_fusion), channel_id=1, source_target_pairs={{0,1},{1,0},{2,3},{3,2},{4,5},{5,4},{6,7},{7,6},{8,9},{9,8},{10,11... | collective-permute-start | bytes 6152 | tf_op jit(solution)/shard_map/ppermute | solution.py:725
  2.1 2.0 %shard_map.82 = bf16[1024,512]{1,0:T(8,128)(2,1)} custom-call(s32[1]{0:T(128)} %bitcast.here_ref, bf16[2048,512]{1,0:T(8,128)(2,1)} %refs_1_), custom_call_target="tpu_custom_call" | custom-call | tf_op jit(solution)/shard_map/pallas_call | solution.py:507
  4.1 0.4 collective-permute-start.1
  4.5 1.1 shard_map.84
  5.7 2.7 %shard_map.83 = (s32[2]{0:T(128)S(1)}, s32[2,36]{1,0:T(2,128)S(1)}, s32[2,36]{1,0:T(2,128)S(1)}, s32[2,36]{1,0:T(2,128)S(1)}, s32[4,16]{1,0:T(4,128)S(1)}, /*ind...) custom-call(s32[1]{0:T(128)} %bitcast.here_ref, ...), custom_call_target="tpu_custom_call" | custom-call | flops 99999997952 | bytes 4096 | tf_op jit(solution)/shard_map/pallas_call | solution.py:694
  8.4 4.1 %collective-permute-start.2 = (bf16[256,512]{1,0:T(8,128)(2,1)S(1)}, bf16[256,512]{1,0:T(8,128)(2,1)S(1)}, u32[]{:S(2)}, u32[]{:S(2)}) collective-permute-start(bf16[256,512]{1,0:T(8,128)(2,1)S(1)} %get-tuple-element.96), channel_id=1, source_target_pairs={{2,0},{4,2},{6,4},{8,6},{10,8},{12,10},{14,12},{16,14},{18,16},{20... | collective-permute-start | bytes 786440 | tf_op jit(solution)/shard_map/ppermute | solution.py:755
  12.8 1.4 %copy.14 = bf16[512,2,512]{2,0,1:T(8,128)(2,1)S(1)} copy(bf16[512,2,512]{2,1,0:T(2,128)(2,1)} %param.10) | data formatting | bytes 2097152 | tf_op jit(solution)/shard_map/optimization_barrier | solution.py:739
  14.2 1.3 %collective-permute-start.3 = (s32[1,32]{1,0:T(1,128)S(1)}, s32[1,32]{1,0:T(1,128)S(1)}, u32[]{:S(2)}, u32[]{:S(2)}) collective-permute-start(s32[1,32]{1,0:T(1,128)S(1)} %get-tuple-element.97), channel_id=1, source_target_pairs={{0,4},{2,6},{4,0},{6,2},{8,12},{10,14},{12,8},{14,10},{16,20},{18,... | collective-permute-start | bytes 392 | tf_op jit(solution)/shard_map/ppermute | solution.py:722
  15.5 0.2 collective-permute-start.4
  15.8 1.3 %collective-permute-done.3.refs_0_ = s32[1,32]{1,0:T(1,128)S(1)} collective-permute-done((s32[1,32]{1,0:T(1,128)S(1)}, s32[1,32]{1,0:T(1,128)S(1)}, u32[]{:S(2)}, u32[]{:S(2)}) %collective-permute-start.3) | collective-permute-done | bytes 160 | tf_op jit(solution)/shard_map/ppermute | solution.py:722
  17.1 1.2 collective-permute-done.4.refs_1_
  18.3 0.7 collective-permute-done.5.refs_2_
  19.0 10.2 %shard_map.85 = (f32[2176,512]{1,0:T(8,128)S(1)}, f32[2176,128]{1,0:T(8,128)S(1)}, bf16[16,512,128]{2,1,0:T(8,128)(2,1)S(1)}, bf16[16,128,512]{2,1,0:T(8,128)(2,...) custom-call(s32[2]{0:T(128)S(1)} %get-tuple-element.83.place_ref, s32[256]{0:T(256)S(1)} %reshape.11.cols_ref, ...), custom_call_target="tpu_custom_call" | custom-call | flops 100000000 | bytes 100000 | tf_op jit(solution)/shard_map/pallas_call | solution.py:307
  29.2 0.1 collective-permute-start.6
  29.4 3.6 %shard_map.86 = (bf16[1024,512]{1,0:T(8,128)(2,1)}, bf16[1024,512]{1,0:T(8,128)(2,1)}, bf16[1024,512]{1,0:T(8,128)(2,1)}, bf16[256,512]{1,0:T(8,128)(2,1)S(1)}) custom-call(s32[2]{0:T(128)S(1)} %get-tuple-element.83.place_ref, s32[1,32]{1,0:T(1,128)S(1)} %collective-permute-done.3.refs_0_, s32[1,32]{1,0:T(1,128)S(1)} %collective-permute-done.4.refs_1_, ...), custom_call_target="tpu_custom_call" | custom-call | flops 1000 | bytes 1000 | tf_op jit(solution)/shard_map/pallas_call | solution.py:599
  33.0 1.0 collective-permute-start.8
  34.1 0.2 collective-permute-start.9
  34.3 16.4 %shard_map.87 = (f32[2176,512]{1,0:T(8,128)S(1)}, f32[2176,128]{1,0:T(8,128)S(1)}) custom-call(s32[2]{0:T(128)S(1)} %get-tuple-element.83.place_ref, s32[256]{0:T(256)S(1)} %reshape.11.cols_ref, s32[2,36]{1,0:T(2,128)S(1)} %get-tuple-element.107.where_ref, bf16[1024,512]{1,0:T(8,128)(2,1)} %collective-permute-done.1.refs_4_.refs_0_.refs_2_, ...), custom_call_target="tpu_custom_call" | custom-call | flops 999999995904 | bytes 100000 | tf_op jit(solution)/shard_map/pallas_call | solution.py:322
  50.8 2.8 %collective-permute-done.6.refs_5_.refs_3_.refs_0_ = bf16[1024,512]{1,0:T(8,128)(2,1)} collective-permute-done((bf16[1024,512]{1,0:T(8,128)(2,1)}, bf16[1024,512]{1,0:T(8,128)(2,1)}, u32[]{:S(2)}, u32[]{:S(2)}) %collective-permute-start.6) | collective-permute-done | bytes 1048608 | tf_op jit(solution)/shard_map/ppermute | solution.py:725
  53.5 3.5 %collective-permute-start.11 = (bf16[256,512]{1,0:T(8,128)(2,1)S(1)}, bf16[256,512]{1,0:T(8,128)(2,1)S(1)}, u32[]{:S(2)}, u32[]{:S(2)}) collective-permute-start(bf16[256,512]{1,0:T(8,128)(2,1)S(1)} %get-tuple-element.136), channel_id=1, source_target_pairs={{0,2},{2,4},{4,6},{6,8},{8,10},{10,12},{12,14},{14,16},{16,18},{18... | collective-permute-start | bytes 786440 | tf_op jit(solution)/shard_map/ppermute | solution.py:792
  57.2 4.3 %collective-permute-start.7 = (bf16[1024,512]{1,0:T(8,128)(2,1)}, bf16[1024,512]{1,0:T(8,128)(2,1)}, u32[]{:S(2)}, u32[]{:S(2)}) collective-permute-start(bf16[1024,512]{1,0:T(8,128)(2,1)} %get-tuple-element.126), channel_id=1, source_target_pairs={{0,8},{2,18},{4,12},{6,22},{8,0},{10,26},{12,4},{14,30},{16,24},{1... | collective-permute-start | bytes 3145736 | tf_op jit(solution)/shard_map/ppermute | solution.py:722
  61.5 3.1 %shard_map.88 = (bf16[1024,512]{1,0:T(8,128)(2,1)}, bf16[1024,512]{1,0:T(8,128)(2,1)S(1)}) custom-call(s32[2]{0:T(128)S(1)} %get-tuple-element.83.place_ref, s32[1,32]{1,0:T(1,128)S(1)} %copy-done.4, s32[1,32]{1,0:T(1,128)S(1)} %copy-done.6, s32[1,32]{1,0:T(1,128)S(1)} %copy-done.8, bf16[2048,512]{1,0:T(8,128)(2,1)S(1)} %copy-done, ...), custom_call_target="tpu_custom_call" | custom-call | flops 1000 | bytes 1000 | tf_op jit(solution)/shard_map/pallas_call | solution.py:599
  64.8 3.4 %shard_map.89 = bf16[2048,512]{1,0:T(8,128)(2,1)} custom-call(s32[2]{0:T(128)S(1)} %get-tuple-element.83.place_ref, s32[1,32]{1,0:T(1,128)S(1)} %collective-permute-done.10.refs_0_, bf16[2048,512]{1,0:T(8,128)(2,1)S(1)} %copy-done, bf16[1024,512]{1,0:T(8,128)(2,1)} %collective-permute-done.1.refs_4_.refs_0_.refs_2_, ...), custom_call_target="tpu_custom_call" | custom-call | flops 1000 | bytes 1000 | tf_op jit(solution)/shard_map/pallas_call | solution.py:599
  68.1 3.7 %collective-permute-start.12 = (bf16[2048,512]{1,0:T(8,128)(2,1)}, bf16[2048,512]{1,0:T(8,128)(2,1)}, u32[]{:S(2)}, u32[]{:S(2)}) collective-permute-start(bf16[2048,512]{1,0:T(8,128)(2,1)} %shard_map.89), channel_id=1, source_target_pairs={{0,2},{2,0},{4,6},{6,4},{8,10},{10,8},{12,14},{14,12},{16,18},{18,... | collective-permute-start | bytes 6291464 | tf_op jit(solution)/shard_map/ppermute | solution.py:722
  71.8 14.0 %shard_map.90 = (f32[2176,512]{1,0:T(8,128)S(1)}, f32[2176,128]{1,0:T(8,128)S(1)}) custom-call(s32[2]{0:T(128)S(1)} %get-tuple-element.83.place_ref, s32[256]{0:T(256)S(1)} %reshape.11.cols_ref, s32[2,36]{1,0:T(2,128)S(1)} %get-tuple-element.141.where_ref, bf16[1024,512]{1,0:T(8,128)(2,1)} %collective-permute-done.6.refs_5_.refs_3_.refs_0_, ...), custom_call_target="tpu_custom_call" | custom-call | flops 999999995904 | bytes 100000 | tf_op jit(solution)/shard_map/pallas_call | solution.py:322
  85.9 9.6 %shard_map.91 = (f32[2176,512]{1,0:T(8,128)S(1)}, f32[2176,128]{1,0:T(8,128)S(1)}) custom-call(s32[2]{0:T(128)S(1)} %get-tuple-element.83.place_ref, s32[4,16]{1,0:T(4,128)S(1)} %bitcast.15, s32[4,16]{1,0:T(4,128)S(1)} %get-tuple-element.129.spots_ref, bf16[2048,512]{1,0:T(8,128)(2,1)} %collective-permute-done.12.refs_0_, ...), custom_call_target="tpu_custom_call" | custom-call | flops 999999995904 | bytes 1048576 | tf_op jit(solution)/shard_map/pallas_call | solution.py:450
  95.5 0.7 collective-permute-start.13
  96.3 2.7 %collective-permute-start.14 = (bf16[1024,512]{1,0:T(8,128)(2,1)}, bf16[1024,512]{1,0:T(8,128)(2,1)S(1)}, u32[]{:S(2)}, u32[]{:S(2)}) collective-permute-start(bf16[1024,512]{1,0:T(8,128)(2,1)} %collective-permute-done.7.refs_1_), channel_id=1, source_target_pairs={{2,3},{3,2},{6,7},{7,6},{10,11},{11,10},{14,15},{15,14},{18,19},{1... | collective-permute-start | bytes 3145736 | tf_op jit(solution)/shard_map/ppermute | solution.py:820
  99.0 12.6 %shard_map.92 = (f32[2176,512]{1,0:T(8,128)S(1)}, f32[2176,128]{1,0:T(8,128)S(1)}, bf16[2048,512]{1,0:T(8,128)(2,1)}) custom-call(s32[2]{0:T(128)S(1)} %get-tuple-element.83.place_ref, s32[4,16]{1,0:T(4,128)S(1)} %bitcast.16, s32[4,16]{1,0:T(4,128)S(1)} %get-tuple-element.152.spots_ref, bf16[1024,512]{1,0:T(8,128)(2,1)} %collective-permute-done.15.refs_0_, ...), custom_call_target="tpu_custom_call" | custom-call | flops 100000000 | bytes 1048576 | tf_op jit(solution)/shard_map/pallas_call | solution.py:450
  111.6 0.7 collective-permute-done.14.refs_1_
  112.3 6.3 %shard_map.93 = bf16[2048,512]{1,0:T(8,128)(2,1)} custom-call(s32[2]{0:T(128)S(1)} %get-tuple-element.83.place_ref, s32[4,16]{1,0:T(4,128)S(1)} %bitcast.17, s32[4,16]{1,0:T(4,128)S(1)} %get-tuple-element.84.spots_ref, bf16[1024,512]{1,0:T(8,128)(2,1)S(1)} %collective-permute-done.13.refs_0_, ...), custom_call_target="tpu_custom_call", output_to_operand_aliasing={{}: (9, {})} | custom-call | flops 100000000 | bytes 1048576 | tf_op jit(solution)/shard_map/pallas_call | solution.py:450
  (49 shorter events, 0.6 us)
Async XLA Ops:
  0.0 4.5 %copy-start = (bf16[2048,512]{1,0:T(8,128)(2,1)S(1)}, bf16[2048,512]{1,0:T(8,128)(2,1)}, u32[]{:S(2)}) copy-start(bf16[2048,512]{1,0:T(8,128)(2,1)} %refs_1_) | copy-start | bytes 6291460
  0.9 3.2 %collective-permute-start = (f32[2,256]{1,0:T(2,128)S(1)}, f32[2,256]{1,0:T(2,128)S(1)}, u32[]{:S(2)}, u32[]{:S(2)}) collective-permute-start(f32[2,256]{1,0:T(2,128)S(1)} %pad_maximum_fusion), channel_id=1, source_target_pairs={{0,1},{1,0},{2,3},{3,2},{4,5},{5,4},{6,7},{7,6},{8,9},{9,8},{10,11... | collective-permute-start | bytes 6152 | tf_op jit(solution)/shard_map/ppermute | solution.py:725
  4.1 1.5 %copy-start.13 = (f32[2,256]{1,0:T(2,128)}, f32[2,256]{1,0:T(2,128)S(1)}, u32[]{:S(2)}) copy-start(f32[2,256]{1,0:T(2,128)S(1)} %collective-permute-done) | copy-start | bytes 6148
  4.1 1.5 %copy-start.9 = (s32[1,4,16]{2,1,0:T(4,128)S(1)}, s32[1,4,16]{2,1,0:T(4,128)}, u32[]{:S(2)}) copy-start(s32[1,4,16]{2,1,0:T(4,128)} %param.15) | copy-start | bytes 772
  4.1 25.1 %collective-permute-start.1 = (bf16[1024,512]{1,0:T(8,128)(2,1)}, bf16[1024,512]{1,0:T(8,128)(2,1)}, u32[]{:S(2)}, u32[]{:S(2)}) collective-permute-start(bf16[1024,512]{1,0:T(8,128)(2,1)} %shard_map.82), channel_id=1, source_target_pairs={{0,1},{1,0},{2,3},{3,2},{4,5},{5,4},{6,7},{7,6},{8,9},{9,8},{10,11... | collective-permute-start | bytes 3145736 | tf_op jit(solution)/shard_map/ppermute | solution.py:725
  5.6 7.0 %copy-start.10 = (s32[32,8]{0,1:T(8,128)S(1)}, s32[32,8]{0,1:T(8,128)}, u32[]{:S(2)}) copy-start(s32[32,8]{0,1:T(8,128)} %param.13) | copy-start | bytes 3076
  8.4 7.2 %copy-start.11 = (f32[256]{0:T(256)S(1)}, f32[256]{0:T(256)}, u32[]{:S(2)}) copy-start(f32[256]{0:T(256)} %param.12) | copy-start | bytes 3076
  8.4 7.2 %copy-start.12 = (f32[256]{0:T(256)S(1)}, f32[256]{0:T(256)}, u32[]{:S(2)}) copy-start(f32[256]{0:T(256)} %param.11) | copy-start | bytes 3076
  8.4 7.2 %copy-start.14 = (f32[2,256]{1,0:T(2,128)S(1)}, f32[2,256]{1,0:T(2,128)}, u32[]{:S(2)}) copy-start(f32[2,256]{1,0:T(2,128)} %copy-done.13) | copy-start | bytes 6148
  8.4 10.6 %copy-start.1 = (bf16[512,512]{1,0:T(8,128)(2,1)S(1)}, bf16[512,512]{1,0:T(8,128)(2,1)}, u32[]{:S(2)}) copy-start(bf16[512,512]{1,0:T(8,128)(2,1)} %wq) | copy-start | bytes 1572868
  8.4 10.6 %collective-permute-start.2 = (bf16[256,512]{1,0:T(8,128)(2,1)S(1)}, bf16[256,512]{1,0:T(8,128)(2,1)S(1)}, u32[]{:S(2)}, u32[]{:S(2)}) collective-permute-start(bf16[256,512]{1,0:T(8,128)(2,1)S(1)} %get-tuple-element.96), channel_id=1, source_target_pairs={{2,0},{4,2},{6,4},{8,6},{10,8},{12,10},{14,12},{16,14},{18,16},{20... | collective-permute-start | bytes 786440 | tf_op jit(solution)/shard_map/ppermute | solution.py:755
  14.2 2.9 %collective-permute-start.3 = (s32[1,32]{1,0:T(1,128)S(1)}, s32[1,32]{1,0:T(1,128)S(1)}, u32[]{:S(2)}, u32[]{:S(2)}) collective-permute-start(s32[1,32]{1,0:T(1,128)S(1)} %get-tuple-element.97), channel_id=1, source_target_pairs={{0,4},{2,6},{4,0},{6,2},{8,12},{10,14},{12,8},{14,10},{16,20},{18,... | collective-permute-start | bytes 392 | tf_op jit(solution)/shard_map/ppermute | solution.py:722
  15.5 2.8 %collective-permute-start.4 = (s32[1,32]{1,0:T(1,128)S(1)}, s32[1,32]{1,0:T(1,128)S(1)}, u32[]{:S(2)}, u32[]{:S(2)}) collective-permute-start(s32[1,32]{1,0:T(1,128)S(1)} %get-tuple-element.98), channel_id=1, source_target_pairs={{0,8},{2,10},{4,12},{6,14},{8,0},{10,2},{12,4},{14,6},{16,24},{18,... | collective-permute-start | bytes 392 | tf_op jit(solution)/shard_map/ppermute | solution.py:722
  15.6 3.4 %collective-permute-start.5 = (s32[1,32]{1,0:T(1,128)S(1)}, s32[1,32]{1,0:T(1,128)S(1)}, u32[]{:S(2)}, u32[]{:S(2)}) collective-permute-start(s32[1,32]{1,0:T(1,128)S(1)} %get-tuple-element.99), channel_id=1, source_target_pairs={{0,16},{2,18},{4,20},{6,22},{8,24},{10,26},{12,28},{14,30},{16,0},... | collective-permute-start | bytes 392 | tf_op jit(solution)/shard_map/ppermute | solution.py:722
  17.1 15.9 %copy-start.3 = (s32[1,32]{1,0:T(1,128)}, s32[1,32]{1,0:T(1,128)S(1)}, u32[]{:S(2)}) copy-start(s32[1,32]{1,0:T(1,128)S(1)} %collective-permute-done.3.refs_0_) | copy-start | bytes 388
  18.3 14.8 %copy-start.5 = (s32[1,32]{1,0:T(1,128)}, s32[1,32]{1,0:T(1,128)S(1)}, u32[]{:S(2)}) copy-start(s32[1,32]{1,0:T(1,128)S(1)} %collective-permute-done.4.refs_1_) | copy-start | bytes 388
  19.0 14.0 %copy-start.7 = (s32[1,32]{1,0:T(1,128)}, s32[1,32]{1,0:T(1,128)S(1)}, u32[]{:S(2)}) copy-start(s32[1,32]{1,0:T(1,128)S(1)} %collective-permute-done.5.refs_2_) | copy-start | bytes 388
  29.2 24.3 %collective-permute-start.6 = (bf16[1024,512]{1,0:T(8,128)(2,1)}, bf16[1024,512]{1,0:T(8,128)(2,1)}, u32[]{:S(2)}, u32[]{:S(2)}) collective-permute-start(bf16[1024,512]{1,0:T(8,128)(2,1)} %get-tuple-element.106), channel_id=1, source_target_pairs={{0,1},{1,0},{2,3},{3,2},{4,5},{5,4},{6,7},{7,6},{8,9},{9,8},{10,11... | collective-permute-start | bytes 3145736 | tf_op jit(solution)/shard_map/ppermute | solution.py:725
  33.0 31.6 %collective-permute-start.8 = (bf16[1024,512]{1,0:T(8,128)(2,1)}, bf16[1024,512]{1,0:T(8,128)(2,1)}, u32[]{:S(2)}, u32[]{:S(2)}) collective-permute-start(bf16[1024,512]{1,0:T(8,128)(2,1)} %get-tuple-element.131), channel_id=1, source_target_pairs={{0,16},{2,10},{4,20},{6,14},{8,24},{10,2},{12,28},{14,6},{16,0},{1... | collective-permute-start | bytes 3145736 | tf_op jit(solution)/shard_map/ppermute | solution.py:722
  34.1 30.6 %collective-permute-start.9 = (bf16[1024,512]{1,0:T(8,128)(2,1)}, bf16[1024,512]{1,0:T(8,128)(2,1)}, u32[]{:S(2)}, u32[]{:S(2)}) collective-permute-start(bf16[1024,512]{1,0:T(8,128)(2,1)} %get-tuple-element.132), channel_id=1, source_target_pairs={{0,4},{2,6},{4,0},{6,2},{8,12},{10,14},{12,8},{14,10},{16,20},{18,... | collective-permute-start | bytes 3145736 | tf_op jit(solution)/shard_map/ppermute | solution.py:722
  34.3 27.2 %copy-start.4 = (s32[1,32]{1,0:T(1,128)S(1)}, s32[1,32]{1,0:T(1,128)}, u32[]{:S(2)}) copy-start(s32[1,32]{1,0:T(1,128)} %copy-done.3) | copy-start | bytes 388
  34.3 27.2 %copy-start.6 = (s32[1,32]{1,0:T(1,128)S(1)}, s32[1,32]{1,0:T(1,128)}, u32[]{:S(2)}) copy-start(s32[1,32]{1,0:T(1,128)} %copy-done.5) | copy-start | bytes 388
  34.3 27.2 %copy-start.8 = (s32[1,32]{1,0:T(1,128)S(1)}, s32[1,32]{1,0:T(1,128)}, u32[]{:S(2)}) copy-start(s32[1,32]{1,0:T(1,128)} %copy-done.7) | copy-start | bytes 388
  53.5 14.6 %collective-permute-start.11 = (bf16[256,512]{1,0:T(8,128)(2,1)S(1)}, bf16[256,512]{1,0:T(8,128)(2,1)S(1)}, u32[]{:S(2)}, u32[]{:S(2)}) collective-permute-start(bf16[256,512]{1,0:T(8,128)(2,1)S(1)} %get-tuple-element.136), channel_id=1, source_target_pairs={{0,2},{2,4},{4,6},{6,8},{8,10},{10,12},{12,14},{14,16},{16,18},{18... | collective-permute-start | bytes 786440 | tf_op jit(solution)/shard_map/ppermute | solution.py:792
  57.1 7.7 %collective-permute-start.10 = (s32[1,32]{1,0:T(1,128)S(1)}, s32[1,32]{1,0:T(1,128)S(1)}, u32[]{:S(2)}, u32[]{:S(2)}) collective-permute-start(s32[1,32]{1,0:T(1,128)S(1)} %get-tuple-element.135), channel_id=1, source_target_pairs={{0,2},{2,0},{4,6},{6,4},{8,10},{10,8},{12,14},{14,12},{16,18},{18,... | collective-permute-start | bytes 392 | tf_op jit(solution)/shard_map/ppermute | solution.py:722
  57.2 38.3 %collective-permute-start.7 = (bf16[1024,512]{1,0:T(8,128)(2,1)}, bf16[1024,512]{1,0:T(8,128)(2,1)}, u32[]{:S(2)}, u32[]{:S(2)}) collective-permute-start(bf16[1024,512]{1,0:T(8,128)(2,1)} %get-tuple-element.126), channel_id=1, source_target_pairs={{0,8},{2,18},{4,12},{6,22},{8,0},{10,26},{12,4},{14,30},{16,24},{1... | collective-permute-start | bytes 3145736 | tf_op jit(solution)/shard_map/ppermute | solution.py:722
  64.6 34.3 %collective-permute-start.15 = (bf16[1024,512]{1,0:T(8,128)(2,1)}, bf16[1024,512]{1,0:T(8,128)(2,1)}, u32[]{:S(2)}, u32[]{:S(2)}) collective-permute-start(bf16[1024,512]{1,0:T(8,128)(2,1)} %get-tuple-element.153), channel_id=1, source_target_pairs={{0,4},{2,6},{4,0},{6,2},{8,12},{10,14},{12,8},{14,10},{16,20},{18,... | collective-permute-start | bytes 3145736 | tf_op jit(solution)/shard_map/ppermute | solution.py:722
  64.7 34.2 %collective-permute-start.16 = (bf16[1024,512]{1,0:T(8,128)(2,1)}, bf16[1024,512]{1,0:T(8,128)(2,1)}, u32[]{:S(2)}, u32[]{:S(2)}) collective-permute-start(bf16[1024,512]{1,0:T(8,128)(2,1)} %collective-permute-done.8.refs_1_), channel_id=1, source_target_pairs={{0,1},{1,0},{2,3},{3,2},{4,5},{5,4},{6,7},{7,6},{8,9},{9,8},{10,11... | collective-permute-start | bytes 3145736 | tf_op jit(solution)/shard_map/ppermute | solution.py:725
  68.1 17.7 %collective-permute-start.12 = (bf16[2048,512]{1,0:T(8,128)(2,1)}, bf16[2048,512]{1,0:T(8,128)(2,1)}, u32[]{:S(2)}, u32[]{:S(2)}) collective-permute-start(bf16[2048,512]{1,0:T(8,128)(2,1)} %shard_map.89), channel_id=1, source_target_pairs={{0,2},{2,0},{4,6},{6,4},{8,10},{10,8},{12,14},{14,12},{16,18},{18,... | collective-permute-start | bytes 6291464 | tf_op jit(solution)/shard_map/ppermute | solution.py:722
  71.8 14.0 %copy-start.2 = (s32[1,4,16]{2,1,0:T(4,128)S(1)}, s32[1,4,16]{2,1,0:T(4,128)}, u32[]{:S(2)}) copy-start(s32[1,4,16]{2,1,0:T(4,128)} %param.14) | copy-start | bytes 772
  95.5 16.1 %collective-permute-start.13 = (bf16[1024,512]{1,0:T(8,128)(2,1)S(1)}, bf16[1024,512]{1,0:T(8,128)(2,1)S(1)}, u32[]{:S(2)}, u32[]{:S(2)}) collective-permute-start(bf16[1024,512]{1,0:T(8,128)(2,1)S(1)} %get-tuple-element.150), channel_id=1, source_target_pairs={{0,8},{4,12},{8,0},{12,4},{16,24},{20,28},{24,16},{28,20},{1,9},{5... | collective-permute-start | bytes 3145736 | tf_op jit(solution)/shard_map/ppermute | solution.py:818
  96.3 16.0 %collective-permute-start.14 = (bf16[1024,512]{1,0:T(8,128)(2,1)}, bf16[1024,512]{1,0:T(8,128)(2,1)S(1)}, u32[]{:S(2)}, u32[]{:S(2)}) collective-permute-start(bf16[1024,512]{1,0:T(8,128)(2,1)} %collective-permute-done.7.refs_1_), channel_id=1, source_target_pairs={{2,3},{3,2},{6,7},{7,6},{10,11},{11,10},{14,15},{15,14},{18,19},{1... | collective-permute-start | bytes 3145736 | tf_op jit(solution)/shard_map/ppermute | solution.py:820

commit v6 on v5

--- a/solution.py
+++ b/solution.py
@@ -331,7 +331,7 @@
         ],
         compiler_params=pltpu.CompilerParams(vmem_limit_bytes=24 * MIB),
         cost_estimate=pl.CostEstimate(
-            flops=10**12, bytes_accessed=10**5, transcendentals=0
+            flops=10**12 if own else 10**8, bytes_accessed=10**5, transcendentals=0
         ),
     )(*tables, *pieces, w, local_q, num, den, *own)
 
@@ -473,7 +473,7 @@
         + [pltpu.VMEM((2 * LANES, width), jnp.bfloat16)],
         compiler_params=pltpu.CompilerParams(vmem_limit_bytes=24 * MIB),
         cost_estimate=pl.CostEstimate(
-            flops=10**8 if gives_out else 10**12, bytes_accessed=own_rows * width, transcendentals=0
+            flops=own_rows * width * 256, bytes_accessed=own_rows * width, transcendentals=0
         ),
     )(*arguments, *([out] if last else []))
 
@@ -792,12 +792,12 @@
         other_halo = lax.ppermute(edge_rows, ("node", "head"), outward)
         wanted_pair = swap(wanted_pair, 0)
         sources = [features, first_half, second_half]
-        late, direct = select(place, ((0, 0, (1,)), (1, 1, (1,))), share, wanted, sources)
+        jobs = ((1, 1, (1,)), (2, 2, (1,)), (0, 0, (0, 1)))
+        late, direct, pair = select(place, jobs, share, [wanted_pair] + wanted, sources)
         num, first, early, late = lax.optimization_barrier((num, first, early, late))
         second = swap(second, 2, 3)
         first_beside = other(first)
         late = swap(late, 1)
-        (pair,) = select(place, ((0, 0, (0, 1)),), share, [wanted_pair], sources)
         num, pair, other_halo = lax.optimization_barrier((num, pair, other_halo))
         pair = swap(pair, 0)
         num, den = more_attention(

time: 120 us -> 117 us (0.975)
  Pallas kernels: 85.1 us -> 82.1 us
    pallas_call x3 -> x2, Pallas kernels: 10.1 us -> 5.92 us  [select(): pl.pallas_call(functools.partial(select_kernel, jobs, share, len(parts),...]
    ppermute x9, starting transfers between devices: 11 us -> 7.14 us  [swap(): lax.ppermute(x, 'node', [(i, i ^ flip[i % 2]) for i in range(blocks)])]
    ppermute x4, waiting for transfers between devices: 2.8 us -> 0.54 us  [other(): return lax.ppermute(x, 'head', [(0, 1), (1, 0)])]
    ppermute x4, starting transfers between devices: 1.84 us -> 4.03 us  [other(): return lax.ppermute(x, 'head', [(0, 1), (1, 0)])]
    pallas_call x2, Pallas kernels: 30.4 us -> 32.5 us  [more_attention(): pl.pallas_call(functools.partial(more_kernel, len(pieces), bool(own), spl...]
    ppermute x1, starting transfers between devices: 2.69 us -> 4.35 us  [local(): second_beside = lax.ppermute(second, ('node', 'head'), sides)]
    ppermute x9, waiting for transfers between devices: 3.24 us -> 4.57 us  [swap(): lax.ppermute(x, 'node', [(i, i ^ flip[i % 2]) for i in range(blocks)])]
    pallas_call x1, Pallas kernels: 10.2 us -> 8.89 us  [own_attention(): pl.pallas_call(functools.partial(own_kernel, split), in_specs=[SMEM] * 3...]
  transfers between devices with their start and end apart: 17 -> 17, of which waited for: 5 -> 8; matrix products, arithmetic and copies ran while one was open for 1% -> 1% of each run, Pallas kernels for 66% -> 65%
where the time goes in v6:
time: 117 us; the launch traced here: 116 us
  Pallas kernels  82.1 us (70%)
  starting transfers between devices  24.1 us (21%)
  waiting for transfers between devices  6.38 us (5%)
  local copies, waits for them, and re-layouts  1.63 us (1%)
    pallas_call x2, Pallas kernels, more_attention(): pl.pallas_call(functools.partial(more_kernel, len(pieces), bool(own), spl...  32.5 us
    pallas_call x3, Pallas kernels, expand_attention(): pl.pallas_call(functools.partial(expand_kernel, len(sources), gives_out,...  29 us
    pallas_call x1, Pallas kernels, own_attention(): pl.pallas_call(functools.partial(own_kernel, split), in_specs=[SMEM] * 3...  8.89 us
    ppermute x9, starting transfers between devices, swap(): lax.ppermute(x, 'node', [(i, i ^ flip[i % 2]) for i in range(blocks)])  7.14 us
    pallas_call x2, Pallas kernels, select(): pl.pallas_call(functools.partial(select_kernel, jobs, share, len(parts),...  5.92 us
    ppermute x9, waiting for transfers between devices, swap(): lax.ppermute(x, 'node', [(i, i ^ flip[i % 2]) for i in range(blocks)])  4.57 us
    ppermute x1, starting transfers between devices, local(): second_beside = lax.ppermute(second, ('node', 'head'), sides)  4.35 us
    ppermute x1, starting transfers between devices, local(): halo = lax.ppermute(edge_rows, ('node', 'head'), inward)  4.14 us
  transfers between devices with their start and end apart: 17, of which 8 were waited for; matrix products, arithmetic and copies ran while one was open for 1% of the time, Pallas kernels for 65%

profile of v6, /device:TPU:25, one launch (start us, length us, event | category | flops | bytes accessed | tf_op | source)
XLA Modules:
  0.0 115.6 jit_solution(14315248857108366515)
XLA Ops:
  0.0 0.9 pad_maximum_fusion
  0.9 1.2 %collective-permute-start = (f32[2,256]{1,0:T(2,128)S(1)}, f32[2,256]{1,0:T(2,128)S(1)}, u32[]{:S(2)}, u32[]{:S(2)}) collective-permute-start(f32[2,256]{1,0:T(2,128)S(1)} %pad_maximum_fusion), channel_id=1, source_target_pairs={{0,1},{1,0},{2,3},{3,2},{4,5},{5,4},{6,7},{7,6},{8,9},{9,8},{10,11... | collective-permute-start | bytes 6152 | tf_op jit(solution)/shard_map/ppermute | solution.py:725
  2.1 2.0 %shard_map.82 = bf16[1024,512]{1,0:T(8,128)(2,1)} custom-call(s32[1]{0:T(128)} %bitcast.here_ref, bf16[2048,512]{1,0:T(8,128)(2,1)} %refs_4_), custom_call_target="tpu_custom_call" | custom-call | tf_op jit(solution)/shard_map/pallas_call | solution.py:507
  4.1 0.4 collective-permute-start.1
  4.5 1.1 shard_map.84
  5.7 2.7 %shard_map.83 = (s32[2]{0:T(128)S(1)}, s32[2,36]{1,0:T(2,128)S(1)}, s32[2,36]{1,0:T(2,128)S(1)}, s32[2,36]{1,0:T(2,128)S(1)}, s32[4,16]{1,0:T(4,128)S(1)}, /*ind...) custom-call(s32[1]{0:T(128)} %bitcast.here_ref, ...), custom_call_target="tpu_custom_call" | custom-call | flops 99999997952 | bytes 4096 | tf_op jit(solution)/shard_map/pallas_call | solution.py:694
  8.4 4.1 %collective-permute-start.2 = (bf16[256,512]{1,0:T(8,128)(2,1)S(1)}, bf16[256,512]{1,0:T(8,128)(2,1)S(1)}, u32[]{:S(2)}, u32[]{:S(2)}) collective-permute-start(bf16[256,512]{1,0:T(8,128)(2,1)S(1)} %get-tuple-element.97), channel_id=1, source_target_pairs={{2,0},{4,2},{6,4},{8,6},{10,8},{12,10},{14,12},{16,14},{18,16},{20... | collective-permute-start | bytes 786440 | tf_op jit(solution)/shard_map/ppermute | solution.py:755
  12.8 1.4 %copy.14 = bf16[512,2,512]{2,0,1:T(8,128)(2,1)S(1)} copy(bf16[512,2,512]{2,1,0:T(2,128)(2,1)} %param.10) | data formatting | bytes 2097152 | tf_op jit(solution)/shard_map/optimization_barrier | solution.py:739
  14.2 1.3 %collective-permute-start.3 = (s32[1,32]{1,0:T(1,128)S(1)}, s32[1,32]{1,0:T(1,128)S(1)}, u32[]{:S(2)}, u32[]{:S(2)}) collective-permute-start(s32[1,32]{1,0:T(1,128)S(1)} %get-tuple-element.98), channel_id=1, source_target_pairs={{0,4},{2,6},{4,0},{6,2},{8,12},{10,14},{12,8},{14,10},{16,20},{18,... | collective-permute-start | bytes 392 | tf_op jit(solution)/shard_map/ppermute | solution.py:722
  15.8 1.3 %collective-permute-done.3.refs_0_.refs_1_ = s32[1,32]{1,0:T(1,128)S(1)} collective-permute-done((s32[1,32]{1,0:T(1,128)S(1)}, s32[1,32]{1,0:T(1,128)S(1)}, u32[]{:S(2)}, u32[]{:S(2)}) %collective-permute-start.3) | collective-permute-done | bytes 160 | tf_op jit(solution)/shard_map/ppermute | solution.py:722
  17.1 1.2 collective-permute-done.4.refs_1_.refs_2_
  18.3 0.7 collective-permute-done.5.refs_2_.refs_3_
  19.0 8.9 %shard_map.85 = (f32[2176,512]{1,0:T(8,128)S(1)}, f32[2176,128]{1,0:T(8,128)S(1)}, bf16[16,512,128]{2,1,0:T(8,128)(2,1)S(1)}, bf16[16,128,512]{2,1,0:T(8,128)(2,...) custom-call(s32[2]{0:T(128)S(1)} %get-tuple-element.84.place_ref, s32[256]{0:T(256)S(1)} %reshape.11.cols_ref, ...), custom_call_target="tpu_custom_call" | custom-call | flops 100000000 | bytes 100000 | tf_op jit(solution)/shard_map/pallas_call | solution.py:307
  27.9 0.3 collective-permute-done.1.refs_4_.refs_0_.refs_5_
  28.2 2.2 %collective-permute-start.6 = (bf16[1024,512]{1,0:T(8,128)(2,1)}, bf16[1024,512]{1,0:T(8,128)(2,1)}, u32[]{:S(2)}, u32[]{:S(2)}) collective-permute-start(bf16[1024,512]{1,0:T(8,128)(2,1)} %get-tuple-element.107), channel_id=1, source_target_pairs={{0,1},{1,0},{2,3},{3,2},{4,5},{5,4},{6,7},{7,6},{8,9},{9,8},{10,11... | collective-permute-start | bytes 3145736 | tf_op jit(solution)/shard_map/ppermute | solution.py:725
  30.4 3.3 %shard_map.86 = (bf16[1024,512]{1,0:T(8,128)(2,1)}, bf16[1024,512]{1,0:T(8,128)(2,1)S(1)}, bf16[1024,512]{1,0:T(8,128)(2,1)}, bf16[256,512]{1,0:T(8,128)(2,1)S(1)}) custom-call(s32[2]{0:T(128)S(1)} %get-tuple-element.84.place_ref, s32[1,32]{1,0:T(1,128)S(1)} %collective-permute-done.3.refs_0_.refs_1_, s32[1,32]{1,0:T(1,128)S(1)} %collective-permute-done.4.refs_1_.refs_2_, ...), custom_call_target="tpu_custom_call" | custom-call | flops 1000 | bytes 1000 | tf_op jit(solution)/shard_map/pallas_call | solution.py:599
  33.8 0.4 collective-permute-start.10
  34.3 18.8 %shard_map.87 = (f32[2176,512]{1,0:T(8,128)S(1)}, f32[2176,128]{1,0:T(8,128)S(1)}) custom-call(s32[2]{0:T(128)S(1)} %get-tuple-element.84.place_ref, s32[256]{0:T(256)S(1)} %reshape.11.cols_ref, s32[2,36]{1,0:T(2,128)S(1)} %get-tuple-element.108.where_ref, bf16[1024,512]{1,0:T(8,128)(2,1)} %collective-permute-done.1.refs_4_.refs_0_.refs_5_, ...), custom_call_target="tpu_custom_call" | custom-call | flops 999999995904 | bytes 100000 | tf_op jit(solution)/shard_map/pallas_call | solution.py:322
  53.1 0.2 collective-permute-done.6.refs_6_.refs_0_
  53.3 3.7 %collective-permute-start.11 = (bf16[256,512]{1,0:T(8,128)(2,1)S(1)}, bf16[256,512]{1,0:T(8,128)(2,1)S(1)}, u32[]{:S(2)}, u32[]{:S(2)}) collective-permute-start(bf16[256,512]{1,0:T(8,128)(2,1)S(1)} %get-tuple-element.138), channel_id=1, source_target_pairs={{0,2},{2,4},{4,6},{6,8},{8,10},{10,12},{12,14},{14,16},{16,18},{18... | collective-permute-start | bytes 786440 | tf_op jit(solution)/shard_map/ppermute | solution.py:792
  57.2 1.1 collective-permute-done.8.refs_0_
  58.3 2.6 %shard_map.88 = (bf16[1024,512]{1,0:T(8,128)(2,1)S(1)}, bf16[1024,512]{1,0:T(8,128)(2,1)S(1)}, bf16[2048,512]{1,0:T(8,128)(2,1)S(1)}) custom-call(s32[2]{0:T(128)S(1)} %get-tuple-element.84.place_ref, s32[1,32]{1,0:T(1,128)S(1)} %collective-permute-done.8.refs_0_, s32[1,32]{1,0:T(1,128)S(1)} %copy-done.4, s32[1,32]{1,0:T(1,128)S(1)} %copy-done.6, ...), custom_call_target="tpu_custom_call" | custom-call | flops 1000 | bytes 1000 | tf_op jit(solution)/shard_map/pallas_call | solution.py:599
  60.9 4.1 %collective-permute-start.12 = (bf16[2048,512]{1,0:T(8,128)(2,1)S(1)}, bf16[2048,512]{1,0:T(8,128)(2,1)S(1)}, u32[]{:S(2)}, u32[]{:S(2)}) collective-permute-start(bf16[2048,512]{1,0:T(8,128)(2,1)S(1)} %get-tuple-element.139), channel_id=1, source_target_pairs={{0,2},{2,0},{4,6},{6,4},{8,10},{10,8},{12,14},{14,12},{16,18},{18,... | collective-permute-start | bytes 6291464 | tf_op jit(solution)/shard_map/ppermute | solution.py:722
  65.0 0.9 collective-permute-start.7
  66.1 13.7 %shard_map.89 = (f32[2176,512]{1,0:T(8,128)S(1)}, f32[2176,128]{1,0:T(8,128)S(1)}) custom-call(s32[2]{0:T(128)S(1)} %get-tuple-element.84.place_ref, s32[256]{0:T(256)S(1)} %reshape.11.cols_ref, s32[2,36]{1,0:T(2,128)S(1)} %get-tuple-element.143.where_ref, bf16[1024,512]{1,0:T(8,128)(2,1)} %collective-permute-done.6.refs_6_.refs_0_, ...), custom_call_target="tpu_custom_call" | custom-call | flops 100000000 | bytes 100000 | tf_op jit(solution)/shard_map/pallas_call | solution.py:322
  79.8 10.7 %shard_map.90 = (f32[2176,512]{1,0:T(8,128)S(1)}, f32[2176,128]{1,0:T(8,128)S(1)}) custom-call(s32[2]{0:T(128)S(1)} %get-tuple-element.84.place_ref, s32[4,16]{1,0:T(4,128)S(1)} %bitcast.15, s32[4,16]{1,0:T(4,128)S(1)} %get-tuple-element.131.spots_ref, bf16[2048,512]{1,0:T(8,128)(2,1)S(1)} %collective-permute-done.12.refs_0_, ...), custom_call_target="tpu_custom_call" | custom-call | flops 268435456 | bytes 1048576 | tf_op jit(solution)/shard_map/pallas_call | solution.py:450
  90.5 0.2 collective-permute-done.7.refs_1_
  90.8 0.7 collective-permute-start.13
  91.5 4.3 %collective-permute-start.14 = (bf16[1024,512]{1,0:T(8,128)(2,1)S(1)}, bf16[1024,512]{1,0:T(8,128)(2,1)S(1)}, u32[]{:S(2)}, u32[]{:S(2)}) collective-permute-start(bf16[1024,512]{1,0:T(8,128)(2,1)S(1)} %collective-permute-done.7.refs_1_), channel_id=1, source_target_pairs={{2,3},{3,2},{6,7},{7,6},{10,11},{11,10},{14,15},{15,14},{18,19},{1... | collective-permute-start | bytes 3145736 | tf_op jit(solution)/shard_map/ppermute | solution.py:820
  95.9 10.9 %shard_map.91 = (f32[2176,512]{1,0:T(8,128)S(1)}, f32[2176,128]{1,0:T(8,128)S(1)}, bf16[2048,512]{1,0:T(8,128)(2,1)}) custom-call(s32[2]{0:T(128)S(1)} %get-tuple-element.84.place_ref, s32[4,16]{1,0:T(4,128)S(1)} %bitcast.16, s32[4,16]{1,0:T(4,128)S(1)} %get-tuple-element.154.spots_ref, bf16[1024,512]{1,0:T(8,128)(2,1)S(1)} %collective-permute-done.15.refs_0_, ...), custom_call_target="tpu_custom_call" | custom-call | flops 268435456 | bytes 1048576 | tf_op jit(solution)/shard_map/pallas_call | solution.py:450
  106.8 1.3 %collective-permute-done.14.refs_1_ = bf16[1024,512]{1,0:T(8,128)(2,1)S(1)} collective-permute-done((bf16[1024,512]{1,0:T(8,128)(2,1)S(1)}, bf16[1024,512]{1,0:T(8,128)(2,1)S(1)}, u32[]{:S(2)}, u32[]{:S(2)}) %collective-permute-start.14) | collective-permute-done | bytes 1048608 | tf_op jit(solution)/shard_map/ppermute | solution.py:820
  108.0 7.4 %shard_map.92 = bf16[2048,512]{1,0:T(8,128)(2,1)} custom-call(s32[2]{0:T(128)S(1)} %get-tuple-element.84.place_ref, s32[4,16]{1,0:T(4,128)S(1)} %bitcast.17, s32[4,16]{1,0:T(4,128)S(1)} %get-tuple-element.85.spots_ref, bf16[1024,512]{1,0:T(8,128)(2,1)S(1)} %collective-permute-done.13.refs_0_, ...), custom_call_target="tpu_custom_call", output_to_operand_aliasing={{}: (9, {})} | custom-call | flops 268435456 | bytes 1048576 | tf_op jit(solution)/shard_map/pallas_call | solution.py:450
  (48 shorter events, 0.8 us)
Async XLA Ops:
  0.0 4.5 %copy-start = (bf16[2048,512]{1,0:T(8,128)(2,1)S(1)}, bf16[2048,512]{1,0:T(8,128)(2,1)}, u32[]{:S(2)}) copy-start(bf16[2048,512]{1,0:T(8,128)(2,1)} %refs_4_) | copy-start | bytes 6291460
  0.9 3.2 %collective-permute-start = (f32[2,256]{1,0:T(2,128)S(1)}, f32[2,256]{1,0:T(2,128)S(1)}, u32[]{:S(2)}, u32[]{:S(2)}) collective-permute-start(f32[2,256]{1,0:T(2,128)S(1)} %pad_maximum_fusion), channel_id=1, source_target_pairs={{0,1},{1,0},{2,3},{3,2},{4,5},{5,4},{6,7},{7,6},{8,9},{9,8},{10,11... | collective-permute-start | bytes 6152 | tf_op jit(solution)/shard_map/ppermute | solution.py:725
  4.1 1.5 %copy-start.13 = (f32[2,256]{1,0:T(2,128)}, f32[2,256]{1,0:T(2,128)S(1)}, u32[]{:S(2)}) copy-start(f32[2,256]{1,0:T(2,128)S(1)} %collective-permute-done) | copy-start | bytes 6148
  4.1 1.5 %copy-start.9 = (s32[1,4,16]{2,1,0:T(4,128)S(1)}, s32[1,4,16]{2,1,0:T(4,128)}, u32[]{:S(2)}) copy-start(s32[1,4,16]{2,1,0:T(4,128)} %param.15) | copy-start | bytes 772
  4.1 24.1 %collective-permute-start.1 = (bf16[1024,512]{1,0:T(8,128)(2,1)}, bf16[1024,512]{1,0:T(8,128)(2,1)}, u32[]{:S(2)}, u32[]{:S(2)}) collective-permute-start(bf16[1024,512]{1,0:T(8,128)(2,1)} %shard_map.82), channel_id=1, source_target_pairs={{0,1},{1,0},{2,3},{3,2},{4,5},{5,4},{6,7},{7,6},{8,9},{9,8},{10,11... | collective-permute-start | bytes 3145736 | tf_op jit(solution)/shard_map/ppermute | solution.py:725
  5.6 7.0 %copy-start.10 = (s32[32,8]{0,1:T(8,128)S(1)}, s32[32,8]{0,1:T(8,128)}, u32[]{:S(2)}) copy-start(s32[32,8]{0,1:T(8,128)} %param.13) | copy-start | bytes 3076
  8.4 7.2 %copy-start.11 = (f32[256]{0:T(256)S(1)}, f32[256]{0:T(256)}, u32[]{:S(2)}) copy-start(f32[256]{0:T(256)} %param.12) | copy-start | bytes 3076
  8.4 7.2 %copy-start.12 = (f32[256]{0:T(256)S(1)}, f32[256]{0:T(256)}, u32[]{:S(2)}) copy-start(f32[256]{0:T(256)} %param.11) | copy-start | bytes 3076
  8.4 7.2 %copy-start.14 = (f32[2,256]{1,0:T(2,128)S(1)}, f32[2,256]{1,0:T(2,128)}, u32[]{:S(2)}) copy-start(f32[2,256]{1,0:T(2,128)} %copy-done.13) | copy-start | bytes 6148
  8.4 10.6 %copy-start.1 = (bf16[512,512]{1,0:T(8,128)(2,1)S(1)}, bf16[512,512]{1,0:T(8,128)(2,1)}, u32[]{:S(2)}) copy-start(bf16[512,512]{1,0:T(8,128)(2,1)} %wq) | copy-start | bytes 1572868
  8.4 10.6 %collective-permute-start.2 = (bf16[256,512]{1,0:T(8,128)(2,1)S(1)}, bf16[256,512]{1,0:T(8,128)(2,1)S(1)}, u32[]{:S(2)}, u32[]{:S(2)}) collective-permute-start(bf16[256,512]{1,0:T(8,128)(2,1)S(1)} %get-tuple-element.97), channel_id=1, source_target_pairs={{2,0},{4,2},{6,4},{8,6},{10,8},{12,10},{14,12},{16,14},{18,16},{20... | collective-permute-start | bytes 786440 | tf_op jit(solution)/shard_map/ppermute | solution.py:755
  14.2 2.9 %collective-permute-start.3 = (s32[1,32]{1,0:T(1,128)S(1)}, s32[1,32]{1,0:T(1,128)S(1)}, u32[]{:S(2)}, u32[]{:S(2)}) collective-permute-start(s32[1,32]{1,0:T(1,128)S(1)} %get-tuple-element.98), channel_id=1, source_target_pairs={{0,4},{2,6},{4,0},{6,2},{8,12},{10,14},{12,8},{14,10},{16,20},{18,... | collective-permute-start | bytes 392 | tf_op jit(solution)/shard_map/ppermute | solution.py:722
  15.5 2.8 %collective-permute-start.4 = (s32[1,32]{1,0:T(1,128)S(1)}, s32[1,32]{1,0:T(1,128)S(1)}, u32[]{:S(2)}, u32[]{:S(2)}) collective-permute-start(s32[1,32]{1,0:T(1,128)S(1)} %get-tuple-element.99), channel_id=1, source_target_pairs={{0,8},{2,10},{4,12},{6,14},{8,0},{10,2},{12,4},{14,6},{16,24},{18,... | collective-permute-start | bytes 392 | tf_op jit(solution)/shard_map/ppermute | solution.py:722
  15.6 3.4 %collective-permute-start.5 = (s32[1,32]{1,0:T(1,128)S(1)}, s32[1,32]{1,0:T(1,128)S(1)}, u32[]{:S(2)}, u32[]{:S(2)}) collective-permute-start(s32[1,32]{1,0:T(1,128)S(1)} %get-tuple-element.100), channel_id=1, source_target_pairs={{0,16},{2,18},{4,20},{6,22},{8,24},{10,26},{12,28},{14,30},{16,0},... | collective-permute-start | bytes 392 | tf_op jit(solution)/shard_map/ppermute | solution.py:722
  17.1 16.7 %copy-start.3 = (s32[1,32]{1,0:T(1,128)}, s32[1,32]{1,0:T(1,128)S(1)}, u32[]{:S(2)}) copy-start(s32[1,32]{1,0:T(1,128)S(1)} %collective-permute-done.3.refs_0_.refs_1_) | copy-start | bytes 388
  18.3 15.5 %copy-start.5 = (s32[1,32]{1,0:T(1,128)}, s32[1,32]{1,0:T(1,128)S(1)}, u32[]{:S(2)}) copy-start(s32[1,32]{1,0:T(1,128)S(1)} %collective-permute-done.4.refs_1_.refs_2_) | copy-start | bytes 388
  19.0 14.8 %copy-start.7 = (s32[1,32]{1,0:T(1,128)}, s32[1,32]{1,0:T(1,128)S(1)}, u32[]{:S(2)}) copy-start(s32[1,32]{1,0:T(1,128)S(1)} %collective-permute-done.5.refs_2_.refs_3_) | copy-start | bytes 388
  28.2 25.1 %collective-permute-start.6 = (bf16[1024,512]{1,0:T(8,128)(2,1)}, bf16[1024,512]{1,0:T(8,128)(2,1)}, u32[]{:S(2)}, u32[]{:S(2)}) collective-permute-start(bf16[1024,512]{1,0:T(8,128)(2,1)} %get-tuple-element.107), channel_id=1, source_target_pairs={{0,1},{1,0},{2,3},{3,2},{4,5},{5,4},{6,7},{7,6},{8,9},{9,8},{10,11... | collective-permute-start | bytes 3145736 | tf_op jit(solution)/shard_map/ppermute | solution.py:725
  33.8 27.1 %collective-permute-start.9 = (bf16[1024,512]{1,0:T(8,128)(2,1)}, bf16[1024,512]{1,0:T(8,128)(2,1)}, u32[]{:S(2)}, u32[]{:S(2)}) collective-permute-start(bf16[1024,512]{1,0:T(8,128)(2,1)} %get-tuple-element.133), channel_id=1, source_target_pairs={{0,16},{2,10},{4,20},{6,14},{8,24},{10,2},{12,28},{14,6},{16,0},{1... | collective-permute-start | bytes 3145736 | tf_op jit(solution)/shard_map/ppermute | solution.py:722
  33.8 27.1 %collective-permute-start.10 = (bf16[1024,512]{1,0:T(8,128)(2,1)}, bf16[1024,512]{1,0:T(8,128)(2,1)}, u32[]{:S(2)}, u32[]{:S(2)}) collective-permute-start(bf16[1024,512]{1,0:T(8,128)(2,1)} %get-tuple-element.134), channel_id=1, source_target_pairs={{0,4},{2,6},{4,0},{6,2},{8,12},{10,14},{12,8},{14,10},{16,20},{18,... | collective-permute-start | bytes 3145736 | tf_op jit(solution)/shard_map/ppermute | solution.py:722
  34.3 24.0 %copy-start.4 = (s32[1,32]{1,0:T(1,128)S(1)}, s32[1,32]{1,0:T(1,128)}, u32[]{:S(2)}) copy-start(s32[1,32]{1,0:T(1,128)} %copy-done.3) | copy-start | bytes 388
  34.3 24.0 %copy-start.6 = (s32[1,32]{1,0:T(1,128)S(1)}, s32[1,32]{1,0:T(1,128)}, u32[]{:S(2)}) copy-start(s32[1,32]{1,0:T(1,128)} %copy-done.5) | copy-start | bytes 388
  34.3 24.0 %copy-start.8 = (s32[1,32]{1,0:T(1,128)S(1)}, s32[1,32]{1,0:T(1,128)}, u32[]{:S(2)}) copy-start(s32[1,32]{1,0:T(1,128)} %copy-done.7) | copy-start | bytes 388
  53.3 7.6 %collective-permute-start.11 = (bf16[256,512]{1,0:T(8,128)(2,1)S(1)}, bf16[256,512]{1,0:T(8,128)(2,1)S(1)}, u32[]{:S(2)}, u32[]{:S(2)}) collective-permute-start(bf16[256,512]{1,0:T(8,128)(2,1)S(1)} %get-tuple-element.138), channel_id=1, source_target_pairs={{0,2},{2,4},{4,6},{6,8},{8,10},{10,12},{12,14},{14,16},{16,18},{18... | collective-permute-start | bytes 786440 | tf_op jit(solution)/shard_map/ppermute | solution.py:792
  57.1 1.2 %collective-permute-start.8 = (s32[1,32]{1,0:T(1,128)S(1)}, s32[1,32]{1,0:T(1,128)S(1)}, u32[]{:S(2)}, u32[]{:S(2)}) collective-permute-start(s32[1,32]{1,0:T(1,128)S(1)} %get-tuple-element.128), channel_id=1, source_target_pairs={{0,2},{2,0},{4,6},{6,4},{8,10},{10,8},{12,14},{14,12},{16,18},{18,... | collective-permute-start | bytes 392 | tf_op jit(solution)/shard_map/ppermute | solution.py:722
  60.9 18.9 %collective-permute-start.12 = (bf16[2048,512]{1,0:T(8,128)(2,1)S(1)}, bf16[2048,512]{1,0:T(8,128)(2,1)S(1)}, u32[]{:S(2)}, u32[]{:S(2)}) collective-permute-start(bf16[2048,512]{1,0:T(8,128)(2,1)S(1)} %get-tuple-element.139), channel_id=1, source_target_pairs={{0,2},{2,0},{4,6},{6,4},{8,10},{10,8},{12,14},{14,12},{16,18},{18,... | collective-permute-start | bytes 6291464 | tf_op jit(solution)/shard_map/ppermute | solution.py:722
  65.0 25.8 %collective-permute-start.7 = (bf16[1024,512]{1,0:T(8,128)(2,1)S(1)}, bf16[1024,512]{1,0:T(8,128)(2,1)S(1)}, u32[]{:S(2)}, u32[]{:S(2)}) collective-permute-start(bf16[1024,512]{1,0:T(8,128)(2,1)S(1)} %get-tuple-element.127), channel_id=1, source_target_pairs={{0,8},{2,18},{4,12},{6,22},{8,0},{10,26},{12,4},{14,30},{16,24},{1... | collective-permute-start | bytes 3145736 | tf_op jit(solution)/shard_map/ppermute | solution.py:722
  65.9 29.9 %collective-permute-start.15 = (bf16[1024,512]{1,0:T(8,128)(2,1)S(1)}, bf16[1024,512]{1,0:T(8,128)(2,1)S(1)}, u32[]{:S(2)}, u32[]{:S(2)}) collective-permute-start(bf16[1024,512]{1,0:T(8,128)(2,1)S(1)} %get-tuple-element.155), channel_id=1, source_target_pairs={{0,4},{2,6},{4,0},{6,2},{8,12},{10,14},{12,8},{14,10},{16,20},{18,... | collective-permute-start | bytes 3145736 | tf_op jit(solution)/shard_map/ppermute | solution.py:722
  65.9 29.9 %collective-permute-start.16 = (bf16[1024,512]{1,0:T(8,128)(2,1)}, bf16[1024,512]{1,0:T(8,128)(2,1)S(1)}, u32[]{:S(2)}, u32[]{:S(2)}) collective-permute-start(bf16[1024,512]{1,0:T(8,128)(2,1)} %collective-permute-done.9.refs_1_), channel_id=1, source_target_pairs={{0,1},{1,0},{2,3},{3,2},{4,5},{5,4},{6,7},{7,6},{8,9},{9,8},{10,11... | collective-permute-start | bytes 3145736 | tf_op jit(solution)/shard_map/ppermute | solution.py:725
  66.1 13.7 %copy-start.2 = (s32[1,4,16]{2,1,0:T(4,128)S(1)}, s32[1,4,16]{2,1,0:T(4,128)}, u32[]{:S(2)}) copy-start(s32[1,4,16]{2,1,0:T(4,128)} %param.14) | copy-start | bytes 772
  90.8 16.0 %collective-permute-start.13 = (bf16[1024,512]{1,0:T(8,128)(2,1)S(1)}, bf16[1024,512]{1,0:T(8,128)(2,1)S(1)}, u32[]{:S(2)}, u32[]{:S(2)}) collective-permute-start(bf16[1024,512]{1,0:T(8,128)(2,1)S(1)} %get-tuple-element.152), channel_id=1, source_target_pairs={{0,8},{4,12},{8,0},{12,4},{16,24},{20,28},{24,16},{28,20},{1,9},{5... | collective-permute-start | bytes 3145736 | tf_op jit(solution)/shard_map/ppermute | solution.py:818
  91.5 16.5 %collective-permute-start.14 = (bf16[1024,512]{1,0:T(8,128)(2,1)S(1)}, bf16[1024,512]{1,0:T(8,128)(2,1)S(1)}, u32[]{:S(2)}, u32[]{:S(2)}) collective-permute-start(bf16[1024,512]{1,0:T(8,128)(2,1)S(1)} %collective-permute-done.7.refs_1_), channel_id=1, source_target_pairs={{2,3},{3,2},{6,7},{7,6},{10,11},{11,10},{14,15},{15,14},{18,19},{1... | collective-permute-start | bytes 3145736 | tf_op jit(solution)/shard_map/ppermute | solution.py:820
